TPU v7x, 32 devices: a whole 2x2x4 slice. The times are simulated.
32 devices in a mesh: row: 4 (over x, core), col: 8 (over z, y).
Axes of the slice: x: 2, y: 2, z: 4, core: 2. Of those that a mesh axis runs over, the one named last changes fastest.
Arguments:
- amp_ladder: bfloat16 [8, 16, 128, 16, 128], P('row', 'col'), may hold values from -6 to 6
- integrals: bfloat16 [8, 12, 128, 16, 128], P(None, 'row', None, 'col'), may hold values from -0.125 to 0.125
- residual_in: float32 [8, 12, 128, 16, 128], P(None, 'row', None, 'col'), may hold values from -6 to 6
Outputs:
- residual_out: float32 [8, 12, 128, 16, 128], P(None, 'row', None, 'col')
All inputs are finite; a program needn't handle non-finite values.
Results may differ from a plain program's by a relative error of at most 0.0003.
Values may be sent and summed in bfloat16 or wider, within the bound.
No kernel may reach another device: no remote copies, remote signals or barrier semaphores. Data moves between devices by JAX's collectives and lax.ppermute only.
A program may use at most 192 MiB of HBM per device.

v0:
```python
import jax
import jax.numpy as jnp
from jax import lax
from jax.sharding import PartitionSpec as P


def per_device(amp_ladder, integrals, residual_in):
    irreps = integrals.shape[0]
    row_blocks = integrals.shape[1]
    block = integrals.shape[2]
    row_count = row_blocks * block
    moved = lax.all_to_all(amp_ladder, "col", split_axis=3, concat_axis=1, tiled=True)
    cycle_amps = lax.all_gather(moved, "row", axis=0, tiled=True)
    col_local = cycle_amps.shape[3]
    shard_piece = lax.all_gather(integrals, "col", axis=3, tiled=True)
    width_now = shard_piece.shape[3]
    left_part = shard_piece.reshape(irreps, row_count, width_now * block)
    right_part = cycle_amps
    right_part = right_part.reshape(irreps, width_now * block, col_local * block)
    summed = jnp.einsum("hik,hkj->hij", left_part, right_part, preferred_element_type=jnp.float32)
    cycle_term = summed.reshape(irreps, row_blocks, block, col_local, block)
    return residual_in + cycle_term


def solution(mesh):
    placed = (
        P("row", "col", None, None, None),
        P(None, "row", None, "col", None),
        P(None, "row", None, "col", None),
    )
    return jax.shard_map(
        per_device,
        mesh=mesh,
        in_specs=placed,
        out_specs=P(None, "row", None, "col", None),
        check_vma=False,
    )
```

profile of v0, /device:TPU:0, one launch (start us, length us, event | category | flops | bytes accessed | tf_op | source)
XLA Modules:
  0.0 363.1 jit_solution(12068683258675877475)
XLA Ops:
  6.5 0.0 copy-start
  6.5 0.0 all-gather.5.cloned.1.call-start
  6.5 2.2 copy.7
  8.8 55.3 %all_to_all.18 = bf16[2,2,128,16,128]{4,2,1,0,3:T(8,128)(2,1)S(1)} all-to-all(bf16[2,2,128,16,128]{4,2,1,0,3:T(8,128)(2,1)S(1)} %copy.7), channel_id=1, replica_groups=mesh['row'=4,'col'=8] {'col'}, dimensions={3} | all-to-all | bytes 4194304 | tf_op jit(solution)/shard_map/all_to_all | solution.py:12
  64.1 1.5 copy.8
  65.6 0.0 all-gather.5.cloned.1.call-update
  65.6 0.0 all-gather.3.cloned.1.call-start
  65.6 0.0 copy-done
  65.7 1.6 copy.5
  67.2 0.0 all-gather.3.cloned.1.call-update
  67.2 55.8 %all-gather.5.cloned.1.call-done = bf16[8,16,128,2,128]{4,2,3,1,0:T(8,128)(2,1)} async-done(((bf16[2,16,128,2,128]{4,2,3,1,0:T(8,128)(2,1)}), bf16[8,16,128,2,128]{4,2,3,1,0:T(8,128)(2,1)}) %all-gather.5.cloned.1.call-update) | async-done | bytes 8388624 | tf_op jit(solution)/shard_map/all_gather | solution.py:13
  123.0 16.3 %copy.9 = bf16[8,16,128,2,128]{4,3,2,1,0:T(2,128)(2,1)} copy(bf16[8,16,128,2,128]{4,2,3,1,0:T(8,128)(2,1)} %all-gather.5.cloned.1.call-done) | data formatting | bytes 16777216 | tf_op jit(solution)/shard_map/all_gather | solution.py:13
  139.3 14.1 %reshape.10 = bf16[8,2048,256]{2,1,0:T(8,128)(2,1)} reshape(bf16[8,16,128,2,128]{4,3,2,1,0:T(2,128)(2,1)} %copy.9) | data formatting | bytes 16777216 | tf_op jit(solution)/shard_map/reshape | solution.py:19
  153.4 148.3 %all-gather.3.cloned.1.call-done = bf16[8,3,128,16,128]{4,2,1,0,3:T(8,128)(2,1)} async-done(((bf16[8,3,128,2,128]{4,2,1,0,3:T(8,128)(2,1)}), bf16[8,3,128,16,128]{4,2,1,0,3:T(8,128)(2,1)}) %all-gather.3.cloned.1.call-update) | async-done | bytes 12582928 | tf_op jit(solution)/shard_map/all_gather | solution.py:15
  301.7 14.5 %copy.6 = bf16[8,3,128,16,128]{4,3,2,1,0:T(8,128)(2,1)} copy(bf16[8,3,128,16,128]{4,2,1,0,3:T(8,128)(2,1)} %all-gather.3.cloned.1.call-done) | data formatting | bytes 25165824 | tf_op jit(solution)/shard_map/all_gather | solution.py:15
  316.2 19.3 %reshape.9 = bf16[8,384,2048]{2,1,0:T(8,128)(2,1)} reshape(bf16[8,3,128,16,128]{4,3,2,1,0:T(8,128)(2,1)} %copy.6) | data formatting | bytes 25165824 | tf_op jit(solution)/shard_map/reshape | solution.py:17
  335.5 12.0 %fusion = f32[8,384,256]{2,1,0:T(8,128)} fusion(bf16[8,384,2048]{2,1,0:T(8,128)(2,1)} %reshape.9, bf16[8,2048,256]{2,1,0:T(8,128)(2,1)} %reshape.10), kind=kOutput, calls=%fused_computation | convolution fusion | flops 3221225472 | bytes 24117248 | tf_op jit(solution)/shard_map/hik,hkj->hij/dot_general | solution.py:20
  347.6 3.5 reshape.11
  351.1 5.2 %add.3 = f32[8,3,128,2,128]{4,3,2,1,0:T(2,128)} add(f32[8,3,128,2,128]{4,3,2,1,0:T(2,128)} %param.5, f32[8,3,128,2,128]{4,3,2,1,0:T(2,128)S(1)} %reshape.11) | non-fusion elementwise | flops 786432 | bytes 9437184 | tf_op jit(solution)/shard_map/add | solution.py:22
Async XLA Ops:
  6.5 59.1 %copy-start = (bf16[8,3,128,2,128]{4,3,2,1,0:T(2,128)(2,1)S(1)}, bf16[8,3,128,2,128]{4,3,2,1,0:T(2,128)(2,1)}, u32[]{:S(2)}) copy-start(bf16[8,3,128,2,128]{4,3,2,1,0:T(2,128)(2,1)} %param.4) | copy-start | bytes 4718596
  6.5 116.5 %all-gather.5.cloned.1.call-start = ((), (), s32[]{:S(2)}) async-start(), calls=%async_computation.2 | async-start | bytes 10485760 | tf_op jit(solution)/shard_map/all_gather | solution.py:13
  65.6 236.1 %all-gather.3.cloned.1.call-start = ((), (), s32[]{:S(2)}) async-start(), calls=%async_computation.1 | async-start | bytes 14155776 | tf_op jit(solution)/shard_map/all_gather | solution.py:15
Sparse Core Ops, SparseCore 0:
  65.7 57.2 all-gather.4
  125.2 176.4 all-gather.2
where the time goes:
time: 364 us; the launch traced here: 363 us
  waiting for transfers between devices  204 us (56%)
  local copies, waits for them, and re-layouts  73 us (20%)
  blocking collectives  55.3 us (15%)
  between operations  13.4 us (4%)
  matrix products  12 us (3%)
  other arithmetic  5.18 us (1%)
    all_gather x1, waiting for transfers between devices, per_device(): shard_piece = lax.all_gather(integrals, 'col', axis=3, tiled=True)  148 us
    all_gather x1, waiting for transfers between devices, per_device(): cycle_amps = lax.all_gather(moved, 'row', axis=0, tiled=True)  55.8 us
    all_to_all x1, blocking collectives, per_device(): lax.all_to_all(amp_ladder, 'col', split_axis=3, concat_axis=1, tiled=True)  55.3 us
    reshape x1, local copies, waits for them, and re-layouts, per_device(): left_part = shard_piece.reshape(irreps, row_count, width_now * block)  19.3 us
    all_gather x1, local copies, waits for them, and re-layouts, per_device(): cycle_amps = lax.all_gather(moved, 'row', axis=0, tiled=True)  16.3 us
    all_gather x1, local copies, waits for them, and re-layouts, per_device(): shard_piece = lax.all_gather(integrals, 'col', axis=3, tiled=True)  14.5 us
    reshape x1, local copies, waits for them, and re-layouts, per_device(): right_part.reshape(irreps, width_now * block, col_local * block)  14.1 us
    dot_general x1, matrix products, per_device(): jnp.einsum('hik,hkj->hij', left_part, right_part, preferred_element_type=...  12 us
  transfers between devices with their start and end apart: 2, of which 2 were waited for; matrix products, arithmetic and copies ran while one was open for 9% of the time, Pallas kernels for 0%

commit v1 on v0

v1 whole, which is shorter than its diff:
```python
import jax
import jax.numpy as jnp
from jax import lax
from jax.sharding import PartitionSpec as P

F32, F16 = jnp.float32, jnp.float16


def gathered(amp_ladder, integrals, residual_in):
    irreps, row_blocks, block = integrals.shape[:3]
    moved = lax.all_to_all(amp_ladder, "col", split_axis=3, concat_axis=1, tiled=True)
    right = lax.all_gather(moved, "row", axis=0, tiled=True)
    left = lax.all_gather(integrals, "col", axis=3, tiled=True)
    inner = left.shape[3] * block
    columns = right.shape[3]
    left = left.reshape(irreps, row_blocks * block, inner)
    right = right.reshape(irreps, inner, columns * block)
    cycle = jnp.einsum("hik,hkj->hij", left, right, preferred_element_type=F32)
    return residual_in + cycle.reshape(irreps, row_blocks, block, columns, block)


def along_z(pairs):
    return [(2 * a + y, 2 * b + y) for a, b in pairs for y in range(2)]


SWAP_Y = [(c, c ^ 1) for c in range(8)]
SWAP_CORE = [(r, r ^ 1) for r in range(4)]
SWAP_X = [(r, r ^ 2) for r in range(4)]
XOR_Z = {d: along_z([(z, z ^ d) for z in range(4)]) for d in (1, 2, 3)}
MIDDLE = along_z([(1, 2), (2, 1)])
INWARD = along_z([(0, 1), (3, 2)])
OUTWARD = along_z([(1, 0), (2, 3)])


def col(x, pairs):
    return lax.ppermute(x, "col", pairs)


def row(x, pairs):
    return lax.ppermute(x, "row", pairs)


def pick(x, i, axis=0):
    return lax.dynamic_index_in_dim(x, i, axis, keepdims=False)


def dot(a, b):
    return jnp.einsum("hik,hkj->hij", a, b, preferred_element_type=F32)


def over_row(piece):
    two = jnp.stack([piece, row(piece, SWAP_X)])
    return jnp.concatenate([two, row(two, SWAP_CORE)])


def mixed(amp_ladder, integrals, residual_in):
    irreps, row_blocks, block, k_blocks, _ = integrals.shape
    rows, kk = row_blocks * block, k_blocks * block
    r, c = lax.axis_index("row"), lax.axis_index("col")
    z, y = c // 2, c % 2
    order = [r, r ^ 2, r ^ 1, r ^ 3]
    middle = (z == 1) | (z == 2)

    left = integrals.reshape(irreps // 2, 2, rows, kk)
    left = [jnp.stack([pick(left[:, s], q) for q in order]) for s in range(2)]
    right = amp_ladder.reshape(2, kk, 4, 2, 2 * block)
    right = right.transpose(0, 2, 3, 1, 4)

    a_own, b0 = left[0], right[0]
    b_own, b_other = pick(b0, y, 1), pick(b0, 1 - y, 1)
    b_in = col(b_other, SWAP_Y)
    a_in = col(a_own, SWAP_Y)
    bo = over_row(b_own)
    bi = over_row(b_in)

    g, b1 = left[1], right[1]
    g1 = col(g, XOR_Z[1])
    gm3 = col(g, MIDDLE)
    gm2 = col(g1, MIDDLE)
    ge2 = col(gm3, OUTWARD)
    ge3 = col(gm2, OUTWARD)
    pieces = [pick(b1, z)] + [col(pick(b1, z ^ d), XOR_Z[d]) for d in (1, 2, 3)]
    near = over_row(jnp.stack(pieces[:2]))
    far = over_row(jnp.stack(pieces[2:]))

    def part(d):
        t = z ^ d
        return dot(a_own, pick(bo, t, 1)) + dot(a_in, pick(bi, t, 1))

    p3, p2, p1, p0 = part(3), part(2), part(1), part(0)
    s1 = col(p3.astype(F16), INWARD)
    send = (p2 + s1.astype(F32)).astype(F16)
    s2a = col(send, INWARD)
    s2b = col(send, MIDDLE)
    s3a = col((p1 + s2b.astype(F32)).astype(F16), XOR_Z[1])
    s3b = col((p3 + s2a.astype(F32)).astype(F16), MIDDLE)
    even = p0 + s3a.astype(F32) + s3b.astype(F32)

    g2 = jnp.where(middle, gm2, ge2)
    g3 = jnp.where(middle, gm3, ge3)

    def column(which):
        take = lambda b, i: pick(b[:, i], which, 1)
        return (dot(g, take(near, 0)) + dot(g1, take(near, 1))) + (dot(g2, take(far, 0)) + dot(g3, take(far, 1)))

    q = col(column(1 - y).astype(F16), SWAP_Y)
    odd = column(y) + q.astype(F32)

    both = jnp.stack([even, odd], 1)
    back = []
    for q in range(irreps // 2):
        m = r ^ q
        back.append(pick(both, (m >> 1) | ((m & 1) << 1)))
    cycle = jnp.concatenate(back).reshape(residual_in.shape)
    return residual_in + cycle


def solution(mesh):
    placed = (
        P("row", "col", None, None, None),
        P(None, "row", None, "col", None),
        P(None, "row", None, "col", None),
    )

    def per_device(amp_ladder, integrals, residual_in):
        fits = mesh.shape["row"] == 4 and mesh.shape["col"] == 8
        fits = fits and amp_ladder.shape[0] == 2 and residual_in.shape[3] == 2 and amp_ladder.shape[1] == 2
        return (mixed if fits else gathered)(amp_ladder, integrals, residual_in)

    return jax.shard_map(
        per_device,
        mesh=mesh,
        in_specs=placed,
        out_specs=P(None, "row", None, "col", None),
        check_vma=False,
    )
```

time: 364 us -> 169 us (0.46)
  waiting for transfers between devices: 204 us -> 85.6 us
  blocking collectives: 55.3 us -> 0 us
  local copies, waits for them, and re-layouts: 73 us -> 19.4 us
  starting transfers between devices: 0.04 us -> 33.4 us
  other arithmetic: 5.18 us -> 22.4 us
  between operations: 13.4 us -> 0.62 us
  matrix products: 12 us -> 6.6 us
    all_gather x2 -> x0, waiting for transfers between devices: 204 us -> none  [the longest x1 148 us: per_device(): shard_piece = lax.all_gather(integrals, 'col', axis=3, tiled=True)]
    ppermute x0 -> x24, waiting for transfers between devices: none -> 85.6 us  [the longest x16 63.9 us: col(): return lax.ppermute(x, 'col', pairs)]
    all_to_all x1 -> x0, blocking collectives: 55.3 us -> none  [per_device(): lax.all_to_all(amp_ladder, 'col', split_axis=3, concat_axis=1, tiled=True)]
    ppermute x0 -> x24, starting transfers between devices: none -> 33.4 us  [the longest x16 29.7 us: col(): return lax.ppermute(x, 'col', pairs)]
    reshape x3 -> x2, local copies, waits for them, and re-layouts: 36.9 us -> 5.91 us  [the longest x1 3.15 us: mixed(): right = amp_ladder.reshape(2, kk, 4, 2, 2 * block)]
    all_gather x2 -> x0, local copies, waits for them, and re-layouts: 30.8 us -> none  [the longest x1 16.3 us: per_device(): cycle_amps = lax.all_gather(moved, 'row', axis=0, tiled=True)]
    another operation x0 -> x11, other arithmetic: none -> 11.9 us  [the longest x6 7.8 us: over_row(): two = jnp.stack([piece, row(piece, SWAP_X)])]
    dynamic_slice x0 -> x10, local copies, waits for them, and re-layouts: none -> 5.64 us  [pick(): return lax.dynamic_index_in_dim(x, i, axis, keepdims=False)]
  transfers between devices with their start and end apart: 2 -> 24, of which waited for: 2 -> 9; matrix products, arithmetic and copies ran while one was open for 9% -> 17% of each run, Pallas kernels for 0% -> 0%
where the time goes in v1:
time: 169 us; the launch traced here: 168 us
  waiting for transfers between devices  85.6 us (51%)
  starting transfers between devices  33.4 us (20%)
  other arithmetic  22.4 us (13%)
  local copies, waits for them, and re-layouts  19.4 us (11%)
  matrix products  6.6 us (4%)
    ppermute x16, waiting for transfers between devices, col(): return lax.ppermute(x, 'col', pairs)  63.9 us
    ppermute x16, starting transfers between devices, col(): return lax.ppermute(x, 'col', pairs)  29.7 us
    ppermute x8, waiting for transfers between devices, row(): return lax.ppermute(x, 'row', pairs)  21.7 us
    another operation x6, other arithmetic, over_row(): two = jnp.stack([piece, row(piece, SWAP_X)])  7.8 us
    dot_general x16, matrix products, dot(): return jnp.einsum('hik,hkj->hij', a, b, preferred_element_type=F32)  6.6 us
    dynamic_slice x10, local copies, waits for them, and re-layouts, pick(): return lax.dynamic_index_in_dim(x, i, axis, keepdims=False)  5.64 us
    add x1, other arithmetic, mixed(): return residual_in + cycle  5.18 us
    concatenate x4, other arithmetic, over_row(): return jnp.concatenate([two, row(two, SWAP_CORE)])  4.62 us
  transfers between devices with their start and end apart: 24, of which 9 were waited for; matrix products, arithmetic and copies ran while one was open for 17% of the time, Pallas kernels for 0%

profile of v1, /device:TPU:0, one launch (start us, length us, event | category | flops | bytes accessed | tf_op | source)
XLA Modules:
  0.0 168.0 jit_solution(17039086165584638815)
XLA Ops:
  0.0 3.1 %reshape.52 = bf16[2,256,4,2,256]{4,3,2,1,0:T(2,128)(2,1)S(1)} reshape(bf16[2,2,128,16,128]{4,3,2,1,0:T(8,128)(2,1)} %param.3) | data formatting | bytes 4194304 | tf_op jit(solution)/shard_map/reshape | solution.py:66
  3.2 2.3 %fusion.69 = (bf16[1,4,2,256,256]{4,2,1,3,0:T(2,128)(2,1)}, bf16[1,4,2,256,256]{4,2,1,3,0:T(2,128)(2,1)S(1)}) fusion(bf16[2,4,2,256,256]{4,2,1,3,0:T(2,128)(2,1)S(1)} %bitcast.136), kind=kLoop, calls=%fused_computation.120 | loop fusion | bytes 4194304 | tf_op jit(solution)/shard_map/slice | solution.py:76
  5.4 2.2 %constant_dynamic-slice_fusion.5 = (bf16[1,4,1,256,256]{4,2,1,3,0:T(2,128)(2,1)S(1)}, bf16[1,4,1,256,256]{4,2,1,3,0:T(2,128)(2,1)S(1)}) fusion(bf16[1,4,2,256,256]{4,2,1,3,0:T(2,128)(2,1)S(1)} %get-tuple-element.14, s32[]{:T(128)S(6)} %select_n.95, s32[]{:T(128)S(6)} %select_n.98), kind=kLoop, calls=%fused_computation.115 | loop fusion | bytes 2097160 | tf_op jit(solution)/shard_map/jit(dynamic_index_in_dim)/dynamic_slice | solution.py:44
  7.6 1.0 copy.24
  8.6 3.0 %collective-permute-start.3 = (bf16[4,256,256]{2,1,0:T(8,128)(2,1)}, bf16[4,256,256]{2,1,0:T(8,128)(2,1)}, u32[]{:S(2)}, u32[]{:S(2)}) collective-permute-start(bf16[4,256,256]{2,1,0:T(8,128)(2,1)} %bitcast.130), channel_id=1, source_target_pairs={{0,1},{1,0},{2,3},{3,2},{4,5},{5,4},{6,7},{7,6},{8,9},{9,8},{10,11... | collective-permute-start | bytes 1572872 | tf_op jit(solution)/shard_map/ppermute | solution.py:36
  11.7 1.6 collective-permute-start
  13.3 0.7 constant_dynamic-slice_fusion.3
  14.0 0.7 copy.25
  14.7 3.6 %collective-permute-start.19 = (bf16[2,256,256]{2,1,0:T(8,128)(2,1)}, bf16[2,256,256]{2,1,0:T(8,128)(2,1)}, u32[]{:S(2)}, u32[]{:S(2)}) collective-permute-start(bf16[2,256,256]{2,1,0:T(8,128)(2,1)} %bitcast.131), channel_id=1, source_target_pairs={{0,6},{1,7},{2,4},{3,5},{4,2},{5,3},{6,0},{7,1},{8,14},{9,15},{10,... | collective-permute-start | bytes 786440 | tf_op jit(solution)/shard_map/ppermute | solution.py:36
  18.4 0.7 copy.27
  19.2 0.8 collective-permute-start.11
  19.9 2.8 %reshape.51 = bf16[4,2,384,256]{3,2,1,0:T(8,128)(2,1)S(1)} reshape(bf16[8,3,128,2,128]{4,3,2,1,0:T(2,128)(2,1)} %param.4) | data formatting | bytes 3145728 | tf_op jit(solution)/shard_map/reshape | solution.py:64
  22.7 1.0 fusion.70
  23.9 1.1 pad_maximum_fusion.9
  25.0 9.9 %collective-permute-done.11 = bf16[2,256,256]{2,1,0:T(8,128)(2,1)} collective-permute-done((bf16[2,256,256]{2,1,0:T(8,128)(2,1)}, bf16[2,256,256]{2,1,0:T(8,128)(2,1)}, u32[]{:S(2)}, u32[]{:S(2)}) %collective-permute-start.11) | collective-permute-done | bytes 262176 | tf_op jit(solution)/shard_map/ppermute | solution.py:36
  35.0 2.5 %collective-permute-start.14 = (bf16[4,384,256]{2,1,0:T(8,128)(2,1)}, bf16[4,384,256]{2,1,0:T(8,128)(2,1)S(1)}, u32[]{:S(2)}, u32[]{:S(2)}) collective-permute-start(bf16[4,384,256]{2,1,0:T(8,128)(2,1)} %pad_maximum_fusion.9), channel_id=1, source_target_pairs={{0,2},{1,3},{2,0},{3,1},{4,6},{5,7},{6,4},{7,5},{8,10},{9,11},{10,... | collective-permute-start | bytes 2359304 | tf_op jit(solution)/shard_map/ppermute | solution.py:36
  37.4 1.0 fusion.66
  39.1 1.4 collective-permute-done.18
  40.5 1.1 fusion.65
  42.2 2.1 %pad_maximum_fusion.4 = bf16[2,4,256,256]{3,2,0,1:T(8,128)(2,1)} fusion(bf16[1,4,256,256]{3,2,0,1:T(8,128)(2,1)} %bitcast.7, bf16[1,4,256,256]{3,2,0,1:T(8,128)(2,1)S(1)} %bitcast.138), kind=kLoop, calls=%fused_computation.20 | loop fusion | flops 524288 | bytes 2097152 | tf_op jit(solution)/shard_map/stack | solution.py:52
  44.3 0.8 collective-permute-start.16
  45.2 8.2 %collective-permute-done.12 = bf16[2,2,256,256]{3,2,1,0:T(8,128)(2,1)S(1)} collective-permute-done((bf16[2,2,256,256]{3,2,1,0:T(8,128)(2,1)S(1)}, bf16[2,2,256,256]{3,2,1,0:T(8,128)(2,1)S(1)}, u32[]{:S(2)}, u32[]{:S(2)}) %collective-permute-start.12) | collective-permute-done | bytes 524320 | tf_op jit(solution)/shard_map/ppermute | solution.py:40
  53.9 1.1 pad_maximum_fusion.6
  55.0 9.6 %collective-permute-done.20 = bf16[2,2,256,256]{3,2,1,0:T(8,128)(2,1)S(1)} collective-permute-done((bf16[2,2,256,256]{3,2,1,0:T(8,128)(2,1)S(1)}, bf16[2,2,256,256]{3,2,1,0:T(8,128)(2,1)S(1)}, u32[]{:S(2)}, u32[]{:S(2)}) %collective-permute-start.20) | collective-permute-done | bytes 524320 | tf_op jit(solution)/shard_map/ppermute | solution.py:40
  64.8 0.7 copy-done.4
  65.5 1.6 collective-permute-start.15
  67.0 1.0 pad_maximum_fusion.8
  68.0 1.2 pad_maximum_fusion.7
  69.3 3.8 %collective-permute-done.4 = bf16[4,256,256]{2,1,0:T(8,128)(2,1)} collective-permute-done((bf16[4,256,256]{2,1,0:T(8,128)(2,1)}, bf16[4,256,256]{2,1,0:T(8,128)(2,1)}, u32[]{:S(2)}, u32[]{:S(2)}) %collective-permute-start.4) | collective-permute-done | bytes 524320 | tf_op jit(solution)/shard_map/ppermute | solution.py:40
  73.6 1.3 pad_maximum_fusion.5
  75.0 1.4 collective-permute-start.17
  76.4 1.6 pad_maximum_fusion
  79.3 1.3 collective-permute-start.22
  80.6 1.4 pad_maximum_fusion.2
  83.6 13.7 %collective-permute-done.17 = bf16[4,384,256]{2,1,0:T(8,128)(2,1)S(1)} collective-permute-done((bf16[4,384,256]{2,1,0:T(8,128)(2,1)S(1)}, bf16[4,384,256]{2,1,0:T(8,128)(2,1)S(1)}, u32[]{:S(2)}, u32[]{:S(2)}) %collective-permute-start.17) | collective-permute-done | bytes 786464 | tf_op jit(solution)/shard_map/ppermute | solution.py:36
  97.8 1.4 pad_maximum_fusion.1
  100.1 2.9 %collective-permute-start.6 = (f16[4,384,256]{2,1,0:T(8,128)(2,1)S(1)}, f16[4,384,256]{2,1,0:T(8,128)(2,1)S(1)}, u32[]{:S(2)}, u32[]{:S(2)}) collective-permute-start(f16[4,384,256]{2,1,0:T(8,128)(2,1)S(1)} %get-tuple-element.37), channel_id=1, source_target_pairs={{0,2},{1,3},{6,4},{7,5},{8,10},{9,11},{14,12},{15,13},{16,18},{17,... | collective-permute-start | bytes 2359304 | tf_op jit(solution)/shard_map/ppermute | solution.py:36
  104.6 14.1 %collective-permute-done.6 = f16[4,384,256]{2,1,0:T(8,128)(2,1)S(1)} collective-permute-done((f16[4,384,256]{2,1,0:T(8,128)(2,1)S(1)}, f16[4,384,256]{2,1,0:T(8,128)(2,1)S(1)}, u32[]{:S(2)}, u32[]{:S(2)}) %collective-permute-start.6) | collective-permute-done | bytes 786464 | tf_op jit(solution)/shard_map/ppermute | solution.py:36
  119.2 4.4 %collective-permute-start.9 = (f16[4,384,256]{2,1,0:T(8,128)(2,1)S(1)}, f16[4,384,256]{2,1,0:T(8,128)(2,1)S(1)}, u32[]{:S(2)}, u32[]{:S(2)}) collective-permute-start(f16[4,384,256]{2,1,0:T(8,128)(2,1)S(1)} %add_convert_fusion.3), channel_id=1, source_target_pairs={{0,2},{1,3},{6,4},{7,5},{8,10},{9,11},{14,12},{15,13},{16,18},{17,... | collective-permute-start | bytes 2359304 | tf_op jit(solution)/shard_map/ppermute | solution.py:36
  124.1 0.7 collective-permute-start.7
  125.8 1.6 collective-permute-start.23
  127.4 11.2 %collective-permute-done.9 = f16[4,384,256]{2,1,0:T(8,128)(2,1)S(1)} collective-permute-done((f16[4,384,256]{2,1,0:T(8,128)(2,1)S(1)}, f16[4,384,256]{2,1,0:T(8,128)(2,1)S(1)}, u32[]{:S(2)}, u32[]{:S(2)}) %collective-permute-start.9) | collective-permute-done | bytes 786464 | tf_op jit(solution)/shard_map/ppermute | solution.py:36
  138.9 0.7 collective-permute-start.10
  140.1 3.8 %collective-permute-start.8 = (f16[4,384,256]{2,1,0:T(8,128)(2,1)S(1)}, f16[4,384,256]{2,1,0:T(8,128)(2,1)S(1)}, u32[]{:S(2)}, u32[]{:S(2)}) collective-permute-start(f16[4,384,256]{2,1,0:T(8,128)(2,1)S(1)} %add_convert_fusion.2), channel_id=1, source_target_pairs={{0,2},{1,3},{2,0},{3,1},{4,6},{5,7},{6,4},{7,5},{8,10},{9,11},{10,... | collective-permute-start | bytes 2359304 | tf_op jit(solution)/shard_map/ppermute | solution.py:36
  145.1 13.5 %collective-permute-done.8 = f16[4,384,256]{2,1,0:T(8,128)(2,1)S(1)} collective-permute-done((f16[4,384,256]{2,1,0:T(8,128)(2,1)S(1)}, f16[4,384,256]{2,1,0:T(8,128)(2,1)S(1)}, u32[]{:S(2)}, u32[]{:S(2)}) %collective-permute-start.8) | collective-permute-done | bytes 786464 | tf_op jit(solution)/shard_map/ppermute | solution.py:36
  159.0 1.1 fusion.1
  161.3 1.5 concatenate.32
  162.9 5.2 %maximum_add_fusion = f32[8,3,128,2,128]{4,3,2,1,0:T(2,128)} fusion(f32[8,3,128,2,128]{4,3,2,1,0:T(2,128)} %param.5, f32[2,3,128,2,128]{4,3,2,1,0:T(2,128)S(1)} %concatenate.35, f32[2,3,128,2,128]{4,3,2,1,0:T(2,128)S(1)} %concatenate.34, f32[2,3,128,2,128]{4,3,2,1,0:T(2,128)S(1)} %concatenate.33, f32[2,3,128,2,128]{4,3,2,1,0:T(2,128)S(1)} %concatenate.32), kind=kLoop, calls=%fused_computation.8 | loop fusion | flops 3145728 | bytes 9437184 | tf_op jit(solution)/shard_map/add | solution.py:115
  (92 shorter events, 13.8 us)
Async XLA Ops:
  7.6 5.7 %copy-start = (bf16[1,4,2,256,256]{4,2,1,3,0:T(2,128)(2,1)S(1)}, bf16[1,4,2,256,256]{4,2,1,3,0:T(2,128)(2,1)}, u32[]{:S(2)}) copy-start(bf16[1,4,2,256,256]{4,2,1,3,0:T(2,128)(2,1)} %get-tuple-element.13) | copy-start | bytes 3145732
  8.6 35.7 %collective-permute-start.3 = (bf16[4,256,256]{2,1,0:T(8,128)(2,1)}, bf16[4,256,256]{2,1,0:T(8,128)(2,1)}, u32[]{:S(2)}, u32[]{:S(2)}) collective-permute-start(bf16[4,256,256]{2,1,0:T(8,128)(2,1)} %bitcast.130), channel_id=1, source_target_pairs={{0,1},{1,0},{2,3},{3,2},{4,5},{5,4},{6,7},{7,6},{8,9},{9,8},{10,11... | collective-permute-start | bytes 1572872 | tf_op jit(solution)/shard_map/ppermute | solution.py:36
  11.7 30.5 %collective-permute-start = (bf16[4,256,256]{2,1,0:T(8,128)(2,1)S(1)}, bf16[4,256,256]{2,1,0:T(8,128)(2,1)}, u32[]{:S(2)}, u32[]{:S(2)}) collective-permute-start(bf16[4,256,256]{2,1,0:T(8,128)(2,1)S(1)} %bitcast.137), channel_id=1, source_target_pairs={{0,16},{8,24},{16,0},{24,8},{1,17},{9,25},{17,1},{25,9},{2,18},{10... | collective-permute-start | bytes 1572872 | tf_op jit(solution)/shard_map/ppermute | solution.py:40
  14.7 23.8 %collective-permute-start.19 = (bf16[2,256,256]{2,1,0:T(8,128)(2,1)}, bf16[2,256,256]{2,1,0:T(8,128)(2,1)}, u32[]{:S(2)}, u32[]{:S(2)}) collective-permute-start(bf16[2,256,256]{2,1,0:T(8,128)(2,1)} %bitcast.131), channel_id=1, source_target_pairs={{0,6},{1,7},{2,4},{3,5},{4,2},{5,3},{6,0},{7,1},{8,14},{9,15},{10,... | collective-permute-start | bytes 786440 | tf_op jit(solution)/shard_map/ppermute | solution.py:36
  18.3 22.1 %collective-permute-start.18 = (bf16[2,256,256]{2,1,0:T(8,128)(2,1)S(1)}, bf16[2,256,256]{2,1,0:T(8,128)(2,1)}, u32[]{:S(2)}, u32[]{:S(2)}) collective-permute-start(bf16[2,256,256]{2,1,0:T(8,128)(2,1)S(1)} %bitcast.145), channel_id=1, source_target_pairs={{0,4},{1,5},{2,6},{3,7},{4,0},{5,1},{6,2},{7,3},{8,12},{9,13},{10,... | collective-permute-start | bytes 786440 | tf_op jit(solution)/shard_map/ppermute | solution.py:36
  19.2 15.8 %collective-permute-start.11 = (bf16[2,256,256]{2,1,0:T(8,128)(2,1)}, bf16[2,256,256]{2,1,0:T(8,128)(2,1)}, u32[]{:S(2)}, u32[]{:S(2)}) collective-permute-start(bf16[2,256,256]{2,1,0:T(8,128)(2,1)} %bitcast.133), channel_id=1, source_target_pairs={{0,2},{1,3},{2,0},{3,1},{4,6},{5,7},{6,4},{7,5},{8,10},{9,11},{10,... | collective-permute-start | bytes 786440 | tf_op jit(solution)/shard_map/ppermute | solution.py:36
  23.8 1.2 copy-start.10
  23.8 1.2 copy-start.12
  23.8 1.2 copy-start.14
  23.8 1.2 copy-start.16
  35.0 29.8 %collective-permute-start.14 = (bf16[4,384,256]{2,1,0:T(8,128)(2,1)}, bf16[4,384,256]{2,1,0:T(8,128)(2,1)S(1)}, u32[]{:S(2)}, u32[]{:S(2)}) collective-permute-start(bf16[4,384,256]{2,1,0:T(8,128)(2,1)} %pad_maximum_fusion.9), channel_id=1, source_target_pairs={{0,2},{1,3},{2,0},{3,1},{4,6},{5,7},{6,4},{7,5},{8,10},{9,11},{10,... | collective-permute-start | bytes 2359304 | tf_op jit(solution)/shard_map/ppermute | solution.py:36
  38.5 14.9 %collective-permute-start.12 = (bf16[2,2,256,256]{3,2,1,0:T(8,128)(2,1)S(1)}, bf16[2,2,256,256]{3,2,1,0:T(8,128)(2,1)S(1)}, u32[]{:S(2)}, u32[]{:S(2)}) collective-permute-start(bf16[2,2,256,256]{3,2,1,0:T(8,128)(2,1)S(1)} %get-tuple-element.34), channel_id=1, source_target_pairs={{0,16},{8,24},{16,0},{24,8},{1,17},{9,25},{17,1},{25,9},{2,18},{10... | collective-permute-start | bytes 1572872 | tf_op jit(solution)/shard_map/ppermute | solution.py:40
  41.6 23.0 %collective-permute-start.20 = (bf16[2,2,256,256]{3,2,1,0:T(8,128)(2,1)S(1)}, bf16[2,2,256,256]{3,2,1,0:T(8,128)(2,1)S(1)}, u32[]{:S(2)}, u32[]{:S(2)}) collective-permute-start(bf16[2,2,256,256]{3,2,1,0:T(8,128)(2,1)S(1)} %get-tuple-element.36), channel_id=1, source_target_pairs={{0,16},{8,24},{16,0},{24,8},{1,17},{9,25},{17,1},{25,9},{2,18},{10... | collective-permute-start | bytes 1572872 | tf_op jit(solution)/shard_map/ppermute | solution.py:40
  44.3 20.3 %copy-start.1 = (bf16[4,1,384,256]{3,2,1,0:T(8,128)(2,1)S(1)}, bf16[4,1,384,256]{3,2,1,0:T(8,128)(2,1)}, u32[]{:S(2)}) copy-start(bf16[4,1,384,256]{3,2,1,0:T(8,128)(2,1)} %get-tuple-element.16) | copy-start | bytes 2359300
  44.3 30.7 %collective-permute-start.1 = (bf16[2,4,256,256]{3,2,0,1:T(8,128)(2,1)}, bf16[2,4,256,256]{3,2,0,1:T(8,128)(2,1)}, u32[]{:S(2)}, u32[]{:S(2)}) collective-permute-start(bf16[2,4,256,256]{3,2,0,1:T(8,128)(2,1)} %pad_maximum_fusion.4), channel_id=1, source_target_pairs={{0,8},{8,0},{16,24},{24,16},{1,9},{9,1},{17,25},{25,17},{2,10},{10... | collective-permute-start | bytes 3145736 | tf_op jit(solution)/shard_map/ppermute | solution.py:40
  44.3 30.6 %collective-permute-start.16 = (bf16[4,384,256]{2,1,0:T(8,128)(2,1)}, bf16[4,384,256]{2,1,0:T(8,128)(2,1)S(1)}, u32[]{:S(2)}, u32[]{:S(2)}) collective-permute-start(bf16[4,384,256]{2,1,0:T(8,128)(2,1)} %pad_maximum_fusion.9), channel_id=1, source_target_pairs={{2,4},{3,5},{4,2},{5,3},{10,12},{11,13},{12,10},{13,11},{18,20},{1... | collective-permute-start | bytes 2359304 | tf_op jit(solution)/shard_map/ppermute | solution.py:36
  53.4 11.3 %copy-start.2 = (bf16[2,2,256,256]{3,2,1,0:T(8,128)(2,1)}, bf16[2,2,256,256]{3,2,1,0:T(8,128)(2,1)S(1)}, u32[]{:S(2)}) copy-start(bf16[2,2,256,256]{3,2,1,0:T(8,128)(2,1)S(1)} %collective-permute-done.12) | copy-start | bytes 1572868
  53.4 19.7 %collective-permute-start.4 = (bf16[4,256,256]{2,1,0:T(8,128)(2,1)}, bf16[4,256,256]{2,1,0:T(8,128)(2,1)}, u32[]{:S(2)}, u32[]{:S(2)}) collective-permute-start(bf16[4,256,256]{2,1,0:T(8,128)(2,1)} %collective-permute-done.3), channel_id=1, source_target_pairs={{0,16},{8,24},{16,0},{24,8},{1,17},{9,25},{17,1},{25,9},{2,18},{10... | collective-permute-start | bytes 1572872 | tf_op jit(solution)/shard_map/ppermute | solution.py:40
  64.6 0.8 copy-start.4
  64.6 14.6 %collective-permute-start.13 = (bf16[2,2,2,256,256]{4,3,0,2,1:T(8,128)(2,1)}, bf16[2,2,2,256,256]{4,3,0,2,1:T(8,128)(2,1)}, u32[]{:S(2)}, u32[]{:S(2)}) collective-permute-start(bf16[2,2,2,256,256]{4,3,0,2,1:T(8,128)(2,1)} %pad_maximum_fusion.6), channel_id=1, source_target_pairs={{0,8},{8,0},{16,24},{24,16},{1,9},{9,1},{17,25},{25,17},{2,10},{10... | collective-permute-start | bytes 3145736 | tf_op jit(solution)/shard_map/ppermute | solution.py:40
  64.7 2.3 %copy-start.6 = (bf16[1,384,256]{2,1,0:T(8,128)(2,1)}, bf16[1,384,256]{2,1,0:T(8,128)(2,1)S(1)}, u32[]{:S(2)}) copy-start(bf16[1,384,256]{2,1,0:T(8,128)(2,1)S(1)} %get-tuple-element.31) | copy-start | bytes 589828
  64.7 2.3 %copy-start.8 = (bf16[1,384,256]{2,1,0:T(8,128)(2,1)}, bf16[1,384,256]{2,1,0:T(8,128)(2,1)S(1)}, u32[]{:S(2)}) copy-start(bf16[1,384,256]{2,1,0:T(8,128)(2,1)S(1)} %get-tuple-element.32) | copy-start | bytes 589828
  65.5 13.4 %collective-permute-start.15 = (bf16[4,384,256]{2,1,0:T(8,128)(2,1)S(1)}, bf16[4,384,256]{2,1,0:T(8,128)(2,1)}, u32[]{:S(2)}, u32[]{:S(2)}) collective-permute-start(bf16[4,384,256]{2,1,0:T(8,128)(2,1)S(1)} %collective-permute-done.14), channel_id=1, source_target_pairs={{2,4},{3,5},{4,2},{5,3},{10,12},{11,13},{12,10},{13,11},{18,20},{1... | collective-permute-start | bytes 2359304 | tf_op jit(solution)/shard_map/ppermute | solution.py:36
  68.0 5.0 %copy-start.18 = (bf16[4,384,256]{2,1,0:T(8,128)(2,1)S(1)}, bf16[4,384,256]{2,1,0:T(8,128)(2,1)}, u32[]{:S(2)}) copy-start(bf16[4,384,256]{2,1,0:T(8,128)(2,1)} %pad_maximum_fusion.8) | copy-start | bytes 2359300
  73.1 26.1 %collective-permute-start.2 = (bf16[4,384,256]{2,1,0:T(8,128)(2,1)S(1)}, bf16[4,384,256]{2,1,0:T(8,128)(2,1)S(1)}, u32[]{:S(2)}, u32[]{:S(2)}) collective-permute-start(bf16[4,384,256]{2,1,0:T(8,128)(2,1)S(1)} %copy-done.18), channel_id=1, source_target_pairs={{0,1},{1,0},{2,3},{3,2},{4,5},{5,4},{6,7},{7,6},{8,9},{9,8},{10,11... | collective-permute-start | bytes 2359304 | tf_op jit(solution)/shard_map/ppermute | solution.py:36
  74.9 3.1 %copy-start.7 = (bf16[1,384,256]{2,1,0:T(8,128)(2,1)S(1)}, bf16[1,384,256]{2,1,0:T(8,128)(2,1)}, u32[]{:S(2)}) copy-start(bf16[1,384,256]{2,1,0:T(8,128)(2,1)} %copy-done.6) | copy-start | bytes 589828
  74.9 3.1 %copy-start.9 = (bf16[1,384,256]{2,1,0:T(8,128)(2,1)S(1)}, bf16[1,384,256]{2,1,0:T(8,128)(2,1)}, u32[]{:S(2)}) copy-start(bf16[1,384,256]{2,1,0:T(8,128)(2,1)} %copy-done.8) | copy-start | bytes 589828
  74.9 7.7 %collective-permute-start.21 = (bf16[2,2,2,256,256]{4,3,0,2,1:T(8,128)(2,1)S(1)}, bf16[2,2,2,256,256]{4,3,0,2,1:T(8,128)(2,1)S(1)}, u32[]{:S(2)}, u32[]{:S(2)}) collective-permute-start(bf16[2,2,2,256,256]{4,3,0,2,1:T(8,128)(2,1)S(1)} %pad_maximum_fusion.7), channel_id=1, source_target_pairs={{0,8},{8,0},{16,24},{24,16},{1,9},{9,1},{17,25},{25,17},{2,10},{10... | collective-permute-start | bytes 3145736 | tf_op jit(solution)/shard_map/ppermute | solution.py:40
  75.0 22.4 %collective-permute-start.17 = (bf16[4,384,256]{2,1,0:T(8,128)(2,1)S(1)}, bf16[4,384,256]{2,1,0:T(8,128)(2,1)S(1)}, u32[]{:S(2)}, u32[]{:S(2)}) collective-permute-start(bf16[4,384,256]{2,1,0:T(8,128)(2,1)S(1)} %collective-permute-done.16), channel_id=1, source_target_pairs={{2,0},{3,1},{4,6},{5,7},{10,8},{11,9},{12,14},{13,15},{18,16},{19,... | collective-permute-start | bytes 2359304 | tf_op jit(solution)/shard_map/ppermute | solution.py:36
  78.4 2.1 %copy-start.3 = (bf16[2,2,256,256]{3,2,1,0:T(8,128)(2,1)S(1)}, bf16[2,2,256,256]{3,2,1,0:T(8,128)(2,1)}, u32[]{:S(2)}) copy-start(bf16[2,2,256,256]{3,2,1,0:T(8,128)(2,1)} %copy-done.2) | copy-start | bytes 1572868
  78.8 18.9 %collective-permute-start.5 = (bf16[2,4,256,256]{3,2,0,1:T(8,128)(2,1)S(1)}, bf16[2,4,256,256]{3,2,0,1:T(8,128)(2,1)S(1)}, u32[]{:S(2)}, u32[]{:S(2)}) collective-permute-start(bf16[2,4,256,256]{3,2,0,1:T(8,128)(2,1)S(1)} %pad_maximum_fusion.5), channel_id=1, source_target_pairs={{0,8},{8,0},{16,24},{24,16},{1,9},{9,1},{17,25},{25,17},{2,10},{10... | collective-permute-start | bytes 3145736 | tf_op jit(solution)/shard_map/ppermute | solution.py:40
  79.3 45.9 %collective-permute-start.22 = (bf16[4,384,256]{2,1,0:T(8,128)(2,1)}, bf16[4,384,256]{2,1,0:T(8,128)(2,1)S(1)}, u32[]{:S(2)}, u32[]{:S(2)}) collective-permute-start(bf16[4,384,256]{2,1,0:T(8,128)(2,1)} %collective-permute-done.15), channel_id=1, source_target_pairs={{2,0},{3,1},{4,6},{5,7},{10,8},{11,9},{12,14},{13,15},{18,16},{19,... | collective-permute-start | bytes 2359304 | tf_op jit(solution)/shard_map/ppermute | solution.py:36
  82.2 1.0 copy-start.5
  100.0 3.4 %copy-start.11 = (bf16[1,384,256]{2,1,0:T(8,128)(2,1)S(1)}, bf16[1,384,256]{2,1,0:T(8,128)(2,1)}, u32[]{:S(2)}) copy-start(bf16[1,384,256]{2,1,0:T(8,128)(2,1)} %copy-done.10) | copy-start | bytes 589828
  100.0 3.4 %copy-start.13 = (bf16[1,384,256]{2,1,0:T(8,128)(2,1)S(1)}, bf16[1,384,256]{2,1,0:T(8,128)(2,1)}, u32[]{:S(2)}) copy-start(bf16[1,384,256]{2,1,0:T(8,128)(2,1)} %copy-done.12) | copy-start | bytes 589828
  100.0 3.4 %copy-start.15 = (bf16[1,384,256]{2,1,0:T(8,128)(2,1)S(1)}, bf16[1,384,256]{2,1,0:T(8,128)(2,1)}, u32[]{:S(2)}) copy-start(bf16[1,384,256]{2,1,0:T(8,128)(2,1)} %copy-done.14) | copy-start | bytes 589828
  100.0 3.4 %copy-start.17 = (bf16[1,384,256]{2,1,0:T(8,128)(2,1)S(1)}, bf16[1,384,256]{2,1,0:T(8,128)(2,1)}, u32[]{:S(2)}) copy-start(bf16[1,384,256]{2,1,0:T(8,128)(2,1)} %copy-done.16) | copy-start | bytes 589828
  100.1 18.6 %collective-permute-start.6 = (f16[4,384,256]{2,1,0:T(8,128)(2,1)S(1)}, f16[4,384,256]{2,1,0:T(8,128)(2,1)S(1)}, u32[]{:S(2)}, u32[]{:S(2)}) collective-permute-start(f16[4,384,256]{2,1,0:T(8,128)(2,1)S(1)} %get-tuple-element.37), channel_id=1, source_target_pairs={{0,2},{1,3},{6,4},{7,5},{8,10},{9,11},{14,12},{15,13},{16,18},{17,... | collective-permute-start | bytes 2359304 | tf_op jit(solution)/shard_map/ppermute | solution.py:36
  119.2 19.4 %collective-permute-start.9 = (f16[4,384,256]{2,1,0:T(8,128)(2,1)S(1)}, f16[4,384,256]{2,1,0:T(8,128)(2,1)S(1)}, u32[]{:S(2)}, u32[]{:S(2)}) collective-permute-start(f16[4,384,256]{2,1,0:T(8,128)(2,1)S(1)} %add_convert_fusion.3), channel_id=1, source_target_pairs={{0,2},{1,3},{6,4},{7,5},{8,10},{9,11},{14,12},{15,13},{16,18},{17,... | collective-permute-start | bytes 2359304 | tf_op jit(solution)/shard_map/ppermute | solution.py:36
  124.1 15.6 %collective-permute-start.7 = (f16[4,384,256]{2,1,0:T(8,128)(2,1)S(1)}, f16[4,384,256]{2,1,0:T(8,128)(2,1)S(1)}, u32[]{:S(2)}, u32[]{:S(2)}) collective-permute-start(f16[4,384,256]{2,1,0:T(8,128)(2,1)S(1)} %add_convert_fusion.3), channel_id=1, source_target_pairs={{2,4},{3,5},{4,2},{5,3},{10,12},{11,13},{12,10},{13,11},{18,20},{1... | collective-permute-start | bytes 2359304 | tf_op jit(solution)/shard_map/ppermute | solution.py:36
  125.8 18.8 %collective-permute-start.23 = (f16[4,384,256]{2,1,0:T(8,128)(2,1)S(1)}, f16[4,384,256]{2,1,0:T(8,128)(2,1)S(1)}, u32[]{:S(2)}, u32[]{:S(2)}) collective-permute-start(f16[4,384,256]{2,1,0:T(8,128)(2,1)S(1)} %add_convert_fusion), channel_id=1, source_target_pairs={{0,1},{1,0},{2,3},{3,2},{4,5},{5,4},{6,7},{7,6},{8,9},{9,8},{10,11... | collective-permute-start | bytes 2359304 | tf_op jit(solution)/shard_map/ppermute | solution.py:36
  138.9 6.2 %collective-permute-start.10 = (f16[4,384,256]{2,1,0:T(8,128)(2,1)S(1)}, f16[4,384,256]{2,1,0:T(8,128)(2,1)S(1)}, u32[]{:S(2)}, u32[]{:S(2)}) collective-permute-start(f16[4,384,256]{2,1,0:T(8,128)(2,1)S(1)} %add_convert_fusion.1), channel_id=1, source_target_pairs={{2,4},{3,5},{4,2},{5,3},{10,12},{11,13},{12,10},{13,11},{18,20},{1... | collective-permute-start | bytes 2359304 | tf_op jit(solution)/shard_map/ppermute | solution.py:36
  140.1 18.6 %collective-permute-start.8 = (f16[4,384,256]{2,1,0:T(8,128)(2,1)S(1)}, f16[4,384,256]{2,1,0:T(8,128)(2,1)S(1)}, u32[]{:S(2)}, u32[]{:S(2)}) collective-permute-start(f16[4,384,256]{2,1,0:T(8,128)(2,1)S(1)} %add_convert_fusion.2), channel_id=1, source_target_pairs={{0,2},{1,3},{2,0},{3,1},{4,6},{5,7},{6,4},{7,5},{8,10},{9,11},{10,... | collective-permute-start | bytes 2359304 | tf_op jit(solution)/shard_map/ppermute | solution.py:36

commit v2 on v0

v2 whole, which is shorter than its diff:
```python
import jax
import jax.numpy as jnp
from jax import lax
from jax.experimental import pallas as pl
from jax.experimental.pallas import tpu as pltpu
from jax.sharding import PartitionSpec as P

BF16, F16, F32 = jnp.bfloat16, jnp.float16, jnp.float32
PARAMS = pltpu.CompilerParams(vmem_limit_bytes=32 * 2**20)


def gathered(amp_ladder, integrals, residual_in):
    irreps, row_blocks, block = integrals.shape[:3]
    moved = lax.all_to_all(amp_ladder, "col", split_axis=3, concat_axis=1, tiled=True)
    right = lax.all_gather(moved, "row", axis=0, tiled=True)
    left = lax.all_gather(integrals, "col", axis=3, tiled=True)
    inner = left.shape[3] * block
    columns = right.shape[3]
    left = left.reshape(irreps, row_blocks * block, inner)
    right = right.reshape(irreps, inner, columns * block)
    cycle = jnp.einsum("hik,hkj->hij", left, right, preferred_element_type=F32)
    return residual_in + cycle.reshape(irreps, row_blocks, block, columns, block)


def along_z(pairs):
    return [(2 * a + y, 2 * b + y) for a, b in pairs for y in range(2)]


SWAP_Y = [(c, c ^ 1) for c in range(8)]
SWAP_CORE = [(r, r ^ 1) for r in range(4)]
SWAP_X = [(r, r ^ 2) for r in range(4)]
XOR_Z = {d: along_z([(z, z ^ d) for z in range(4)]) for d in (1, 2, 3)}
MIDDLE = along_z([(1, 2), (2, 1)])
INWARD = along_z([(0, 1), (3, 2)])
OUTWARD = along_z([(1, 0), (2, 3)])


def col(x, pairs):
    return lax.ppermute(x, "col", pairs)


def row(x, pairs):
    return lax.ppermute(x, "row", pairs)


def after(x, *others):
    return lax.optimization_barrier((x, *others))[0]


def call(body, place, grid, ins, outs, shapes, operands, scratch=(), flops=0, **more):
    given = sum(o.size * o.dtype.itemsize for o in operands)
    made = sum(o.size * o.dtype.itemsize for o in jax.tree.leaves(shapes))
    return pl.pallas_call(
        body,
        grid_spec=pltpu.PrefetchScalarGridSpec(
            num_scalar_prefetch=1, grid=grid, in_specs=ins, out_specs=outs, scratch_shapes=list(scratch)
        ),
        out_shape=shapes,
        compiler_params=PARAMS,
        cost_estimate=pl.CostEstimate(flops=flops, bytes_accessed=given + made, transcendentals=0),
        **more,
    )(place, *operands)


def split_rows(place, pairs):
    irreps, double, lanes = pairs.shape
    rows = double // 2

    def body(_, in_ref, even_ref, odd_ref, wide):
        for n, out in enumerate((even_ref, odd_ref)):
            wide[...] = in_ref[n].astype(F32)
            for b in range(2):
                out[0, :, b * lanes : (b + 1) * lanes] = wide[pl.ds(b, rows, stride=2), :].astype(BF16)

    shape = jax.ShapeDtypeStruct((irreps // 2, rows, 2 * lanes), BF16)
    spec = pl.BlockSpec((1, rows, 2 * lanes), lambda i, _: (i, 0, 0))
    return call(
        body, place, (irreps // 2,),
        [pl.BlockSpec((2, double, lanes), lambda i, _: (i, 0, 0))],
        [spec, spec], [shape, shape], [pairs], [pltpu.VMEM((double, lanes), F32)],
    )


def pick_columns(place, amps, irrep, tables):
    _, k_blocks, block, columns, lanes = amps.shape
    sizes = [len(t) for t in tables([0, 0, 0])]

    def body(place_ref, in_ref, *refs):
        outs, wide = refs[:-1], refs[-1]
        wide[...] = in_ref[0, 0].astype(F32).reshape(wide.shape)
        for out, table in zip(outs, tables(place_ref)):
            for n, pair in enumerate(table):
                for b, j in enumerate(pair):
                    out[n, :, b * lanes : (b + 1) * lanes] = wide[pl.ds(j, block, stride=columns), :].astype(BF16)

    return call(
        body, place, (k_blocks,),
        [pl.BlockSpec((1, 1, block, columns, lanes), lambda k, _: (irrep, k, 0, 0, 0))],
        [pl.BlockSpec((n, block, 2 * lanes), lambda k, _: (0, k, 0)) for n in sizes],
        [jax.ShapeDtypeStruct((n, k_blocks * block, 2 * lanes), BF16) for n in sizes],
        [amps], [pltpu.VMEM((block * columns, lanes), F32)],
    )


def across(m):
    return (0, 2, 1, 3)[m]


def parts(place, lefts, rights, steps):
    irreps, rows, kk = lefts[0].shape
    wide = rights[0][0].shape[-1]
    flat = [b for source in rights for b in source]

    def body(place_ref, *refs):
        a_refs, refs = refs[: len(lefts)], refs[len(lefts) :]
        b_refs, outs = refs[: len(flat) * len(steps)], refs[len(flat) * len(steps) :]
        for m in range(4):

            @pl.when(pl.program_id(0) == m)
            def _():
                for n, out in enumerate(outs):
                    total = None
                    for s, a in enumerate(a_refs):
                        b = b_refs[n * len(flat) + 4 * s + m]
                        term = jnp.dot(a[0], b[0], preferred_element_type=F32)
                        total = term if total is None else total + term
                    out[0] = total

    irrep_of = lambda m, p: (p[0] ^ (((m & 1) << 1) | (m >> 1)), 0, 0)
    return call(
        body, place, (irreps,),
        [pl.BlockSpec((1, rows, kk), irrep_of)] * len(lefts)
        + [pl.BlockSpec((1, kk, wide), lambda m, p, d=d: (p[1] ^ d, 0, 0)) for d in steps for _ in flat],
        [pl.BlockSpec((1, rows, wide), irrep_of)] * len(steps),
        [jax.ShapeDtypeStruct((irreps, rows, wide), F32)] * len(steps),
        [*lefts, *(flat * len(steps))],
        flops=2 * irreps * rows * kk * wide * len(lefts) * len(steps),
    )


def column(place, lefts, pairs, other):
    irreps, rows, kk = lefts[0].shape
    wide = pairs[0][0].shape[-1]
    flat = [b for pair in pairs for b in pair]

    def body(place_ref, *refs):
        a_refs, b_refs, out = refs[:4], refs[4:-1], refs[-1]
        for m in range(4):

            @pl.when(pl.program_id(0) == m)
            def _():
                total = None
                for s, a in enumerate(a_refs):
                    b = b_refs[4 * (s // 2) + m]
                    term = jnp.dot(a[0], b[s % 2, 0], preferred_element_type=F32)
                    total = term if total is None else total + term
                out[0] = total

    irrep_of = lambda m, p: (p[0] ^ (((m & 1) << 1) | (m >> 1)), 0, 0)
    return call(
        body, place, (irreps,),
        [pl.BlockSpec((1, rows, kk), irrep_of)] * 4
        + [pl.BlockSpec((2, 1, kk, wide), lambda m, p: (0, p[2] ^ other, 0, 0))] * len(flat),
        pl.BlockSpec((1, rows, wide), irrep_of),
        jax.ShapeDtypeStruct((irreps, rows, wide), F32),
        [*lefts, *flat],
        flops=2 * irreps * rows * kk * wide * 4,
    )


def add_half(place, residual, cycle, parity, result=None):
    irreps, double, lanes = residual.shape
    rows = double // 2

    def body(_, res_ref, add_ref, *refs):
        out = refs[-1]
        for b in range(2):
            place = pl.ds(b, rows, stride=2)
            out[0, place, :] = res_ref[0, place, :] + add_ref[0, :, b * lanes : (b + 1) * lanes]

    mine = pl.BlockSpec((1, double, lanes), lambda i, _: (2 * i + parity, 0, 0))
    given = [] if result is None else [result]
    return call(
        body, place, (irreps // 2,),
        [mine, pl.BlockSpec((1, rows, 2 * lanes), lambda i, _: (i, 0, 0))] + [pl.BlockSpec(memory_space=pl.ANY)] * len(given),
        mine,
        jax.ShapeDtypeStruct(residual.shape, F32),
        [residual, cycle, *given],
        input_output_aliases={3: 0} if given else {},
    )


def mixed(amp_ladder, integrals, residual_in):
    irreps, row_blocks, block, k_blocks, _ = integrals.shape
    r, c = lax.axis_index("row"), lax.axis_index("col")
    z, y = c // 2, c % 2
    middle = (z == 1) | (z == 2)
    place = jnp.stack([r, z, y]).astype(jnp.int32)

    tables = lambda p: [[[4 * t + 2 * w + b for b in range(2)] for t in range(4)] for w in (p[2], 1 - p[2])]
    b_own, b_other = pick_columns(place, amp_ladder, 0, tables)
    a_even, g = split_rows(place, integrals.reshape(irreps, row_blocks * block * k_blocks, block))
    tables = lambda p: [[[4 * (p[1] ^ d) + 2 * w + b for b in range(2)] for w in range(2)] for d in range(4)]
    pieces = pick_columns(place, amp_ladder, 1, tables)

    hold = lax.optimization_barrier
    core = lambda a, b: [a, b, row(a, SWAP_CORE), row(b, SWAP_CORE)]

    g1 = col(g, XOR_Z[1])
    g3_mid = col(g, MIDDLE)
    b_in = col(b_other, SWAP_Y)
    x_own = row(b_own, SWAP_X)

    b_in, *pieces = hold((b_in, *pieces))
    got = [col(pieces[d], XOR_Z[d]) for d in (1, 2, 3)]
    a_in = col(after(a_even, b_in), SWAP_Y)
    x_in = row(b_in, SWAP_X)

    g1, g3_mid, x_own, x_in = hold((g1, g3_mid, x_own, x_in))
    g2_mid = col(g1, MIDDLE)
    g2_end = col(g3_mid, OUTWARD)
    b_rows = [core(b_own, x_own), core(b_in, x_in)]
    a_in, got, b_rows = hold((a_in, got, b_rows))

    (p3,) = parts(place, [a_even, a_in], b_rows, [3])
    i3 = col(p3.astype(F16), INWARD)
    near = jnp.stack([pieces[0], got[0]])
    near = core(near, row(after(near, p3), SWAP_X))
    p2, p1, p0 = parts(place, [after(a_even, p3), a_in], b_rows, [2, 1, 0])

    i3, g2_mid, g2_end, p2, near = hold((i3, g2_mid, g2_end, p2, near))
    i2 = col(p2.astype(F16), INWARD)
    m2 = col((p2 + i3.astype(F32)).astype(F16), MIDDLE)
    g3_end = col(g2_mid, OUTWARD)
    far = jnp.stack([got[1], got[2]])
    far = core(far, row(after(far, near[0]), SWAP_X))

    i2, m2, g3_end, far, p3 = hold((i2, m2, g3_end, far, p3))
    s1 = col((p1 + m2.astype(F32)).astype(F16), XOR_Z[1])
    m3 = col((p3 + i2.astype(F32)).astype(F16), MIDDLE)
    lefts = [g, g1, jnp.where(middle, g2_mid, g2_end), jnp.where(middle, g3_mid, g3_end)]
    q = col(column(place, lefts, [near, far], 1).astype(F16), SWAP_Y)
    even = (p0 + s1.astype(F32)) + m3.astype(F32)
    odd = column(place, lefts, [near, far], 0) + q.astype(F32)

    result = residual_in.reshape(irreps, row_blocks * block * 2, block)
    done = add_half(place, result, odd, 1)
    done = add_half(place, result, even, 0, done)
    return done.reshape(residual_in.shape)


def solution(mesh):
    placed = (
        P("row", "col", None, None, None),
        P(None, "row", None, "col", None),
        P(None, "row", None, "col", None),
    )

    def per_device(amp_ladder, integrals, residual_in):
        fits = mesh.shape["row"] == 4 and mesh.shape["col"] == 8
        fits = fits and amp_ladder.shape[0] == 2 and residual_in.shape[3] == 2 and amp_ladder.shape[1] == 2
        return (mixed if fits else gathered)(amp_ladder, integrals, residual_in)

    return jax.shard_map(
        per_device,
        mesh=mesh,
        in_specs=placed,
        out_specs=P(None, "row", None, "col", None),
        check_vma=False,
    )
```

time: 364 us -> 140 us (0.38)
  waiting for transfers between devices: 204 us -> 63.6 us
  local copies, waits for them, and re-layouts: 73 us -> 3.75 us
  blocking collectives: 55.3 us -> 0 us
  starting transfers between devices: 0.04 us -> 42.2 us
  Pallas kernels: 0 us -> 20.3 us
  between operations: 13.4 us -> 0.38 us
  matrix products: 12 us -> 0 us
    all_gather x2 -> x0, waiting for transfers between devices: 204 us -> none  [the longest x1 148 us: per_device(): shard_piece = lax.all_gather(integrals, 'col', axis=3, tiled=True)]
    ppermute x0 -> x28, waiting for transfers between devices: none -> 63.6 us  [the longest x16 52.3 us: col(): return lax.ppermute(x, 'col', pairs)]
    all_to_all x1 -> x0, blocking collectives: 55.3 us -> none  [per_device(): lax.all_to_all(amp_ladder, 'col', split_axis=3, concat_axis=1, tiled=True)]
    ppermute x0 -> x28, starting transfers between devices: none -> 42.2 us  [the longest x16 35.6 us: col(): return lax.ppermute(x, 'col', pairs)]
    reshape x3 -> x0, local copies, waits for them, and re-layouts: 36.9 us -> none  [the longest x1 19.3 us: per_device(): left_part = shard_piece.reshape(irreps, row_count, width_now * block)]
    all_gather x2 -> x0, local copies, waits for them, and re-layouts: 30.8 us -> none  [the longest x1 16.3 us: per_device(): cycle_amps = lax.all_gather(moved, 'row', axis=0, tiled=True)]
    pallas_call x0 -> x9, Pallas kernels: none -> 20.3 us  [call(): pl.pallas_call(body, grid_spec=pltpu.PrefetchScalarGridSpec(num_scalar_pr...]
    dot_general x1 -> x0, matrix products: 12 us -> none  [per_device(): jnp.einsum('hik,hkj->hij', left_part, right_part, preferred_element_type=...]
  transfers between devices with their start and end apart: 2 -> 28, of which waited for: 2 -> 14; matrix products, arithmetic and copies ran while one was open for 9% -> 4% of each run, Pallas kernels for 0% -> 8%
where the time goes in v2:
time: 140 us; the launch traced here: 138 us
  waiting for transfers between devices  63.6 us (45%)
  starting transfers between devices  42.2 us (30%)
  Pallas kernels  20.3 us (14%)
  other arithmetic  7.69 us (5%)
  local copies, waits for them, and re-layouts  3.75 us (3%)
    ppermute x16, waiting for transfers between devices, col(): return lax.ppermute(x, 'col', pairs)  52.3 us
    ppermute x16, starting transfers between devices, col(): return lax.ppermute(x, 'col', pairs)  35.6 us
    pallas_call x9, Pallas kernels, call(): pl.pallas_call(body, grid_spec=pltpu.PrefetchScalarGridSpec(num_scalar_pr...  20.3 us
    ppermute x12, waiting for transfers between devices, row(): return lax.ppermute(x, 'row', pairs)  11.3 us
    ppermute x12, starting transfers between devices, row(): return lax.ppermute(x, 'row', pairs)  6.64 us
    unnamed x38, local copies, waits for them, and re-layouts  3.75 us
  transfers between devices with their start and end apart: 28, of which 14 were waited for; matrix products, arithmetic and copies ran while one was open for 4% of the time, Pallas kernels for 8%

profile of v2, /device:TPU:0, one launch (start us, length us, event | category | flops | bytes accessed | tf_op | source)
XLA Modules:
  0.0 137.9 jit_solution(13777360390108574790)
XLA Ops:
  0.1 1.6 %copy-done.1 = bf16[2,2,128,16,128]{4,3,2,1,0:T(8,128)(2,1)S(1)} copy-done((bf16[2,2,128,16,128]{4,3,2,1,0:T(8,128)(2,1)S(1)}, bf16[2,2,128,16,128]{4,3,2,1,0:T(8,128)(2,1)}, u32[]{:S(2)}) %copy-start.1) | copy-done | bytes 2097176
  1.7 1.5 %shard_map.38 = (bf16[4,256,256]{2,1,0:T(8,128)(2,1)S(1)}, bf16[4,256,256]{2,1,0:T(8,128)(2,1)S(1)}) custom-call(s32[3]{0:T(128)S(1)} %pad_add_fusion._.place_ref, bf16[2,2,128,16,128]{4,3,2,1,0:T(8,128)(2,1)S(1)} %copy-done.1), custom_call_target="tpu_custom_call" | custom-call | bytes 3145728 | tf_op jit(solution)/shard_map/pallas_call | solution.py:53
  3.2 3.0 %collective-permute-start = (bf16[4,256,256]{2,1,0:T(8,128)(2,1)S(1)}, bf16[4,256,256]{2,1,0:T(8,128)(2,1)S(1)}, u32[]{:S(2)}, u32[]{:S(2)}) collective-permute-start(bf16[4,256,256]{2,1,0:T(8,128)(2,1)S(1)} %get-tuple-element.58), channel_id=1, source_target_pairs={{0,1},{1,0},{2,3},{3,2},{4,5},{5,4},{6,7},{7,6},{8,9},{9,8},{10,11... | collective-permute-start | bytes 1572872 | tf_op jit(solution)/shard_map/ppermute | solution.py:39
  6.3 1.4 %copy-done.11 = bf16[8,3,128,2,128]{4,3,2,1,0:T(2,128)(2,1)S(1)} copy-done((bf16[8,3,128,2,128]{4,3,2,1,0:T(2,128)(2,1)S(1)}, bf16[8,3,128,2,128]{4,3,2,1,0:T(2,128)(2,1)}, u32[]{:S(2)}) %copy-start.11) | copy-done | bytes 1572888
  7.7 1.1 shard_map.37
  8.7 1.6 %collective-permute-start.5 = (bf16[4,384,256]{2,1,0:T(8,128)(2,1)S(1)}, bf16[4,384,256]{2,1,0:T(8,128)(2,1)S(1)}, u32[]{:S(2)}, u32[]{:S(2)}) collective-permute-start(bf16[4,384,256]{2,1,0:T(8,128)(2,1)S(1)} %get-tuple-element.69.refs_0_), channel_id=1, source_target_pairs={{0,2},{1,3},{2,0},{3,1},{4,6},{5,7},{6,4},{7,5},{8,10},{9,11},{10,... | collective-permute-start | bytes 2359304 | tf_op jit(solution)/shard_map/ppermute | solution.py:39
  10.4 0.7 collective-permute-start.6
  11.1 1.6 %collective-permute-start.7 = (bf16[4,256,256]{2,1,0:T(8,128)(2,1)S(1)}, bf16[4,256,256]{2,1,0:T(8,128)(2,1)S(1)}, u32[]{:S(2)}, u32[]{:S(2)}) collective-permute-start(bf16[4,256,256]{2,1,0:T(8,128)(2,1)S(1)} %get-tuple-element.73.refs_2_.refs_10_.refs_18_), channel_id=1, source_target_pairs={{0,16},{8,24},{16,0},{24,8},{1,17},{9,25},{17,1},{25,9},{2,18},{10... | collective-permute-start | bytes 1572872 | tf_op jit(solution)/shard_map/ppermute | solution.py:43
  12.7 1.5 %shard_map.39 = (bf16[2,256,256]{2,1,0:T(8,128)(2,1)S(1)}, bf16[2,256,256]{2,1,0:T(8,128)(2,1)S(1)}, bf16[2,256,256]{2,1,0:T(8,128)(2,1)S(1)}, bf16[2,256,256]{2,1,0:T(8,128)(2,1)S(1)}) custom-call(s32[3]{0:T(128)S(1)} %pad_add_fusion._.place_ref, bf16[2,2,128,16,128]{4,3,2,1,0:T(8,128)(2,1)S(1)} %copy-done.2), custom_call_target="tpu_custom_call" | custom-call | bytes 3145728 | tf_op jit(solution)/shard_map/pallas_call | solution.py:53
  14.2 4.0 %collective-permute-done.refs_6_.refs_14_.refs_22_ = bf16[4,256,256]{2,1,0:T(8,128)(2,1)S(1)} collective-permute-done((bf16[4,256,256]{2,1,0:T(8,128)(2,1)S(1)}, bf16[4,256,256]{2,1,0:T(8,128)(2,1)S(1)}, u32[]{:S(2)}, u32[]{:S(2)}) %collective-permute-start) | collective-permute-done | bytes 524320 | tf_op jit(solution)/shard_map/ppermute | solution.py:39
  18.2 1.7 %collective-permute-start.8 = (bf16[4,256,256]{2,1,0:T(8,128)(2,1)S(1)}, bf16[4,256,256]{2,1,0:T(8,128)(2,1)S(1)}, u32[]{:S(2)}, u32[]{:S(2)}) collective-permute-start(bf16[4,256,256]{2,1,0:T(8,128)(2,1)S(1)} %collective-permute-done.refs_6_.refs_14_.refs_22_), channel_id=1, source_target_pairs={{0,16},{8,24},{16,0},{24,8},{1,17},{9,25},{17,1},{25,9},{2,18},{10... | collective-permute-start | bytes 1572872 | tf_op jit(solution)/shard_map/ppermute | solution.py:43
  19.9 6.1 %collective-permute-done.7.refs_3_.refs_11_.refs_19_ = bf16[4,256,256]{2,1,0:T(8,128)(2,1)S(1)} collective-permute-done((bf16[4,256,256]{2,1,0:T(8,128)(2,1)S(1)}, bf16[4,256,256]{2,1,0:T(8,128)(2,1)S(1)}, u32[]{:S(2)}, u32[]{:S(2)}) %collective-permute-start.7) | collective-permute-done | bytes 524320 | tf_op jit(solution)/shard_map/ppermute | solution.py:43
  26.0 0.5 collective-permute-start.1
  26.5 1.3 collective-permute-done.5.refs_1_
  27.8 3.1 %collective-permute-start.2 = (bf16[2,256,256]{2,1,0:T(8,128)(2,1)S(1)}, bf16[2,256,256]{2,1,0:T(8,128)(2,1)S(1)}, u32[]{:S(2)}, u32[]{:S(2)}) collective-permute-start(bf16[2,256,256]{2,1,0:T(8,128)(2,1)S(1)} %get-tuple-element.65), channel_id=1, source_target_pairs={{0,2},{1,3},{2,0},{3,1},{4,6},{5,7},{6,4},{7,5},{8,10},{9,11},{10,... | collective-permute-start | bytes 786440 | tf_op jit(solution)/shard_map/ppermute | solution.py:39
  30.9 4.6 %collective-permute-done.8.refs_7_.refs_15_.refs_23_ = bf16[4,256,256]{2,1,0:T(8,128)(2,1)S(1)} collective-permute-done((bf16[4,256,256]{2,1,0:T(8,128)(2,1)S(1)}, bf16[4,256,256]{2,1,0:T(8,128)(2,1)S(1)}, u32[]{:S(2)}, u32[]{:S(2)}) %collective-permute-start.8) | collective-permute-done | bytes 524320 | tf_op jit(solution)/shard_map/ppermute | solution.py:43
  35.5 3.8 %collective-permute-start.3 = (bf16[2,256,256]{2,1,0:T(8,128)(2,1)S(1)}, bf16[2,256,256]{2,1,0:T(8,128)(2,1)S(1)}, u32[]{:S(2)}, u32[]{:S(2)}) collective-permute-start(bf16[2,256,256]{2,1,0:T(8,128)(2,1)S(1)} %get-tuple-element.66), channel_id=1, source_target_pairs={{0,4},{1,5},{2,6},{3,7},{4,0},{5,1},{6,2},{7,3},{8,12},{9,13},{10,... | collective-permute-start | bytes 786440 | tf_op jit(solution)/shard_map/ppermute | solution.py:39
  39.3 0.5 collective-permute-start.12
  39.8 9.9 %collective-permute-done.3 = bf16[2,256,256]{2,1,0:T(8,128)(2,1)S(1)} collective-permute-done((bf16[2,256,256]{2,1,0:T(8,128)(2,1)S(1)}, bf16[2,256,256]{2,1,0:T(8,128)(2,1)S(1)}, u32[]{:S(2)}, u32[]{:S(2)}) %collective-permute-start.3) | collective-permute-done | bytes 262176 | tf_op jit(solution)/shard_map/ppermute | solution.py:39
  49.7 3.1 %collective-permute-start.4 = (bf16[2,256,256]{2,1,0:T(8,128)(2,1)S(1)}, bf16[2,256,256]{2,1,0:T(8,128)(2,1)S(1)}, u32[]{:S(2)}, u32[]{:S(2)}) collective-permute-start(bf16[2,256,256]{2,1,0:T(8,128)(2,1)S(1)} %get-tuple-element.67), channel_id=1, source_target_pairs={{0,6},{1,7},{2,4},{3,5},{4,2},{5,3},{6,0},{7,1},{8,14},{9,15},{10,... | collective-permute-start | bytes 786440 | tf_op jit(solution)/shard_map/ppermute | solution.py:39
  52.9 5.1 %collective-permute-done.4 = bf16[2,256,256]{2,1,0:T(8,128)(2,1)S(1)} collective-permute-done((bf16[2,256,256]{2,1,0:T(8,128)(2,1)S(1)}, bf16[2,256,256]{2,1,0:T(8,128)(2,1)S(1)}, u32[]{:S(2)}, u32[]{:S(2)}) %collective-permute-start.4) | collective-permute-done | bytes 262176 | tf_op jit(solution)/shard_map/ppermute | solution.py:39
  58.0 1.7 %shard_map.40 = f32[4,384,256]{2,1,0:T(8,128)S(1)} custom-call(s32[3]{0:T(128)S(1)} %pad_add_fusion._.place_ref, bf16[4,384,256]{2,1,0:T(8,128)(2,1)S(1)} %get-tuple-element.81.refs_0_, bf16[4,384,256]{2,1,0:T(8,128)(2,1)S(1)} %collective-permute-done.1.refs_1_, bf16[4,256,256]{2,1,0:T(8,128)(2,1)S(1)} %get-tuple-element.73.refs_2_.refs_10_.refs_18_, ...), custom_call_target="tpu_custom_call" | custom-call | flops 402653184 | bytes 7340032 | tf_op jit(solution)/shard_map/pallas_call | solution.py:53
  59.8 1.6 %collective-permute-start.16 = (bf16[2,2,256,256]{3,2,1,0:T(8,128)(2,1)S(1)}, bf16[2,2,256,256]{3,2,1,0:T(8,128)(2,1)S(1)}, u32[]{:S(2)}, u32[]{:S(2)}) collective-permute-start(bf16[2,2,256,256]{3,2,1,0:T(8,128)(2,1)S(1)} %pad_maximum_fusion.refs_4_), channel_id=1, source_target_pairs={{0,16},{8,24},{16,0},{24,8},{1,17},{9,25},{17,1},{25,9},{2,18},{10... | collective-permute-start | bytes 1572872 | tf_op jit(solution)/shard_map/ppermute | solution.py:43
  61.3 1.5 %collective-permute-start.14 = (bf16[4,384,256]{2,1,0:T(8,128)(2,1)S(1)}, bf16[4,384,256]{2,1,0:T(8,128)(2,1)}, u32[]{:S(2)}, u32[]{:S(2)}) collective-permute-start(bf16[4,384,256]{2,1,0:T(8,128)(2,1)S(1)} %collective-permute-done.5.refs_1_), channel_id=1, source_target_pairs={{2,4},{3,5},{4,2},{5,3},{10,12},{11,13},{12,10},{13,11},{18,20},{1... | collective-permute-start | bytes 2359304 | tf_op jit(solution)/shard_map/ppermute | solution.py:39
  62.9 1.3 collective-permute-start.15
  64.3 7.4 %collective-permute-start.13 = (f16[4,384,256]{2,1,0:T(8,128)(2,1)S(1)}, f16[4,384,256]{2,1,0:T(8,128)(2,1)S(1)}, u32[]{:S(2)}, u32[]{:S(2)}) collective-permute-start(f16[4,384,256]{2,1,0:T(8,128)(2,1)S(1)} %convert_element_type.36), channel_id=1, source_target_pairs={{0,2},{1,3},{6,4},{7,5},{8,10},{9,11},{14,12},{15,13},{16,18},{17,... | collective-permute-start | bytes 2359304 | tf_op jit(solution)/shard_map/ppermute | solution.py:39
  72.3 2.7 %shard_map.41 = (f32[4,384,256]{2,1,0:T(8,128)S(1)}, f32[4,384,256]{2,1,0:T(8,128)S(1)}, f32[4,384,256]{2,1,0:T(8,128)S(1)}) custom-call(s32[3]{0:T(128)S(1)} %pad_add_fusion._.place_ref, bf16[4,384,256]{2,1,0:T(8,128)(2,1)S(1)} %get-tuple-element.81.refs_0_, bf16[4,384,256]{2,1,0:T(8,128)(2,1)S(1)} %collective-permute-done.1.refs_1_, ...), custom_call_target="tpu_custom_call" | custom-call | flops 1207959552 | bytes 18874368 | tf_op jit(solution)/shard_map/pallas_call | solution.py:53
  75.1 9.8 %collective-permute-done.15 = bf16[4,384,256]{2,1,0:T(8,128)(2,1)S(1)} collective-permute-done((bf16[4,384,256]{2,1,0:T(8,128)(2,1)S(1)}, bf16[4,384,256]{2,1,0:T(8,128)(2,1)S(1)}, u32[]{:S(2)}, u32[]{:S(2)}) %collective-permute-start.15) | collective-permute-done | bytes 786464 | tf_op jit(solution)/shard_map/ppermute | solution.py:39
  84.9 1.4 collective-permute-done.13
  86.3 0.5 collective-permute-start.22
  86.8 1.5 %add_convert_fusion.2 = (f16[4,384,256]{2,1,0:T(8,128)(2,1)}, f16[4,384,256]{2,1,0:T(8,128)(2,1)}) fusion(f32[4,384,256]{2,1,0:T(8,128)S(1)} %get-tuple-element.90, f16[4,384,256]{2,1,0:T(8,128)(2,1)S(1)} %collective-permute-done.13), kind=kLoop, calls=%fused_computation.4 | loop fusion | flops 1572864 | bytes 3932160 | tf_op jit(solution)/shard_map/convert_element_type | solution.py:233
  88.3 5.3 %collective-permute-start.19 = (f16[4,384,256]{2,1,0:T(8,128)(2,1)}, f16[4,384,256]{2,1,0:T(8,128)(2,1)}, u32[]{:S(2)}, u32[]{:S(2)}) collective-permute-start(f16[4,384,256]{2,1,0:T(8,128)(2,1)} %get-tuple-element.110), channel_id=1, source_target_pairs={{0,2},{1,3},{6,4},{7,5},{8,10},{9,11},{14,12},{15,13},{16,18},{17,... | collective-permute-start | bytes 2359304 | tf_op jit(solution)/shard_map/ppermute | solution.py:39
  93.6 1.5 %collective-permute-start.20 = (f16[4,384,256]{2,1,0:T(8,128)(2,1)}, f16[4,384,256]{2,1,0:T(8,128)(2,1)}, u32[]{:S(2)}, u32[]{:S(2)}) collective-permute-start(f16[4,384,256]{2,1,0:T(8,128)(2,1)} %get-tuple-element.109), channel_id=1, source_target_pairs={{2,4},{3,5},{4,2},{5,3},{10,12},{11,13},{12,10},{13,11},{18,20},{1... | collective-permute-start | bytes 2359304 | tf_op jit(solution)/shard_map/ppermute | solution.py:39
  95.2 1.3 collective-permute-start.21
  97.1 1.3 broadcast_select_fusion.1.refs_2_
  98.6 7.9 %collective-permute-done.19 = f16[4,384,256]{2,1,0:T(8,128)(2,1)} collective-permute-done((f16[4,384,256]{2,1,0:T(8,128)(2,1)}, f16[4,384,256]{2,1,0:T(8,128)(2,1)}, u32[]{:S(2)}, u32[]{:S(2)}) %collective-permute-start.19) | collective-permute-done | bytes 786464 | tf_op jit(solution)/shard_map/ppermute | solution.py:39
  106.4 6.5 %collective-permute-done.21 = bf16[4,384,256]{2,1,0:T(8,128)(2,1)} collective-permute-done((bf16[4,384,256]{2,1,0:T(8,128)(2,1)}, bf16[4,384,256]{2,1,0:T(8,128)(2,1)}, u32[]{:S(2)}, u32[]{:S(2)}) %collective-permute-start.21) | collective-permute-done | bytes 786464 | tf_op jit(solution)/shard_map/ppermute | solution.py:39
  113.0 1.2 broadcast_select_fusion.refs_3_
  114.3 3.6 %shard_map.43 = f32[4,384,256]{2,1,0:T(8,128)S(1)} custom-call(s32[3]{0:T(128)S(1)} %pad_add_fusion._.place_ref, bf16[4,384,256]{2,1,0:T(8,128)(2,1)S(1)} %get-tuple-element.69.refs_0_, bf16[4,384,256]{2,1,0:T(8,128)(2,1)S(1)} %copy-done.4, bf16[4,384,256]{2,1,0:T(8,128)(2,1)S(1)} %broadcast_select_fusion.1.refs_2_, ...), custom_call_target="tpu_custom_call" | custom-call | flops 805306368 | bytes 8912896 | tf_op jit(solution)/shard_map/pallas_call | solution.py:53
  118.0 0.6 collective-permute-start.27
  118.6 0.7 copy-done.13
  119.2 1.4 add_convert_fusion.1
  120.7 1.4 %add_convert_fusion = f16[4,384,256]{2,1,0:T(8,128)(2,1)S(1)} fusion(f32[4,384,256]{2,1,0:T(8,128)S(1)} %shard_map.40, f16[4,384,256]{2,1,0:T(8,128)(2,1)} %collective-permute-done.19), kind=kLoop, calls=%fused_computation.2 | loop fusion | flops 1179648 | bytes 3145728 | tf_op jit(solution)/shard_map/convert_element_type | solution.py:240
  122.1 0.7 collective-permute-start.26
  122.8 3.6 %shard_map.42 = f32[4,384,256]{2,1,0:T(8,128)S(1)} custom-call(s32[3]{0:T(128)S(1)} %pad_add_fusion._.place_ref, bf16[4,384,256]{2,1,0:T(8,128)(2,1)S(1)} %get-tuple-element.69.refs_0_, bf16[4,384,256]{2,1,0:T(8,128)(2,1)S(1)} %copy-done.4, bf16[4,384,256]{2,1,0:T(8,128)(2,1)S(1)} %broadcast_select_fusion.1.refs_2_, ...), custom_call_target="tpu_custom_call" | custom-call | flops 805306368 | bytes 8912896 | tf_op jit(solution)/shard_map/pallas_call | solution.py:53
  126.4 6.3 %collective-permute-done.27 = f16[4,384,256]{2,1,0:T(8,128)(2,1)S(1)} collective-permute-done((f16[4,384,256]{2,1,0:T(8,128)(2,1)S(1)}, f16[4,384,256]{2,1,0:T(8,128)(2,1)S(1)}, u32[]{:S(2)}, u32[]{:S(2)}) %collective-permute-start.27) | collective-permute-done | bytes 786464 | tf_op jit(solution)/shard_map/ppermute | solution.py:39
  132.9 2.3 %shard_map.44.refs_0_ = f32[8,768,128]{2,1,0:T(8,128)} custom-call(s32[3]{0:T(128)S(1)} %pad_add_fusion._.place_ref, f32[8,768,128]{2,1,0:T(8,128)S(1)} %bitcast.10, f32[4,384,256]{2,1,0:T(8,128)S(1)} %convert_add_fusion.add_ref), custom_call_target="tpu_custom_call" | custom-call | bytes 7864320 | tf_op jit(solution)/shard_map/pallas_call | solution.py:53
  135.6 2.3 %shard_map.45 = f32[8,768,128]{2,1,0:T(8,128)} custom-call(s32[3]{0:T(128)S(1)} %pad_add_fusion._.place_ref, f32[8,768,128]{2,1,0:T(8,128)S(1)} %bitcast.11, f32[4,384,256]{2,1,0:T(8,128)S(1)} %convert_add_fusion.1.add_ref, f32[8,768,128]{2,1,0:T(8,128)} %shard_map.44.refs_0_), custom_call_target="tpu_custom_call", output_to_operand_aliasing={{}: (3, {})} | custom-call | bytes 11010048 | tf_op jit(solution)/shard_map/pallas_call | solution.py:53
  (67 shorter events, 2.5 us)
Async XLA Ops:
  0.1 1.6 %copy-start.1 = (bf16[2,2,128,16,128]{4,3,2,1,0:T(8,128)(2,1)S(1)}, bf16[2,2,128,16,128]{4,3,2,1,0:T(8,128)(2,1)}, u32[]{:S(2)}) copy-start(bf16[2,2,128,16,128]{4,3,2,1,0:T(8,128)(2,1)} %in_ref.3) | copy-start | bytes 6291460
  1.7 11.0 %copy-start.2 = (bf16[2,2,128,16,128]{4,3,2,1,0:T(8,128)(2,1)S(1)}, bf16[2,2,128,16,128]{4,3,2,1,0:T(8,128)(2,1)}, u32[]{:S(2)}) copy-start(bf16[2,2,128,16,128]{4,3,2,1,0:T(8,128)(2,1)} %in_ref.3) | copy-start | bytes 6291460
  3.2 15.0 %collective-permute-start = (bf16[4,256,256]{2,1,0:T(8,128)(2,1)S(1)}, bf16[4,256,256]{2,1,0:T(8,128)(2,1)S(1)}, u32[]{:S(2)}, u32[]{:S(2)}) collective-permute-start(bf16[4,256,256]{2,1,0:T(8,128)(2,1)S(1)} %get-tuple-element.58), channel_id=1, source_target_pairs={{0,1},{1,0},{2,3},{3,2},{4,5},{5,4},{6,7},{7,6},{8,9},{9,8},{10,11... | collective-permute-start | bytes 1572872 | tf_op jit(solution)/shard_map/ppermute | solution.py:39
  6.3 1.4 %copy-start.11 = (bf16[8,3,128,2,128]{4,3,2,1,0:T(2,128)(2,1)S(1)}, bf16[8,3,128,2,128]{4,3,2,1,0:T(2,128)(2,1)}, u32[]{:S(2)}) copy-start(bf16[8,3,128,2,128]{4,3,2,1,0:T(2,128)(2,1)} %param.4) | copy-start | bytes 4718596
  8.7 19.1 %collective-permute-start.5 = (bf16[4,384,256]{2,1,0:T(8,128)(2,1)S(1)}, bf16[4,384,256]{2,1,0:T(8,128)(2,1)S(1)}, u32[]{:S(2)}, u32[]{:S(2)}) collective-permute-start(bf16[4,384,256]{2,1,0:T(8,128)(2,1)S(1)} %get-tuple-element.69.refs_0_), channel_id=1, source_target_pairs={{0,2},{1,3},{2,0},{3,1},{4,6},{5,7},{6,4},{7,5},{8,10},{9,11},{10,... | collective-permute-start | bytes 2359304 | tf_op jit(solution)/shard_map/ppermute | solution.py:39
  10.4 20.5 %collective-permute-start.6 = (bf16[4,384,256]{2,1,0:T(8,128)(2,1)S(1)}, bf16[4,384,256]{2,1,0:T(8,128)(2,1)S(1)}, u32[]{:S(2)}, u32[]{:S(2)}) collective-permute-start(bf16[4,384,256]{2,1,0:T(8,128)(2,1)S(1)} %get-tuple-element.69.refs_0_), channel_id=1, source_target_pairs={{2,4},{3,5},{4,2},{5,3},{10,12},{11,13},{12,10},{13,11},{18,20},{1... | collective-permute-start | bytes 2359304 | tf_op jit(solution)/shard_map/ppermute | solution.py:39
  11.1 14.9 %collective-permute-start.7 = (bf16[4,256,256]{2,1,0:T(8,128)(2,1)S(1)}, bf16[4,256,256]{2,1,0:T(8,128)(2,1)S(1)}, u32[]{:S(2)}, u32[]{:S(2)}) collective-permute-start(bf16[4,256,256]{2,1,0:T(8,128)(2,1)S(1)} %get-tuple-element.73.refs_2_.refs_10_.refs_18_), channel_id=1, source_target_pairs={{0,16},{8,24},{16,0},{24,8},{1,17},{9,25},{17,1},{25,9},{2,18},{10... | collective-permute-start | bytes 1572872 | tf_op jit(solution)/shard_map/ppermute | solution.py:43
  18.2 17.3 %collective-permute-start.8 = (bf16[4,256,256]{2,1,0:T(8,128)(2,1)S(1)}, bf16[4,256,256]{2,1,0:T(8,128)(2,1)S(1)}, u32[]{:S(2)}, u32[]{:S(2)}) collective-permute-start(bf16[4,256,256]{2,1,0:T(8,128)(2,1)S(1)} %collective-permute-done.refs_6_.refs_14_.refs_22_), channel_id=1, source_target_pairs={{0,16},{8,24},{16,0},{24,8},{1,17},{9,25},{17,1},{25,9},{2,18},{10... | collective-permute-start | bytes 1572872 | tf_op jit(solution)/shard_map/ppermute | solution.py:43
  19.9 19.4 %collective-permute-start.9 = (bf16[4,256,256]{2,1,0:T(8,128)(2,1)S(1)}, bf16[4,256,256]{2,1,0:T(8,128)(2,1)S(1)}, u32[]{:S(2)}, u32[]{:S(2)}) collective-permute-start(bf16[4,256,256]{2,1,0:T(8,128)(2,1)S(1)} %get-tuple-element.73.refs_2_.refs_10_.refs_18_), channel_id=1, source_target_pairs={{0,8},{8,0},{16,24},{24,16},{1,9},{9,1},{17,25},{25,17},{2,10},{10... | collective-permute-start | bytes 1572872 | tf_op jit(solution)/shard_map/ppermute | solution.py:43
  26.0 31.9 %collective-permute-start.1 = (bf16[4,384,256]{2,1,0:T(8,128)(2,1)S(1)}, bf16[4,384,256]{2,1,0:T(8,128)(2,1)S(1)}, u32[]{:S(2)}, u32[]{:S(2)}) collective-permute-start(bf16[4,384,256]{2,1,0:T(8,128)(2,1)S(1)} %get-tuple-element.81.refs_0_), channel_id=1, source_target_pairs={{0,1},{1,0},{2,3},{3,2},{4,5},{5,4},{6,7},{7,6},{8,9},{9,8},{10,11... | collective-permute-start | bytes 2359304 | tf_op jit(solution)/shard_map/ppermute | solution.py:39
  27.8 33.5 %copy-start.3 = (bf16[4,384,256]{2,1,0:T(8,128)(2,1)}, bf16[4,384,256]{2,1,0:T(8,128)(2,1)S(1)}, u32[]{:S(2)}) copy-start(bf16[4,384,256]{2,1,0:T(8,128)(2,1)S(1)} %collective-permute-done.5.refs_1_) | copy-start | bytes 2359300
  27.8 11.5 %collective-permute-start.2 = (bf16[2,256,256]{2,1,0:T(8,128)(2,1)S(1)}, bf16[2,256,256]{2,1,0:T(8,128)(2,1)S(1)}, u32[]{:S(2)}, u32[]{:S(2)}) collective-permute-start(bf16[2,256,256]{2,1,0:T(8,128)(2,1)S(1)} %get-tuple-element.65), channel_id=1, source_target_pairs={{0,2},{1,3},{2,0},{3,1},{4,6},{5,7},{6,4},{7,5},{8,10},{9,11},{10,... | collective-permute-start | bytes 786440 | tf_op jit(solution)/shard_map/ppermute | solution.py:39
  30.9 32.0 %copy-start.16 = (bf16[4,384,256]{2,1,0:T(8,128)(2,1)}, bf16[4,384,256]{2,1,0:T(8,128)(2,1)S(1)}, u32[]{:S(2)}) copy-start(bf16[4,384,256]{2,1,0:T(8,128)(2,1)S(1)} %collective-permute-done.6) | copy-start | bytes 2359300
  30.9 27.1 %collective-permute-start.11 = (bf16[4,256,256]{2,1,0:T(8,128)(2,1)S(1)}, bf16[4,256,256]{2,1,0:T(8,128)(2,1)S(1)}, u32[]{:S(2)}, u32[]{:S(2)}) collective-permute-start(bf16[4,256,256]{2,1,0:T(8,128)(2,1)S(1)} %collective-permute-done.refs_6_.refs_14_.refs_22_), channel_id=1, source_target_pairs={{0,8},{8,0},{16,24},{24,16},{1,9},{9,1},{17,25},{25,17},{2,10},{10... | collective-permute-start | bytes 1572872 | tf_op jit(solution)/shard_map/ppermute | solution.py:43
  35.5 14.2 %collective-permute-start.3 = (bf16[2,256,256]{2,1,0:T(8,128)(2,1)S(1)}, bf16[2,256,256]{2,1,0:T(8,128)(2,1)S(1)}, u32[]{:S(2)}, u32[]{:S(2)}) collective-permute-start(bf16[2,256,256]{2,1,0:T(8,128)(2,1)S(1)} %get-tuple-element.66), channel_id=1, source_target_pairs={{0,4},{1,5},{2,6},{3,7},{4,0},{5,1},{6,2},{7,3},{8,12},{9,13},{10,... | collective-permute-start | bytes 786440 | tf_op jit(solution)/shard_map/ppermute | solution.py:39
  39.3 18.7 %collective-permute-start.10 = (bf16[4,256,256]{2,1,0:T(8,128)(2,1)S(1)}, bf16[4,256,256]{2,1,0:T(8,128)(2,1)S(1)}, u32[]{:S(2)}, u32[]{:S(2)}) collective-permute-start(bf16[4,256,256]{2,1,0:T(8,128)(2,1)S(1)} %collective-permute-done.7.refs_3_.refs_11_.refs_19_), channel_id=1, source_target_pairs={{0,8},{8,0},{16,24},{24,16},{1,9},{9,1},{17,25},{25,17},{2,10},{10... | collective-permute-start | bytes 1572872 | tf_op jit(solution)/shard_map/ppermute | solution.py:43
  39.3 18.7 %collective-permute-start.12 = (bf16[4,256,256]{2,1,0:T(8,128)(2,1)S(1)}, bf16[4,256,256]{2,1,0:T(8,128)(2,1)S(1)}, u32[]{:S(2)}, u32[]{:S(2)}) collective-permute-start(bf16[4,256,256]{2,1,0:T(8,128)(2,1)S(1)} %collective-permute-done.8.refs_7_.refs_15_.refs_23_), channel_id=1, source_target_pairs={{0,8},{8,0},{16,24},{24,16},{1,9},{9,1},{17,25},{25,17},{2,10},{10... | collective-permute-start | bytes 1572872 | tf_op jit(solution)/shard_map/ppermute | solution.py:43
  49.7 8.2 %collective-permute-start.4 = (bf16[2,256,256]{2,1,0:T(8,128)(2,1)S(1)}, bf16[2,256,256]{2,1,0:T(8,128)(2,1)S(1)}, u32[]{:S(2)}, u32[]{:S(2)}) collective-permute-start(bf16[2,256,256]{2,1,0:T(8,128)(2,1)S(1)} %get-tuple-element.67), channel_id=1, source_target_pairs={{0,6},{1,7},{2,4},{3,5},{4,2},{5,3},{6,0},{7,1},{8,14},{9,15},{10,... | collective-permute-start | bytes 786440 | tf_op jit(solution)/shard_map/ppermute | solution.py:39
  59.8 12.0 %collective-permute-start.16 = (bf16[2,2,256,256]{3,2,1,0:T(8,128)(2,1)S(1)}, bf16[2,2,256,256]{3,2,1,0:T(8,128)(2,1)S(1)}, u32[]{:S(2)}, u32[]{:S(2)}) collective-permute-start(bf16[2,2,256,256]{3,2,1,0:T(8,128)(2,1)S(1)} %pad_maximum_fusion.refs_4_), channel_id=1, source_target_pairs={{0,16},{8,24},{16,0},{24,8},{1,17},{9,25},{17,1},{25,9},{2,18},{10... | collective-permute-start | bytes 1572872 | tf_op jit(solution)/shard_map/ppermute | solution.py:43
  61.3 13.8 %collective-permute-start.14 = (bf16[4,384,256]{2,1,0:T(8,128)(2,1)S(1)}, bf16[4,384,256]{2,1,0:T(8,128)(2,1)}, u32[]{:S(2)}, u32[]{:S(2)}) collective-permute-start(bf16[4,384,256]{2,1,0:T(8,128)(2,1)S(1)} %collective-permute-done.5.refs_1_), channel_id=1, source_target_pairs={{2,4},{3,5},{4,2},{5,3},{10,12},{11,13},{12,10},{13,11},{18,20},{1... | collective-permute-start | bytes 2359304 | tf_op jit(solution)/shard_map/ppermute | solution.py:39
  62.9 22.0 %collective-permute-start.15 = (bf16[4,384,256]{2,1,0:T(8,128)(2,1)S(1)}, bf16[4,384,256]{2,1,0:T(8,128)(2,1)S(1)}, u32[]{:S(2)}, u32[]{:S(2)}) collective-permute-start(bf16[4,384,256]{2,1,0:T(8,128)(2,1)S(1)} %collective-permute-done.6), channel_id=1, source_target_pairs={{2,0},{3,1},{4,6},{5,7},{10,8},{11,9},{12,14},{13,15},{18,16},{19,... | collective-permute-start | bytes 2359304 | tf_op jit(solution)/shard_map/ppermute | solution.py:39
  64.3 21.9 %collective-permute-start.13 = (f16[4,384,256]{2,1,0:T(8,128)(2,1)S(1)}, f16[4,384,256]{2,1,0:T(8,128)(2,1)S(1)}, u32[]{:S(2)}, u32[]{:S(2)}) collective-permute-start(f16[4,384,256]{2,1,0:T(8,128)(2,1)S(1)} %convert_element_type.36), channel_id=1, source_target_pairs={{0,2},{1,3},{6,4},{7,5},{8,10},{9,11},{14,12},{15,13},{16,18},{17,... | collective-permute-start | bytes 2359304 | tf_op jit(solution)/shard_map/ppermute | solution.py:39
  71.7 13.2 %collective-permute-start.17 = (bf16[2,2,256,256]{3,2,1,0:T(8,128)(2,1)S(1)}, bf16[2,2,256,256]{3,2,1,0:T(8,128)(2,1)S(1)}, u32[]{:S(2)}, u32[]{:S(2)}) collective-permute-start(bf16[2,2,256,256]{3,2,1,0:T(8,128)(2,1)S(1)} %pad_maximum_fusion.refs_4_), channel_id=1, source_target_pairs={{0,8},{8,0},{16,24},{24,16},{1,9},{9,1},{17,25},{25,17},{2,10},{10... | collective-permute-start | bytes 1572872 | tf_op jit(solution)/shard_map/ppermute | solution.py:43
  71.8 3.2 %copy-start.5 = (bf16[2,2,256,256]{3,2,1,0:T(8,128)(2,1)}, bf16[2,2,256,256]{3,2,1,0:T(8,128)(2,1)S(1)}, u32[]{:S(2)}) copy-start(bf16[2,2,256,256]{3,2,1,0:T(8,128)(2,1)S(1)} %collective-permute-done.16.refs_5_) | copy-start | bytes 1572868
  71.8 14.4 %collective-permute-start.18 = (bf16[2,2,256,256]{3,2,1,0:T(8,128)(2,1)S(1)}, bf16[2,2,256,256]{3,2,1,0:T(8,128)(2,1)S(1)}, u32[]{:S(2)}, u32[]{:S(2)}) collective-permute-start(bf16[2,2,256,256]{3,2,1,0:T(8,128)(2,1)S(1)} %collective-permute-done.16.refs_5_), channel_id=1, source_target_pairs={{0,8},{8,0},{16,24},{24,16},{1,9},{9,1},{17,25},{25,17},{2,10},{10... | collective-permute-start | bytes 1572872 | tf_op jit(solution)/shard_map/ppermute | solution.py:43
  75.0 13.3 %copy-start.12 = (f32[4,384,256]{2,1,0:T(8,128)}, f32[4,384,256]{2,1,0:T(8,128)S(1)}, u32[]{:S(2)}) copy-start(f32[4,384,256]{2,1,0:T(8,128)S(1)} %get-tuple-element.83) | copy-start | bytes 4718596
  75.1 13.3 %copy-start.14 = (f32[4,384,256]{2,1,0:T(8,128)}, f32[4,384,256]{2,1,0:T(8,128)S(1)}, u32[]{:S(2)}) copy-start(f32[4,384,256]{2,1,0:T(8,128)S(1)} %get-tuple-element.82) | copy-start | bytes 4718596
  84.9 3.4 %copy-start.18 = (bf16[4,384,256]{2,1,0:T(8,128)(2,1)}, bf16[4,384,256]{2,1,0:T(8,128)(2,1)S(1)}, u32[]{:S(2)}) copy-start(bf16[4,384,256]{2,1,0:T(8,128)(2,1)S(1)} %collective-permute-done.15) | copy-start | bytes 2359300
  84.9 3.4 %copy-start.7 = (bf16[2,2,256,256]{3,2,1,0:T(8,128)(2,1)}, bf16[2,2,256,256]{3,2,1,0:T(8,128)(2,1)S(1)}, u32[]{:S(2)}) copy-start(bf16[2,2,256,256]{3,2,1,0:T(8,128)(2,1)S(1)} %collective-permute-done.17.refs_6_) | copy-start | bytes 1572868
  86.3 2.1 %copy-start.9 = (bf16[2,2,256,256]{3,2,1,0:T(8,128)(2,1)}, bf16[2,2,256,256]{3,2,1,0:T(8,128)(2,1)S(1)}, u32[]{:S(2)}) copy-start(bf16[2,2,256,256]{3,2,1,0:T(8,128)(2,1)S(1)} %collective-permute-done.18.refs_7_) | copy-start | bytes 1572868
  86.3 10.6 %collective-permute-start.22 = (bf16[2,2,256,256]{3,2,1,0:T(8,128)(2,1)S(1)}, bf16[2,2,256,256]{3,2,1,0:T(8,128)(2,1)}, u32[]{:S(2)}, u32[]{:S(2)}) collective-permute-start(bf16[2,2,256,256]{3,2,1,0:T(8,128)(2,1)S(1)} %pad_maximum_fusion.1.refs_8_), channel_id=1, source_target_pairs={{0,16},{8,24},{16,0},{24,8},{1,17},{9,25},{17,1},{25,9},{2,18},{10... | collective-permute-start | bytes 1572872 | tf_op jit(solution)/shard_map/ppermute | solution.py:43
  88.3 18.1 %collective-permute-start.19 = (f16[4,384,256]{2,1,0:T(8,128)(2,1)}, f16[4,384,256]{2,1,0:T(8,128)(2,1)}, u32[]{:S(2)}, u32[]{:S(2)}) collective-permute-start(f16[4,384,256]{2,1,0:T(8,128)(2,1)} %get-tuple-element.110), channel_id=1, source_target_pairs={{0,2},{1,3},{6,4},{7,5},{8,10},{9,11},{14,12},{15,13},{16,18},{17,... | collective-permute-start | bytes 2359304 | tf_op jit(solution)/shard_map/ppermute | solution.py:39
  93.6 12.8 %collective-permute-start.20 = (f16[4,384,256]{2,1,0:T(8,128)(2,1)}, f16[4,384,256]{2,1,0:T(8,128)(2,1)}, u32[]{:S(2)}, u32[]{:S(2)}) collective-permute-start(f16[4,384,256]{2,1,0:T(8,128)(2,1)} %get-tuple-element.109), channel_id=1, source_target_pairs={{2,4},{3,5},{4,2},{5,3},{10,12},{11,13},{12,10},{13,11},{18,20},{1... | collective-permute-start | bytes 2359304 | tf_op jit(solution)/shard_map/ppermute | solution.py:39
  95.2 17.8 %collective-permute-start.21 = (bf16[4,384,256]{2,1,0:T(8,128)(2,1)}, bf16[4,384,256]{2,1,0:T(8,128)(2,1)}, u32[]{:S(2)}, u32[]{:S(2)}) collective-permute-start(bf16[4,384,256]{2,1,0:T(8,128)(2,1)} %collective-permute-done.14), channel_id=1, source_target_pairs={{2,0},{3,1},{4,6},{5,7},{10,8},{11,9},{12,14},{13,15},{18,16},{19,... | collective-permute-start | bytes 2359304 | tf_op jit(solution)/shard_map/ppermute | solution.py:39
  96.5 2.1 %collective-permute-start.23 = (bf16[2,2,256,256]{3,2,1,0:T(8,128)(2,1)S(1)}, bf16[2,2,256,256]{3,2,1,0:T(8,128)(2,1)}, u32[]{:S(2)}, u32[]{:S(2)}) collective-permute-start(bf16[2,2,256,256]{3,2,1,0:T(8,128)(2,1)S(1)} %pad_maximum_fusion.1.refs_8_), channel_id=1, source_target_pairs={{0,8},{8,0},{16,24},{24,16},{1,9},{9,1},{17,25},{25,17},{2,10},{10... | collective-permute-start | bytes 1572872 | tf_op jit(solution)/shard_map/ppermute | solution.py:43
  96.9 16.1 %collective-permute-start.24 = (bf16[2,2,256,256]{3,2,1,0:T(8,128)(2,1)}, bf16[2,2,256,256]{3,2,1,0:T(8,128)(2,1)}, u32[]{:S(2)}, u32[]{:S(2)}) collective-permute-start(bf16[2,2,256,256]{3,2,1,0:T(8,128)(2,1)} %collective-permute-done.22.refs_9_), channel_id=1, source_target_pairs={{0,8},{8,0},{16,24},{24,16},{1,9},{9,1},{17,25},{25,17},{2,10},{10... | collective-permute-start | bytes 1572872 | tf_op jit(solution)/shard_map/ppermute | solution.py:43
  97.0 15.9 %copy-start.17 = (bf16[4,384,256]{2,1,0:T(8,128)(2,1)S(1)}, bf16[4,384,256]{2,1,0:T(8,128)(2,1)}, u32[]{:S(2)}) copy-start(bf16[4,384,256]{2,1,0:T(8,128)(2,1)} %copy-done.16) | copy-start | bytes 2359300
  98.3 15.9 %copy-start.4 = (bf16[4,384,256]{2,1,0:T(8,128)(2,1)S(1)}, bf16[4,384,256]{2,1,0:T(8,128)(2,1)}, u32[]{:S(2)}) copy-start(bf16[4,384,256]{2,1,0:T(8,128)(2,1)} %copy-done.3) | copy-start | bytes 2359300
  98.4 15.9 %copy-start.6 = (bf16[2,2,256,256]{3,2,1,0:T(8,128)(2,1)S(1)}, bf16[2,2,256,256]{3,2,1,0:T(8,128)(2,1)}, u32[]{:S(2)}) copy-start(bf16[2,2,256,256]{3,2,1,0:T(8,128)(2,1)} %copy-done.5) | copy-start | bytes 1572868
  98.4 15.9 %copy-start.8 = (bf16[2,2,256,256]{3,2,1,0:T(8,128)(2,1)S(1)}, bf16[2,2,256,256]{3,2,1,0:T(8,128)(2,1)}, u32[]{:S(2)}) copy-start(bf16[2,2,256,256]{3,2,1,0:T(8,128)(2,1)} %copy-done.7) | copy-start | bytes 1572868
  98.4 15.9 %copy-start.10 = (bf16[2,2,256,256]{3,2,1,0:T(8,128)(2,1)S(1)}, bf16[2,2,256,256]{3,2,1,0:T(8,128)(2,1)}, u32[]{:S(2)}) copy-start(bf16[2,2,256,256]{3,2,1,0:T(8,128)(2,1)} %copy-done.9) | copy-start | bytes 1572868
  117.8 1.4 %copy-start.13 = (f32[4,384,256]{2,1,0:T(8,128)S(1)}, f32[4,384,256]{2,1,0:T(8,128)}, u32[]{:S(2)}) copy-start(f32[4,384,256]{2,1,0:T(8,128)} %copy-done.12) | copy-start | bytes 4718596
  118.0 14.7 %collective-permute-start.27 = (f16[4,384,256]{2,1,0:T(8,128)(2,1)S(1)}, f16[4,384,256]{2,1,0:T(8,128)(2,1)S(1)}, u32[]{:S(2)}, u32[]{:S(2)}) collective-permute-start(f16[4,384,256]{2,1,0:T(8,128)(2,1)S(1)} %convert_element_type.46), channel_id=1, source_target_pairs={{0,1},{1,0},{2,3},{3,2},{4,5},{5,4},{6,7},{7,6},{8,9},{9,8},{10,11... | collective-permute-start | bytes 2359304 | tf_op jit(solution)/shard_map/ppermute | solution.py:39
  120.6 14.7 %collective-permute-start.25 = (f16[4,384,256]{2,1,0:T(8,128)(2,1)S(1)}, f16[4,384,256]{2,1,0:T(8,128)(2,1)S(1)}, u32[]{:S(2)}, u32[]{:S(2)}) collective-permute-start(f16[4,384,256]{2,1,0:T(8,128)(2,1)S(1)} %add_convert_fusion.1), channel_id=1, source_target_pairs={{0,2},{1,3},{2,0},{3,1},{4,6},{5,7},{6,4},{7,5},{8,10},{9,11},{10,... | collective-permute-start | bytes 2359304 | tf_op jit(solution)/shard_map/ppermute | solution.py:39
  122.1 13.2 %collective-permute-start.26 = (f16[4,384,256]{2,1,0:T(8,128)(2,1)S(1)}, f16[4,384,256]{2,1,0:T(8,128)(2,1)S(1)}, u32[]{:S(2)}, u32[]{:S(2)}) collective-permute-start(f16[4,384,256]{2,1,0:T(8,128)(2,1)S(1)} %add_convert_fusion), channel_id=1, source_target_pairs={{2,4},{3,5},{4,2},{5,3},{10,12},{11,13},{12,10},{13,11},{18,20},{1... | collective-permute-start | bytes 2359304 | tf_op jit(solution)/shard_map/ppermute | solution.py:39
  126.4 6.5 %copy-start = (f32[8,3,128,2,128]{4,3,2,1,0:T(2,128)S(1)}, f32[8,3,128,2,128]{4,3,2,1,0:T(2,128)}, u32[]{:S(2)}) copy-start(f32[8,3,128,2,128]{4,3,2,1,0:T(2,128)} %param.5) | copy-start | bytes 9437188
  132.9 2.4 %copy-start.15 = (f32[4,384,256]{2,1,0:T(8,128)S(1)}, f32[4,384,256]{2,1,0:T(8,128)}, u32[]{:S(2)}) copy-start(f32[4,384,256]{2,1,0:T(8,128)} %copy-done.14) | copy-start | bytes 4718596

commit v3 on v2

--- a/solution.py
+++ b/solution.py
@@ -6,6 +6,8 @@
 from jax.sharding import PartitionSpec as P
 
 BF16, F16, F32 = jnp.bfloat16, jnp.float16, jnp.float32
+WIRE = 32.0
+LONG = 48 * 2**20
 PARAMS = pltpu.CompilerParams(vmem_limit_bytes=32 * 2**20)
 
 
@@ -43,13 +45,19 @@
     return lax.ppermute(x, "row", pairs)
 
 
+def to_wire(x, pairs):
+    return col((x * WIRE).astype(F16), pairs)
+
+
+def from_wire(x):
+    return x.astype(F32) * (1 / WIRE)
+
+
 def after(x, *others):
     return lax.optimization_barrier((x, *others))[0]
 
 
-def call(body, place, grid, ins, outs, shapes, operands, scratch=(), flops=0, **more):
-    given = sum(o.size * o.dtype.itemsize for o in operands)
-    made = sum(o.size * o.dtype.itemsize for o in jax.tree.leaves(shapes))
+def call(body, place, grid, ins, outs, shapes, operands, scratch=(), cost=0, **more):
     return pl.pallas_call(
         body,
         grid_spec=pltpu.PrefetchScalarGridSpec(
@@ -57,7 +65,7 @@
         ),
         out_shape=shapes,
         compiler_params=PARAMS,
-        cost_estimate=pl.CostEstimate(flops=flops, bytes_accessed=given + made, transcendentals=0),
+        cost_estimate=pl.CostEstimate(flops=0, bytes_accessed=cost, transcendentals=0),
         **more,
     )(place, *operands)
 
@@ -106,7 +114,7 @@
     return (0, 2, 1, 3)[m]
 
 
-def parts(place, lefts, rights, steps):
+def parts(place, lefts, rights, steps, cost=0):
     irreps, rows, kk = lefts[0].shape
     wide = rights[0][0].shape[-1]
     flat = [b for source in rights for b in source]
@@ -134,59 +142,72 @@
         [pl.BlockSpec((1, rows, wide), irrep_of)] * len(steps),
         [jax.ShapeDtypeStruct((irreps, rows, wide), F32)] * len(steps),
         [*lefts, *(flat * len(steps))],
-        flops=2 * irreps * rows * kk * wide * len(lefts) * len(steps),
-    )
-
-
-def column(place, lefts, pairs, other):
-    irreps, rows, kk = lefts[0].shape
-    wide = pairs[0][0].shape[-1]
-    flat = [b for pair in pairs for b in pair]
+        cost=cost,
+    )
+
+
+def column(place, terms, other, cost, start=None):
+    irreps, rows, kk = terms[0][0].shape
+    wide = terms[0][1][0].shape[-1]
+    lefts = [t[0] for t in terms]
+    flat = [b for t in terms for b in t[1]]
+    given = [] if start is None else [start]
 
     def body(place_ref, *refs):
-        a_refs, b_refs, out = refs[:4], refs[4:-1], refs[-1]
+        a_refs, b_refs, out = refs[: len(terms)], refs[len(terms) : 5 * len(terms)], refs[-1]
         for m in range(4):
 
             @pl.when(pl.program_id(0) == m)
             def _():
-                total = None
+                total = refs[-2][0] if given else None
                 for s, a in enumerate(a_refs):
-                    b = b_refs[4 * (s // 2) + m]
-                    term = jnp.dot(a[0], b[s % 2, 0], preferred_element_type=F32)
+                    term = jnp.dot(a[0], b_refs[4 * s + m][0, 0], preferred_element_type=F32)
                     total = term if total is None else total + term
                 out[0] = total
 
     irrep_of = lambda m, p: (p[0] ^ (((m & 1) << 1) | (m >> 1)), 0, 0)
+    sums = pl.BlockSpec((1, rows, wide), irrep_of)
     return call(
         body, place, (irreps,),
-        [pl.BlockSpec((1, rows, kk), irrep_of)] * 4
-        + [pl.BlockSpec((2, 1, kk, wide), lambda m, p: (0, p[2] ^ other, 0, 0))] * len(flat),
-        pl.BlockSpec((1, rows, wide), irrep_of),
+        [pl.BlockSpec((1, rows, kk), irrep_of)] * len(terms)
+        + [pl.BlockSpec((1, 1, kk, wide), lambda m, p, n=t[2]: (n, p[2] ^ other, 0, 0)) for t in terms for _ in range(4)]
+        + [sums] * len(given),
+        sums,
         jax.ShapeDtypeStruct((irreps, rows, wide), F32),
-        [*lefts, *flat],
-        flops=2 * irreps * rows * kk * wide * 4,
-    )
-
-
-def add_half(place, residual, cycle, parity, result=None):
+        [*lefts, *flat, *given],
+        cost=cost,
+    )
+
+
+def stretch(place, cost):
+    def body(in_ref, out_ref):
+        for n in range(place.shape[0]):
+            out_ref[n] = in_ref[n]
+
+    return pl.pallas_call(
+        body,
+        in_specs=[pl.BlockSpec(memory_space=pltpu.SMEM)],
+        out_specs=pl.BlockSpec(memory_space=pltpu.SMEM),
+        out_shape=jax.ShapeDtypeStruct(place.shape, place.dtype),
+        cost_estimate=pl.CostEstimate(flops=0, bytes_accessed=cost, transcendentals=0),
+    )(place)
+
+
+def add_all(place, residual, even, odd):
     irreps, double, lanes = residual.shape
     rows = double // 2
 
-    def body(_, res_ref, add_ref, *refs):
-        out = refs[-1]
-        for b in range(2):
-            place = pl.ds(b, rows, stride=2)
-            out[0, place, :] = res_ref[0, place, :] + add_ref[0, :, b * lanes : (b + 1) * lanes]
-
-    mine = pl.BlockSpec((1, double, lanes), lambda i, _: (2 * i + parity, 0, 0))
-    given = [] if result is None else [result]
-    return call(
-        body, place, (irreps // 2,),
-        [mine, pl.BlockSpec((1, rows, 2 * lanes), lambda i, _: (i, 0, 0))] + [pl.BlockSpec(memory_space=pl.ANY)] * len(given),
-        mine,
-        jax.ShapeDtypeStruct(residual.shape, F32),
-        [residual, cycle, *given],
-        input_output_aliases={3: 0} if given else {},
+    def body(_, res_ref, even_ref, odd_ref, out):
+        for n, add_ref in enumerate((even_ref, odd_ref)):
+            for b in range(2):
+                spot = pl.ds(b, rows, stride=2)
+                out[n, spot, :] = res_ref[n, spot, :] + add_ref[0, :, b * lanes : (b + 1) * lanes]
+
+    pair = pl.BlockSpec((2, double, lanes), lambda i, _: (i, 0, 0))
+    half = pl.BlockSpec((1, rows, 2 * lanes), lambda i, _: (i, 0, 0))
+    return call(
+        body, place, (irreps // 2,), [pair, half, half], pair,
+        jax.ShapeDtypeStruct(residual.shape, F32), [residual, even, odd],
     )
 
 
@@ -197,55 +218,67 @@
     middle = (z == 1) | (z == 2)
     place = jnp.stack([r, z, y]).astype(jnp.int32)
 
+    a_even, g = split_rows(place, integrals.reshape(irreps, row_blocks * block * k_blocks, block))
+    amp_ladder = after(amp_ladder, g)
     tables = lambda p: [[[4 * t + 2 * w + b for b in range(2)] for t in range(4)] for w in (p[2], 1 - p[2])]
     b_own, b_other = pick_columns(place, amp_ladder, 0, tables)
-    a_even, g = split_rows(place, integrals.reshape(irreps, row_blocks * block * k_blocks, block))
     tables = lambda p: [[[4 * (p[1] ^ d) + 2 * w + b for b in range(2)] for w in range(2)] for d in range(4)]
     pieces = pick_columns(place, amp_ladder, 1, tables)
 
     hold = lax.optimization_barrier
-    core = lambda a, b: [a, b, row(a, SWAP_CORE), row(b, SWAP_CORE)]
 
     g1 = col(g, XOR_Z[1])
-    g3_mid = col(g, MIDDLE)
     b_in = col(b_other, SWAP_Y)
     x_own = row(b_own, SWAP_X)
-
-    b_in, *pieces = hold((b_in, *pieces))
-    got = [col(pieces[d], XOR_Z[d]) for d in (1, 2, 3)]
+    g3_mid = col(after(g, b_other), MIDDLE)
+    pieces, g1, g3_mid, x_own, b_in, b_own = hold((pieces, g1, g3_mid, x_own, b_in, b_own))
+
+    x_in = row(b_in, SWAP_X)
     a_in = col(after(a_even, b_in), SWAP_Y)
-    x_in = row(b_in, SWAP_X)
-
-    g1, g3_mid, x_own, x_in = hold((g1, g3_mid, x_own, x_in))
+    swapped = [row(b, SWAP_CORE) for b in (b_own, x_own, b_in)]
+    pieces, swapped = hold((pieces, swapped))
+    got = [col(pieces[d], XOR_Z[d]) for d in (3, 2, 1)]
+    x_in, got = hold((x_in, got))
+
+    swapped.append(row(x_in, SWAP_CORE))
+    a_in, got, swapped = hold((a_in, got, swapped))
+    b_rows = [[b_own, x_own, swapped[0], swapped[1]], [b_in, x_in, swapped[2], swapped[3]]]
+
+    (p3,) = parts(place, [a_even, a_in], b_rows, [3])
+    wire3 = (p3 * WIRE).astype(F16)
+
+    wire3, g1, g3_mid, got = hold((wire3, g1, g3_mid, got))
+    got = jnp.stack([pieces[0], got[2], got[1], got[0]])
+    i3 = col(wire3, INWARD)
+    g2_end = col(g3_mid, OUTWARD)
     g2_mid = col(g1, MIDDLE)
-    g2_end = col(g3_mid, OUTWARD)
-    b_rows = [core(b_own, x_own), core(b_in, x_in)]
-    a_in, got, b_rows = hold((a_in, got, b_rows))
-
-    (p3,) = parts(place, [a_even, a_in], b_rows, [3])
-    i3 = col(p3.astype(F16), INWARD)
-    near = jnp.stack([pieces[0], got[0]])
-    near = core(near, row(after(near, p3), SWAP_X))
-    p2, p1, p0 = parts(place, [after(a_even, p3), a_in], b_rows, [2, 1, 0])
-
-    i3, g2_mid, g2_end, p2, near = hold((i3, g2_mid, g2_end, p2, near))
-    i2 = col(p2.astype(F16), INWARD)
-    m2 = col((p2 + i3.astype(F32)).astype(F16), MIDDLE)
+    got_x = row(got, SWAP_X)
+    p2, p1, p0 = parts(place, [after(a_even, wire3), a_in], b_rows, [2, 1, 0])
+    wire2 = (p2 * WIRE).astype(F16)
+    i2 = col(wire2, INWARD)
+    turn2 = ((p2 + from_wire(i3)) * WIRE).astype(F16)
+    turn2, p1, g2_mid, got_x, g2_end = hold((turn2, p1, g2_mid, got_x, g2_end))
+
+
+    m2 = col(turn2, MIDDLE)
     g3_end = col(g2_mid, OUTWARD)
-    far = jnp.stack([got[1], got[2]])
-    far = core(far, row(after(far, near[0]), SWAP_X))
-
-    i2, m2, g3_end, far, p3 = hold((i2, m2, g3_end, far, p3))
-    s1 = col((p1 + m2.astype(F32)).astype(F16), XOR_Z[1])
-    m3 = col((p3 + i2.astype(F32)).astype(F16), MIDDLE)
+    got_rows = [got, got_x, row(got, SWAP_CORE), row(got_x, SWAP_CORE)]
+
     lefts = [g, g1, jnp.where(middle, g2_mid, g2_end), jnp.where(middle, g3_mid, g3_end)]
-    q = col(column(place, lefts, [near, far], 1).astype(F16), SWAP_Y)
-    even = (p0 + s1.astype(F32)) + m3.astype(F32)
-    odd = column(place, lefts, [near, far], 0) + q.astype(F32)
+    terms = [(left, got_rows, n) for n, left in enumerate(lefts)]
+    other = (column(place, terms, 1, 0) * WIRE).astype(F16)
+    turn3 = ((p3 + from_wire(i2)) * WIRE).astype(F16)
+    turn3, m2, other = hold((turn3, m2, other))
+
+    q = col(other, SWAP_Y)
+    s1 = to_wire(p1 + from_wire(m2), XOR_Z[1])
+    m3 = col(turn3, MIDDLE)
+    odd = column(place, terms, 0, 0) + from_wire(q)
+    even, m3, odd = hold((p0 + from_wire(s1), m3, odd))
+    even = even + from_wire(m3)
 
     result = residual_in.reshape(irreps, row_blocks * block * 2, block)
-    done = add_half(place, result, odd, 1)
-    done = add_half(place, result, even, 0, done)
+    done = add_all(place, result, even, odd)
     return done.reshape(residual_in.shape)
 
 

time: 140 us -> 137 us (0.979)
  starting transfers between devices: 42.2 us -> 36.6 us
  waiting for transfers between devices: 63.6 us -> 68.3 us
  Pallas kernels: 20.3 us -> 18.1 us
  local copies, waits for them, and re-layouts: 3.75 us -> 5.94 us
    ppermute x16, waiting for transfers between devices: 52.3 us -> 61.8 us  [col(): return lax.ppermute(x, 'col', pairs)]
    ppermute x12 -> x9, waiting for transfers between devices: 11.3 us -> 6.48 us  [row(): return lax.ppermute(x, 'row', pairs)]
    ppermute x16, starting transfers between devices: 35.6 us -> 30.8 us  [col(): return lax.ppermute(x, 'col', pairs)]
    pallas_call x9 -> x8, Pallas kernels: 20.3 us -> 18.1 us  [call(): pl.pallas_call(body, grid_spec=pltpu.PrefetchScalarGridSpec(num_scalar_pr...]
    unnamed x38 -> x32, local copies, waits for them, and re-layouts: 3.75 us -> 5.94 us
    ppermute x12 -> x9, starting transfers between devices: 6.64 us -> 5.78 us  [row(): return lax.ppermute(x, 'row', pairs)]
  transfers between devices with their start and end apart: 28 -> 25, of which waited for: 14 -> 14; matrix products, arithmetic and copies ran while one was open for 4% -> 5% of each run, Pallas kernels for 8% -> 9%
where the time goes in v3:
time: 137 us; the launch traced here: 136 us
  waiting for transfers between devices  68.3 us (50%)
  starting transfers between devices  36.6 us (27%)
  Pallas kernels  18.1 us (13%)
  other arithmetic  6.96 us (5%)
  local copies, waits for them, and re-layouts  5.94 us (4%)
    ppermute x16, waiting for transfers between devices, col(): return lax.ppermute(x, 'col', pairs)  61.8 us
    ppermute x16, starting transfers between devices, col(): return lax.ppermute(x, 'col', pairs)  30.8 us
    pallas_call x8, Pallas kernels, call(): pl.pallas_call(body, grid_spec=pltpu.PrefetchScalarGridSpec(num_scalar_pr...  18.1 us
    ppermute x9, waiting for transfers between devices, row(): return lax.ppermute(x, 'row', pairs)  6.48 us
    unnamed x32, local copies, waits for them, and re-layouts  5.94 us
    ppermute x9, starting transfers between devices, row(): return lax.ppermute(x, 'row', pairs)  5.78 us
  transfers between devices with their start and end apart: 25, of which 14 were waited for; matrix products, arithmetic and copies ran while one was open for 5% of the time, Pallas kernels for 9%

profile of v3, /device:TPU:0, one launch (start us, length us, event | category | flops | bytes accessed | tf_op | source)
XLA Modules:
  0.0 136.2 jit_solution(9586237888875163720)
XLA Ops:
  0.1 1.4 %copy-done.8 = bf16[8,3,128,2,128]{4,3,2,1,0:T(2,128)(2,1)S(1)} copy-done((bf16[8,3,128,2,128]{4,3,2,1,0:T(2,128)(2,1)S(1)}, bf16[8,3,128,2,128]{4,3,2,1,0:T(2,128)(2,1)}, u32[]{:S(2)}) %copy-start.8) | copy-done | bytes 1572888
  1.5 1.1 shard_map.37
  2.6 3.1 %collective-permute-start = (bf16[4,384,256]{2,1,0:T(8,128)(2,1)S(1)}, bf16[4,384,256]{2,1,0:T(8,128)(2,1)S(1)}, u32[]{:S(2)}, u32[]{:S(2)}) collective-permute-start(bf16[4,384,256]{2,1,0:T(8,128)(2,1)S(1)} %get-tuple-element.73.refs_0_), channel_id=1, source_target_pairs={{0,2},{1,3},{2,0},{3,1},{4,6},{5,7},{6,4},{7,5},{8,10},{9,11},{10,... | collective-permute-start | bytes 2359304 | tf_op jit(solution)/shard_map/ppermute | solution.py:41
  5.7 1.6 %copy-done.2 = bf16[2,2,128,16,128]{4,3,2,1,0:T(8,128)(2,1)S(1)} copy-done((bf16[2,2,128,16,128]{4,3,2,1,0:T(8,128)(2,1)S(1)}, bf16[2,2,128,16,128]{4,3,2,1,0:T(8,128)(2,1)}, u32[]{:S(2)}) %copy-start.2) | copy-done | bytes 2097176
  7.3 1.5 %shard_map.39 = (bf16[4,256,256]{2,1,0:T(8,128)(2,1)S(1)}, bf16[4,256,256]{2,1,0:T(8,128)(2,1)S(1)}) custom-call(s32[3]{0:T(128)S(1)} %pad_add_fusion._.place_ref, bf16[2,2,128,16,128]{4,3,2,1,0:T(8,128)(2,1)S(1)} %copy-done.2), custom_call_target="tpu_custom_call" | custom-call | tf_op jit(solution)/shard_map/pallas_call | solution.py:61
  8.8 0.7 collective-permute-start.1
  9.5 1.6 %collective-permute-start.3 = (bf16[4,256,256]{2,1,0:T(8,128)(2,1)S(1)}, bf16[4,256,256]{2,1,0:T(8,128)(2,1)S(1)}, u32[]{:S(2)}, u32[]{:S(2)}) collective-permute-start(bf16[4,256,256]{2,1,0:T(8,128)(2,1)S(1)} %get-tuple-element.72), channel_id=1, source_target_pairs={{0,1},{1,0},{2,3},{3,2},{4,5},{5,4},{6,7},{7,6},{8,9},{9,8},{10,11... | collective-permute-start | bytes 1572872 | tf_op jit(solution)/shard_map/ppermute | solution.py:41
  11.1 1.5 %collective-permute-start.2 = (bf16[4,256,256]{2,1,0:T(8,128)(2,1)S(1)}, bf16[4,256,256]{2,1,0:T(8,128)(2,1)S(1)}, u32[]{:S(2)}, u32[]{:S(2)}) collective-permute-start(bf16[4,256,256]{2,1,0:T(8,128)(2,1)S(1)} %get-tuple-element.81.refs_2_.refs_10_.refs_18_), channel_id=1, source_target_pairs={{0,16},{8,24},{16,0},{24,8},{1,17},{9,25},{17,1},{25,9},{2,18},{10... | collective-permute-start | bytes 1572872 | tf_op jit(solution)/shard_map/ppermute | solution.py:45
  12.6 1.5 %shard_map.38 = (bf16[2,256,256]{2,1,0:T(8,128)(2,1)S(1)}, bf16[2,256,256]{2,1,0:T(8,128)(2,1)S(1)}, bf16[2,256,256]{2,1,0:T(8,128)(2,1)S(1)}, bf16[2,256,256]{2,1,0:T(8,128)(2,1)S(1)}) custom-call(s32[3]{0:T(128)S(1)} %pad_add_fusion._.place_ref, bf16[2,2,128,16,128]{4,3,2,1,0:T(8,128)(2,1)S(1)} %copy-done.2), custom_call_target="tpu_custom_call" | custom-call | tf_op jit(solution)/shard_map/pallas_call | solution.py:61
  14.1 8.8 %collective-permute-done.3.refs_6_.refs_14_.refs_22_ = bf16[4,256,256]{2,1,0:T(8,128)(2,1)S(1)} collective-permute-done((bf16[4,256,256]{2,1,0:T(8,128)(2,1)S(1)}, bf16[4,256,256]{2,1,0:T(8,128)(2,1)S(1)}, u32[]{:S(2)}, u32[]{:S(2)}) %collective-permute-start.3) | collective-permute-done | bytes 524320 | tf_op jit(solution)/shard_map/ppermute | solution.py:41
  23.0 1.2 collective-permute-done.2.refs_3_.refs_11_.refs_19_
  24.9 1.5 %collective-permute-start.5 = (bf16[4,256,256]{2,1,0:T(8,128)(2,1)S(1)}, bf16[4,256,256]{2,1,0:T(8,128)(2,1)S(1)}, u32[]{:S(2)}, u32[]{:S(2)}) collective-permute-start(bf16[4,256,256]{2,1,0:T(8,128)(2,1)S(1)} %collective-permute-done.3.refs_6_.refs_14_.refs_22_), channel_id=1, source_target_pairs={{0,16},{8,24},{16,0},{24,8},{1,17},{9,25},{17,1},{25,9},{2,18},{10... | collective-permute-start | bytes 1572872 | tf_op jit(solution)/shard_map/ppermute | solution.py:45
  26.4 0.6 collective-permute-done.7.refs_5_.refs_13_.refs_21_
  27.0 0.7 collective-permute-done.8.refs_8_.refs_16_.refs_24_
  27.7 2.7 %collective-permute-start.9 = (bf16[2,256,256]{2,1,0:T(8,128)(2,1)S(1)}, bf16[2,256,256]{2,1,0:T(8,128)(2,1)S(1)}, u32[]{:S(2)}, u32[]{:S(2)}) collective-permute-start(bf16[2,256,256]{2,1,0:T(8,128)(2,1)S(1)} %get-tuple-element.83), channel_id=1, source_target_pairs={{0,6},{1,7},{2,4},{3,5},{4,2},{5,3},{6,0},{7,1},{8,14},{9,15},{10,... | collective-permute-start | bytes 786440 | tf_op jit(solution)/shard_map/ppermute | solution.py:41
  30.5 5.5 %collective-permute-start.10 = (bf16[2,256,256]{2,1,0:T(8,128)(2,1)S(1)}, bf16[2,256,256]{2,1,0:T(8,128)(2,1)S(1)}, u32[]{:S(2)}, u32[]{:S(2)}) collective-permute-start(bf16[2,256,256]{2,1,0:T(8,128)(2,1)S(1)} %get-tuple-element.84), channel_id=1, source_target_pairs={{0,4},{1,5},{2,6},{3,7},{4,0},{5,1},{6,2},{7,3},{8,12},{9,13},{10,... | collective-permute-start | bytes 786440 | tf_op jit(solution)/shard_map/ppermute | solution.py:41
  36.3 1.5 %collective-permute-start.4 = (bf16[4,384,256]{2,1,0:T(8,128)(2,1)S(1)}, bf16[4,384,256]{2,1,0:T(8,128)(2,1)S(1)}, u32[]{:S(2)}, u32[]{:S(2)}) collective-permute-start(bf16[4,384,256]{2,1,0:T(8,128)(2,1)S(1)} %get-tuple-element.104.refs_0_), channel_id=1, source_target_pairs={{0,1},{1,0},{2,3},{3,2},{4,5},{5,4},{6,7},{7,6},{8,9},{9,8},{10,11... | collective-permute-start | bytes 2359304 | tf_op jit(solution)/shard_map/ppermute | solution.py:41
  37.8 1.4 %collective-permute-done.5.refs_7_.refs_15_.refs_23_ = bf16[4,256,256]{2,1,0:T(8,128)(2,1)S(1)} collective-permute-done((bf16[4,256,256]{2,1,0:T(8,128)(2,1)S(1)}, bf16[4,256,256]{2,1,0:T(8,128)(2,1)S(1)}, u32[]{:S(2)}, u32[]{:S(2)}) %collective-permute-start.5) | collective-permute-done | bytes 524320 | tf_op jit(solution)/shard_map/ppermute | solution.py:45
  39.2 15.5 %collective-permute-done.10 = bf16[2,256,256]{2,1,0:T(8,128)(2,1)S(1)} collective-permute-done((bf16[2,256,256]{2,1,0:T(8,128)(2,1)S(1)}, bf16[2,256,256]{2,1,0:T(8,128)(2,1)S(1)}, u32[]{:S(2)}, u32[]{:S(2)}) %collective-permute-start.10) | collective-permute-done | bytes 262176 | tf_op jit(solution)/shard_map/ppermute | solution.py:41
  54.7 0.5 collective-permute-done.4.refs_1_
  55.3 1.3 collective-permute-done.12.refs_9_.refs_17_.refs_25_
  56.6 1.7 %shard_map.40 = f32[4,384,256]{2,1,0:T(8,128)S(1)} custom-call(s32[3]{0:T(128)S(1)} %pad_add_fusion._.place_ref, bf16[4,384,256]{2,1,0:T(8,128)(2,1)S(1)} %get-tuple-element.104.refs_0_, bf16[4,384,256]{2,1,0:T(8,128)(2,1)S(1)} %collective-permute-done.4.refs_1_, bf16[4,256,256]{2,1,0:T(8,128)(2,1)S(1)} %get-tuple-element.81.refs_2_.refs_10_.refs_18_, ...), custom_call_target="tpu_custom_call" | custom-call | tf_op jit(solution)/shard_map/pallas_call | solution.py:61
  58.6 2.1 %collective-permute-start.13 = (f16[4,384,256]{2,1,0:T(8,128)(2,1)S(1)}, f16[4,384,256]{2,1,0:T(8,128)(2,1)S(1)}, u32[]{:S(2)}, u32[]{:S(2)}) collective-permute-start(f16[4,384,256]{2,1,0:T(8,128)(2,1)S(1)} %multiply_convert_fusion.5), channel_id=1, source_target_pairs={{0,2},{1,3},{6,4},{7,5},{8,10},{9,11},{14,12},{15,13},{16,18},{17,... | collective-permute-start | bytes 2359304 | tf_op jit(solution)/shard_map/ppermute | solution.py:41
  60.8 1.6 %collective-permute-start.15 = (bf16[4,2,256,256]{3,2,1,0:T(8,128)(2,1)S(1)}, bf16[4,2,256,256]{3,2,1,0:T(8,128)(2,1)S(1)}, u32[]{:S(2)}, u32[]{:S(2)}) collective-permute-start(bf16[4,2,256,256]{3,2,1,0:T(8,128)(2,1)S(1)} %pad_maximum_fusion.refs_4_.refs_8_.refs_12_.refs_16_), channel_id=1, source_target_pairs={{0,16},{8,24},{16,0},{24,8},{1,17},{9,25},{17,1},{25,9},{2,18},{10... | collective-permute-start | bytes 3145736 | tf_op jit(solution)/shard_map/ppermute | solution.py:45
  62.4 1.3 collective-permute-start.16
  63.7 1.7 %collective-permute-start.14 = (bf16[4,384,256]{2,1,0:T(8,128)(2,1)S(1)}, bf16[4,384,256]{2,1,0:T(8,128)(2,1)}, u32[]{:S(2)}, u32[]{:S(2)}) collective-permute-start(bf16[4,384,256]{2,1,0:T(8,128)(2,1)S(1)} %collective-permute-done.refs_1_), channel_id=1, source_target_pairs={{2,4},{3,5},{4,2},{5,3},{10,12},{11,13},{12,10},{13,11},{18,20},{1... | collective-permute-start | bytes 2359304 | tf_op jit(solution)/shard_map/ppermute | solution.py:41
  65.3 2.7 %shard_map.41 = (f32[4,384,256]{2,1,0:T(8,128)S(1)}, f32[4,384,256]{2,1,0:T(8,128)S(1)}, f32[4,384,256]{2,1,0:T(8,128)S(1)}) custom-call(s32[3]{0:T(128)S(1)} %pad_add_fusion._.place_ref, bf16[4,384,256]{2,1,0:T(8,128)(2,1)S(1)} %get-tuple-element.104.refs_0_, bf16[4,384,256]{2,1,0:T(8,128)(2,1)S(1)} %collective-permute-done.4.refs_1_, ...), custom_call_target="tpu_custom_call" | custom-call | tf_op jit(solution)/shard_map/pallas_call | solution.py:61
  68.0 9.4 %collective-permute-done.13 = f16[4,384,256]{2,1,0:T(8,128)(2,1)S(1)} collective-permute-done((f16[4,384,256]{2,1,0:T(8,128)(2,1)S(1)}, f16[4,384,256]{2,1,0:T(8,128)(2,1)S(1)}, u32[]{:S(2)}, u32[]{:S(2)}) %collective-permute-start.13) | collective-permute-done | bytes 786464 | tf_op jit(solution)/shard_map/ppermute | solution.py:41
  77.5 1.6 %multiply_convert_fusion.3 = (f16[4,384,256]{2,1,0:T(8,128)(2,1)}, f16[4,384,256]{2,1,0:T(8,128)(2,1)}) fusion(f32[4,384,256]{2,1,0:T(8,128)S(1)} %get-tuple-element.106, f16[4,384,256]{2,1,0:T(8,128)(2,1)S(1)} %collective-permute-done.13), kind=kLoop, calls=%fused_computation.6 | loop fusion | flops 2752512 | bytes 3932160 | tf_op jit(solution)/shard_map/convert_element_type | solution.py:257
  79.1 5.3 %collective-permute-start.17 = (f16[4,384,256]{2,1,0:T(8,128)(2,1)}, f16[4,384,256]{2,1,0:T(8,128)(2,1)}, u32[]{:S(2)}, u32[]{:S(2)}) collective-permute-start(f16[4,384,256]{2,1,0:T(8,128)(2,1)} %get-tuple-element.125), channel_id=1, source_target_pairs={{0,2},{1,3},{6,4},{7,5},{8,10},{9,11},{14,12},{15,13},{16,18},{17,... | collective-permute-start | bytes 2359304 | tf_op jit(solution)/shard_map/ppermute | solution.py:41
  84.4 1.2 collective-permute-done.15.refs_5_.refs_9_.refs_13_.refs_17_
  85.6 1.3 collective-permute-start.19
  87.4 0.8 collective-permute-start.18
  88.3 1.2 broadcast_select_fusion.1.refs_2_
  89.5 10.3 %collective-permute-done.17 = f16[4,384,256]{2,1,0:T(8,128)(2,1)} collective-permute-done((f16[4,384,256]{2,1,0:T(8,128)(2,1)}, f16[4,384,256]{2,1,0:T(8,128)(2,1)}, u32[]{:S(2)}, u32[]{:S(2)}) %collective-permute-start.17) | collective-permute-done | bytes 786464 | tf_op jit(solution)/shard_map/ppermute | solution.py:41
  99.9 1.5 %multiply_convert_fusion.2 = f16[4,384,256]{2,1,0:T(8,128)(2,1)S(1)} fusion(f32[4,384,256]{2,1,0:T(8,128)S(1)} %copy-done.1, f16[4,384,256]{2,1,0:T(8,128)(2,1)} %collective-permute-done.17), kind=kLoop, calls=%fused_computation.5 | loop fusion | flops 1966080 | bytes 3145728 | tf_op jit(solution)/shard_map/convert_element_type | solution.py:270
  101.4 4.6 %collective-permute-done.19 = bf16[4,384,256]{2,1,0:T(8,128)(2,1)} collective-permute-done((bf16[4,384,256]{2,1,0:T(8,128)(2,1)}, bf16[4,384,256]{2,1,0:T(8,128)(2,1)}, u32[]{:S(2)}, u32[]{:S(2)}) %collective-permute-start.19) | collective-permute-done | bytes 786464 | tf_op jit(solution)/shard_map/ppermute | solution.py:41
  106.0 1.2 broadcast_select_fusion.refs_3_
  107.2 3.4 %shard_map.42 = f32[4,384,256]{2,1,0:T(8,128)S(1)} custom-call(s32[3]{0:T(128)S(1)} %pad_add_fusion._.place_ref, bf16[4,384,256]{2,1,0:T(8,128)(2,1)S(1)} %copy-done.4, bf16[4,384,256]{2,1,0:T(8,128)(2,1)S(1)} %copy-done.6, bf16[4,384,256]{2,1,0:T(8,128)(2,1)S(1)} %broadcast_select_fusion.1.refs_2_, bf16[4,384,256]{2,1,0:T(8,128)(2,1)S(1)} %broadcast_select_fusion.refs_3_, ...), custom_call_target="tpu_custom_call" | custom-call | tf_op jit(solution)/shard_map/pallas_call | solution.py:61
  110.8 1.2 copy-done.10
  112.3 0.7 collective-permute-start.22
  113.1 1.5 %collective-permute-start.24 = (f16[4,384,256]{2,1,0:T(8,128)(2,1)S(1)}, f16[4,384,256]{2,1,0:T(8,128)(2,1)S(1)}, u32[]{:S(2)}, u32[]{:S(2)}) collective-permute-start(f16[4,384,256]{2,1,0:T(8,128)(2,1)S(1)} %multiply_convert_fusion.1), channel_id=1, source_target_pairs={{0,1},{1,0},{2,3},{3,2},{4,5},{5,4},{6,7},{7,6},{8,9},{9,8},{10,11... | collective-permute-start | bytes 2359304 | tf_op jit(solution)/shard_map/ppermute | solution.py:41
  114.6 0.7 collective-permute-start.23
  115.3 3.4 %shard_map.43 = f32[4,384,256]{2,1,0:T(8,128)S(1)} custom-call(s32[3]{0:T(128)S(1)} %pad_add_fusion._.place_ref, bf16[4,384,256]{2,1,0:T(8,128)(2,1)S(1)} %copy-done.4, bf16[4,384,256]{2,1,0:T(8,128)(2,1)S(1)} %copy-done.6, bf16[4,384,256]{2,1,0:T(8,128)(2,1)S(1)} %broadcast_select_fusion.1.refs_2_, bf16[4,384,256]{2,1,0:T(8,128)(2,1)S(1)} %broadcast_select_fusion.refs_3_, ...), custom_call_target="tpu_custom_call" | custom-call | tf_op jit(solution)/shard_map/pallas_call | solution.py:61
  118.7 11.3 %collective-permute-done.22 = f16[4,384,256]{2,1,0:T(8,128)(2,1)S(1)} collective-permute-done((f16[4,384,256]{2,1,0:T(8,128)(2,1)S(1)}, f16[4,384,256]{2,1,0:T(8,128)(2,1)S(1)}, u32[]{:S(2)}, u32[]{:S(2)}) %collective-permute-start.22) | collective-permute-done | bytes 786464 | tf_op jit(solution)/shard_map/ppermute | solution.py:41
  130.1 1.3 collective-permute-done.24
  131.8 1.7 %copy-done.7 = f32[8,3,128,2,128]{4,3,2,1,0:T(2,128)S(1)} copy-done((f32[8,3,128,2,128]{4,3,2,1,0:T(2,128)S(1)}, f32[8,3,128,2,128]{4,3,2,1,0:T(2,128)}, u32[]{:S(2)}) %copy-start.7) | copy-done | bytes 3145752
  133.5 2.8 %shard_map.44 = f32[8,768,128]{2,1,0:T(8,128)} custom-call(s32[3]{0:T(128)S(1)} %pad_add_fusion._.place_ref, f32[8,768,128]{2,1,0:T(8,128)S(1)} %bitcast.10, f32[4,384,256]{2,1,0:T(8,128)S(1)} %multiply_add_fusion.even_ref, f32[4,384,256]{2,1,0:T(8,128)S(1)} %multiply_add_fusion.1.odd_ref), custom_call_target="tpu_custom_call" | custom-call | tf_op jit(solution)/shard_map/pallas_call | solution.py:61
  (54 shorter events, 3.0 us)
Async XLA Ops:
  0.1 1.4 %copy-start.8 = (bf16[8,3,128,2,128]{4,3,2,1,0:T(2,128)(2,1)S(1)}, bf16[8,3,128,2,128]{4,3,2,1,0:T(2,128)(2,1)}, u32[]{:S(2)}) copy-start(bf16[8,3,128,2,128]{4,3,2,1,0:T(2,128)(2,1)} %param.4) | copy-start | bytes 4718596
  2.6 11.6 %copy-start.3 = (bf16[4,384,256]{2,1,0:T(8,128)(2,1)}, bf16[4,384,256]{2,1,0:T(8,128)(2,1)S(1)}, u32[]{:S(2)}) copy-start(bf16[4,384,256]{2,1,0:T(8,128)(2,1)S(1)} %get-tuple-element.73.refs_0_) | copy-start | bytes 2359300
  2.6 21.6 %collective-permute-start = (bf16[4,384,256]{2,1,0:T(8,128)(2,1)S(1)}, bf16[4,384,256]{2,1,0:T(8,128)(2,1)S(1)}, u32[]{:S(2)}, u32[]{:S(2)}) collective-permute-start(bf16[4,384,256]{2,1,0:T(8,128)(2,1)S(1)} %get-tuple-element.73.refs_0_), channel_id=1, source_target_pairs={{0,2},{1,3},{2,0},{3,1},{4,6},{5,7},{6,4},{7,5},{8,10},{9,11},{10,... | collective-permute-start | bytes 2359304 | tf_op jit(solution)/shard_map/ppermute | solution.py:41
  5.7 1.6 %copy-start.2 = (bf16[2,2,128,16,128]{4,3,2,1,0:T(8,128)(2,1)S(1)}, bf16[2,2,128,16,128]{4,3,2,1,0:T(8,128)(2,1)}, u32[]{:S(2)}) copy-start(bf16[2,2,128,16,128]{4,3,2,1,0:T(8,128)(2,1)} %in_ref.1) | copy-start | bytes 6291460
  8.8 15.4 %collective-permute-start.1 = (bf16[4,384,256]{2,1,0:T(8,128)(2,1)S(1)}, bf16[4,384,256]{2,1,0:T(8,128)(2,1)S(1)}, u32[]{:S(2)}, u32[]{:S(2)}) collective-permute-start(bf16[4,384,256]{2,1,0:T(8,128)(2,1)S(1)} %get-tuple-element.73.refs_0_), channel_id=1, source_target_pairs={{2,4},{3,5},{4,2},{5,3},{10,12},{11,13},{12,10},{13,11},{18,20},{1... | collective-permute-start | bytes 2359304 | tf_op jit(solution)/shard_map/ppermute | solution.py:41
  9.5 13.4 %collective-permute-start.3 = (bf16[4,256,256]{2,1,0:T(8,128)(2,1)S(1)}, bf16[4,256,256]{2,1,0:T(8,128)(2,1)S(1)}, u32[]{:S(2)}, u32[]{:S(2)}) collective-permute-start(bf16[4,256,256]{2,1,0:T(8,128)(2,1)S(1)} %get-tuple-element.72), channel_id=1, source_target_pairs={{0,1},{1,0},{2,3},{3,2},{4,5},{5,4},{6,7},{7,6},{8,9},{9,8},{10,11... | collective-permute-start | bytes 1572872 | tf_op jit(solution)/shard_map/ppermute | solution.py:41
  11.1 13.1 %collective-permute-start.2 = (bf16[4,256,256]{2,1,0:T(8,128)(2,1)S(1)}, bf16[4,256,256]{2,1,0:T(8,128)(2,1)S(1)}, u32[]{:S(2)}, u32[]{:S(2)}) collective-permute-start(bf16[4,256,256]{2,1,0:T(8,128)(2,1)S(1)} %get-tuple-element.81.refs_2_.refs_10_.refs_18_), channel_id=1, source_target_pairs={{0,16},{8,24},{16,0},{24,8},{1,17},{9,25},{17,1},{25,9},{2,18},{10... | collective-permute-start | bytes 1572872 | tf_op jit(solution)/shard_map/ppermute | solution.py:45
  24.2 39.4 %copy-start.5 = (bf16[4,384,256]{2,1,0:T(8,128)(2,1)}, bf16[4,384,256]{2,1,0:T(8,128)(2,1)S(1)}, u32[]{:S(2)}) copy-start(bf16[4,384,256]{2,1,0:T(8,128)(2,1)S(1)} %collective-permute-done.refs_1_) | copy-start | bytes 2359300
  24.2 38.1 %copy-start.13 = (bf16[4,384,256]{2,1,0:T(8,128)(2,1)}, bf16[4,384,256]{2,1,0:T(8,128)(2,1)S(1)}, u32[]{:S(2)}) copy-start(bf16[4,384,256]{2,1,0:T(8,128)(2,1)S(1)} %collective-permute-done.1) | copy-start | bytes 2359300
  24.2 2.1 %collective-permute-start.6 = (bf16[4,256,256]{2,1,0:T(8,128)(2,1)S(1)}, bf16[4,256,256]{2,1,0:T(8,128)(2,1)S(1)}, u32[]{:S(2)}, u32[]{:S(2)}) collective-permute-start(bf16[4,256,256]{2,1,0:T(8,128)(2,1)S(1)} %get-tuple-element.81.refs_2_.refs_10_.refs_18_), channel_id=1, source_target_pairs={{0,8},{8,0},{16,24},{24,16},{1,9},{9,1},{17,25},{25,17},{2,10},{10... | collective-permute-start | bytes 1572872 | tf_op jit(solution)/shard_map/ppermute | solution.py:45
  24.3 2.6 %collective-permute-start.7 = (bf16[4,256,256]{2,1,0:T(8,128)(2,1)S(1)}, bf16[4,256,256]{2,1,0:T(8,128)(2,1)S(1)}, u32[]{:S(2)}, u32[]{:S(2)}) collective-permute-start(bf16[4,256,256]{2,1,0:T(8,128)(2,1)S(1)} %collective-permute-done.2.refs_3_.refs_11_.refs_19_), channel_id=1, source_target_pairs={{0,8},{8,0},{16,24},{24,16},{1,9},{9,1},{17,25},{25,17},{2,10},{10... | collective-permute-start | bytes 1572872 | tf_op jit(solution)/shard_map/ppermute | solution.py:45
  24.8 2.9 %collective-permute-start.8 = (bf16[4,256,256]{2,1,0:T(8,128)(2,1)S(1)}, bf16[4,256,256]{2,1,0:T(8,128)(2,1)S(1)}, u32[]{:S(2)}, u32[]{:S(2)}) collective-permute-start(bf16[4,256,256]{2,1,0:T(8,128)(2,1)S(1)} %collective-permute-done.3.refs_6_.refs_14_.refs_22_), channel_id=1, source_target_pairs={{0,8},{8,0},{16,24},{24,16},{1,9},{9,1},{17,25},{25,17},{2,10},{10... | collective-permute-start | bytes 1572872 | tf_op jit(solution)/shard_map/ppermute | solution.py:45
  24.9 14.3 %collective-permute-start.5 = (bf16[4,256,256]{2,1,0:T(8,128)(2,1)S(1)}, bf16[4,256,256]{2,1,0:T(8,128)(2,1)S(1)}, u32[]{:S(2)}, u32[]{:S(2)}) collective-permute-start(bf16[4,256,256]{2,1,0:T(8,128)(2,1)S(1)} %collective-permute-done.3.refs_6_.refs_14_.refs_22_), channel_id=1, source_target_pairs={{0,16},{8,24},{16,0},{24,8},{1,17},{9,25},{17,1},{25,9},{2,18},{10... | collective-permute-start | bytes 1572872 | tf_op jit(solution)/shard_map/ppermute | solution.py:45
  27.7 11.5 %collective-permute-start.9 = (bf16[2,256,256]{2,1,0:T(8,128)(2,1)S(1)}, bf16[2,256,256]{2,1,0:T(8,128)(2,1)S(1)}, u32[]{:S(2)}, u32[]{:S(2)}) collective-permute-start(bf16[2,256,256]{2,1,0:T(8,128)(2,1)S(1)} %get-tuple-element.83), channel_id=1, source_target_pairs={{0,6},{1,7},{2,4},{3,5},{4,2},{5,3},{6,0},{7,1},{8,14},{9,15},{10,... | collective-permute-start | bytes 786440 | tf_op jit(solution)/shard_map/ppermute | solution.py:41
  30.5 24.3 %collective-permute-start.10 = (bf16[2,256,256]{2,1,0:T(8,128)(2,1)S(1)}, bf16[2,256,256]{2,1,0:T(8,128)(2,1)S(1)}, u32[]{:S(2)}, u32[]{:S(2)}) collective-permute-start(bf16[2,256,256]{2,1,0:T(8,128)(2,1)S(1)} %get-tuple-element.84), channel_id=1, source_target_pairs={{0,4},{1,5},{2,6},{3,7},{4,0},{5,1},{6,2},{7,3},{8,12},{9,13},{10,... | collective-permute-start | bytes 786440 | tf_op jit(solution)/shard_map/ppermute | solution.py:41
  36.0 18.7 %collective-permute-start.11 = (bf16[2,256,256]{2,1,0:T(8,128)(2,1)S(1)}, bf16[2,256,256]{2,1,0:T(8,128)(2,1)S(1)}, u32[]{:S(2)}, u32[]{:S(2)}) collective-permute-start(bf16[2,256,256]{2,1,0:T(8,128)(2,1)S(1)} %get-tuple-element.85), channel_id=1, source_target_pairs={{0,2},{1,3},{2,0},{3,1},{4,6},{5,7},{6,4},{7,5},{8,10},{9,11},{10,... | collective-permute-start | bytes 786440 | tf_op jit(solution)/shard_map/ppermute | solution.py:41
  36.3 19.0 %collective-permute-start.4 = (bf16[4,384,256]{2,1,0:T(8,128)(2,1)S(1)}, bf16[4,384,256]{2,1,0:T(8,128)(2,1)S(1)}, u32[]{:S(2)}, u32[]{:S(2)}) collective-permute-start(bf16[4,384,256]{2,1,0:T(8,128)(2,1)S(1)} %get-tuple-element.104.refs_0_), channel_id=1, source_target_pairs={{0,1},{1,0},{2,3},{3,2},{4,5},{5,4},{6,7},{7,6},{8,9},{9,8},{10,11... | collective-permute-start | bytes 2359304 | tf_op jit(solution)/shard_map/ppermute | solution.py:41
  54.7 1.9 %collective-permute-start.12 = (bf16[4,256,256]{2,1,0:T(8,128)(2,1)S(1)}, bf16[4,256,256]{2,1,0:T(8,128)(2,1)S(1)}, u32[]{:S(2)}, u32[]{:S(2)}) collective-permute-start(bf16[4,256,256]{2,1,0:T(8,128)(2,1)S(1)} %collective-permute-done.5.refs_7_.refs_15_.refs_23_), channel_id=1, source_target_pairs={{0,8},{8,0},{16,24},{24,16},{1,9},{9,1},{17,25},{25,17},{2,10},{10... | collective-permute-start | bytes 1572872 | tf_op jit(solution)/shard_map/ppermute | solution.py:45
  58.4 2.4 %copy-start = (f32[4,384,256]{2,1,0:T(8,128)}, f32[4,384,256]{2,1,0:T(8,128)S(1)}, u32[]{:S(2)}) copy-start(f32[4,384,256]{2,1,0:T(8,128)S(1)} %shard_map.40) | copy-start | bytes 4718596
  58.6 18.9 %collective-permute-start.13 = (f16[4,384,256]{2,1,0:T(8,128)(2,1)S(1)}, f16[4,384,256]{2,1,0:T(8,128)(2,1)S(1)}, u32[]{:S(2)}, u32[]{:S(2)}) collective-permute-start(f16[4,384,256]{2,1,0:T(8,128)(2,1)S(1)} %multiply_convert_fusion.5), channel_id=1, source_target_pairs={{0,2},{1,3},{6,4},{7,5},{8,10},{9,11},{14,12},{15,13},{16,18},{17,... | collective-permute-start | bytes 2359304 | tf_op jit(solution)/shard_map/ppermute | solution.py:41
  60.8 24.8 %collective-permute-start.15 = (bf16[4,2,256,256]{3,2,1,0:T(8,128)(2,1)S(1)}, bf16[4,2,256,256]{3,2,1,0:T(8,128)(2,1)S(1)}, u32[]{:S(2)}, u32[]{:S(2)}) collective-permute-start(bf16[4,2,256,256]{3,2,1,0:T(8,128)(2,1)S(1)} %pad_maximum_fusion.refs_4_.refs_8_.refs_12_.refs_16_), channel_id=1, source_target_pairs={{0,16},{8,24},{16,0},{24,8},{1,17},{9,25},{17,1},{25,9},{2,18},{10... | collective-permute-start | bytes 3145736 | tf_op jit(solution)/shard_map/ppermute | solution.py:45
  62.4 22.0 %collective-permute-start.16 = (bf16[4,384,256]{2,1,0:T(8,128)(2,1)S(1)}, bf16[4,384,256]{2,1,0:T(8,128)(2,1)S(1)}, u32[]{:S(2)}, u32[]{:S(2)}) collective-permute-start(bf16[4,384,256]{2,1,0:T(8,128)(2,1)S(1)} %collective-permute-done.1), channel_id=1, source_target_pairs={{2,0},{3,1},{4,6},{5,7},{10,8},{11,9},{12,14},{13,15},{18,16},{19,... | collective-permute-start | bytes 2359304 | tf_op jit(solution)/shard_map/ppermute | solution.py:41
  63.7 20.7 %collective-permute-start.14 = (bf16[4,384,256]{2,1,0:T(8,128)(2,1)S(1)}, bf16[4,384,256]{2,1,0:T(8,128)(2,1)}, u32[]{:S(2)}, u32[]{:S(2)}) collective-permute-start(bf16[4,384,256]{2,1,0:T(8,128)(2,1)S(1)} %collective-permute-done.refs_1_), channel_id=1, source_target_pairs={{2,4},{3,5},{4,2},{5,3},{10,12},{11,13},{12,10},{13,11},{18,20},{1... | collective-permute-start | bytes 2359304 | tf_op jit(solution)/shard_map/ppermute | solution.py:41
  68.0 11.1 %copy-start.9 = (f32[4,384,256]{2,1,0:T(8,128)}, f32[4,384,256]{2,1,0:T(8,128)S(1)}, u32[]{:S(2)}) copy-start(f32[4,384,256]{2,1,0:T(8,128)S(1)} %get-tuple-element.114) | copy-start | bytes 4718596
  68.0 11.0 %copy-start.11 = (f32[4,384,256]{2,1,0:T(8,128)}, f32[4,384,256]{2,1,0:T(8,128)S(1)}, u32[]{:S(2)}) copy-start(f32[4,384,256]{2,1,0:T(8,128)S(1)} %get-tuple-element.105) | copy-start | bytes 4718596
  79.1 20.8 %collective-permute-start.17 = (f16[4,384,256]{2,1,0:T(8,128)(2,1)}, f16[4,384,256]{2,1,0:T(8,128)(2,1)}, u32[]{:S(2)}, u32[]{:S(2)}) collective-permute-start(f16[4,384,256]{2,1,0:T(8,128)(2,1)} %get-tuple-element.125), channel_id=1, source_target_pairs={{0,2},{1,3},{6,4},{7,5},{8,10},{9,11},{14,12},{15,13},{16,18},{17,... | collective-permute-start | bytes 2359304 | tf_op jit(solution)/shard_map/ppermute | solution.py:41
  84.4 2.5 %copy-start.15 = (bf16[4,384,256]{2,1,0:T(8,128)(2,1)}, bf16[4,384,256]{2,1,0:T(8,128)(2,1)S(1)}, u32[]{:S(2)}) copy-start(bf16[4,384,256]{2,1,0:T(8,128)(2,1)S(1)} %collective-permute-done.16) | copy-start | bytes 2359300
  85.6 20.4 %collective-permute-start.19 = (bf16[4,384,256]{2,1,0:T(8,128)(2,1)}, bf16[4,384,256]{2,1,0:T(8,128)(2,1)}, u32[]{:S(2)}, u32[]{:S(2)}) collective-permute-start(bf16[4,384,256]{2,1,0:T(8,128)(2,1)} %collective-permute-done.14), channel_id=1, source_target_pairs={{2,0},{3,1},{4,6},{5,7},{10,8},{11,9},{12,14},{13,15},{18,16},{19,... | collective-permute-start | bytes 2359304 | tf_op jit(solution)/shard_map/ppermute | solution.py:41
  86.9 20.3 %collective-permute-start.20 = (bf16[4,2,256,256]{3,2,1,0:T(8,128)(2,1)S(1)}, bf16[4,2,256,256]{3,2,1,0:T(8,128)(2,1)S(1)}, u32[]{:S(2)}, u32[]{:S(2)}) collective-permute-start(bf16[4,2,256,256]{3,2,1,0:T(8,128)(2,1)S(1)} %pad_maximum_fusion.refs_4_.refs_8_.refs_12_.refs_16_), channel_id=1, source_target_pairs={{0,8},{8,0},{16,24},{24,16},{1,9},{9,1},{17,25},{25,17},{2,10},{10... | collective-permute-start | bytes 3145736 | tf_op jit(solution)/shard_map/ppermute | solution.py:45
  86.9 20.2 %collective-permute-start.21 = (bf16[4,2,256,256]{3,2,1,0:T(8,128)(2,1)S(1)}, bf16[4,2,256,256]{3,2,1,0:T(8,128)(2,1)}, u32[]{:S(2)}, u32[]{:S(2)}) collective-permute-start(bf16[4,2,256,256]{3,2,1,0:T(8,128)(2,1)S(1)} %collective-permute-done.15.refs_5_.refs_9_.refs_13_.refs_17_), channel_id=1, source_target_pairs={{0,8},{8,0},{16,24},{24,16},{1,9},{9,1},{17,25},{25,17},{2,10},{10... | collective-permute-start | bytes 3145736 | tf_op jit(solution)/shard_map/ppermute | solution.py:45
  87.4 12.4 %copy-start.1 = (f32[4,384,256]{2,1,0:T(8,128)S(1)}, f32[4,384,256]{2,1,0:T(8,128)}, u32[]{:S(2)}) copy-start(f32[4,384,256]{2,1,0:T(8,128)} %copy-done) | copy-start | bytes 4718596
  87.4 23.3 %collective-permute-start.18 = (f16[4,384,256]{2,1,0:T(8,128)(2,1)}, f16[4,384,256]{2,1,0:T(8,128)(2,1)S(1)}, u32[]{:S(2)}, u32[]{:S(2)}) collective-permute-start(f16[4,384,256]{2,1,0:T(8,128)(2,1)} %get-tuple-element.115), channel_id=1, source_target_pairs={{2,4},{3,5},{4,2},{5,3},{10,12},{11,13},{12,10},{13,11},{18,20},{1... | collective-permute-start | bytes 2359304 | tf_op jit(solution)/shard_map/ppermute | solution.py:41
  89.5 16.4 %copy-start.14 = (bf16[4,384,256]{2,1,0:T(8,128)(2,1)S(1)}, bf16[4,384,256]{2,1,0:T(8,128)(2,1)}, u32[]{:S(2)}) copy-start(bf16[4,384,256]{2,1,0:T(8,128)(2,1)} %copy-done.13) | copy-start | bytes 2359300
  101.4 5.8 %copy-start.4 = (bf16[4,384,256]{2,1,0:T(8,128)(2,1)S(1)}, bf16[4,384,256]{2,1,0:T(8,128)(2,1)}, u32[]{:S(2)}) copy-start(bf16[4,384,256]{2,1,0:T(8,128)(2,1)} %copy-done.3) | copy-start | bytes 2359300
  101.4 5.8 %copy-start.6 = (bf16[4,384,256]{2,1,0:T(8,128)(2,1)S(1)}, bf16[4,384,256]{2,1,0:T(8,128)(2,1)}, u32[]{:S(2)}) copy-start(bf16[4,384,256]{2,1,0:T(8,128)(2,1)} %copy-done.5) | copy-start | bytes 2359300
  110.6 1.4 %copy-start.10 = (f32[4,384,256]{2,1,0:T(8,128)S(1)}, f32[4,384,256]{2,1,0:T(8,128)}, u32[]{:S(2)}) copy-start(f32[4,384,256]{2,1,0:T(8,128)} %copy-done.9) | copy-start | bytes 4718596
  112.3 17.6 %copy-start.12 = (f32[4,384,256]{2,1,0:T(8,128)S(1)}, f32[4,384,256]{2,1,0:T(8,128)}, u32[]{:S(2)}) copy-start(f32[4,384,256]{2,1,0:T(8,128)} %copy-done.11) | copy-start | bytes 4718596
  112.3 17.6 %collective-permute-start.22 = (f16[4,384,256]{2,1,0:T(8,128)(2,1)S(1)}, f16[4,384,256]{2,1,0:T(8,128)(2,1)S(1)}, u32[]{:S(2)}, u32[]{:S(2)}) collective-permute-start(f16[4,384,256]{2,1,0:T(8,128)(2,1)S(1)} %multiply_convert_fusion), channel_id=1, source_target_pairs={{0,2},{1,3},{2,0},{3,1},{4,6},{5,7},{6,4},{7,5},{8,10},{9,11},{10,... | collective-permute-start | bytes 2359304 | tf_op jit(solution)/shard_map/ppermute | solution.py:41
  113.1 18.3 %collective-permute-start.24 = (f16[4,384,256]{2,1,0:T(8,128)(2,1)S(1)}, f16[4,384,256]{2,1,0:T(8,128)(2,1)S(1)}, u32[]{:S(2)}, u32[]{:S(2)}) collective-permute-start(f16[4,384,256]{2,1,0:T(8,128)(2,1)S(1)} %multiply_convert_fusion.1), channel_id=1, source_target_pairs={{0,1},{1,0},{2,3},{3,2},{4,5},{5,4},{6,7},{7,6},{8,9},{9,8},{10,11... | collective-permute-start | bytes 2359304 | tf_op jit(solution)/shard_map/ppermute | solution.py:41
  114.6 17.0 %collective-permute-start.23 = (f16[4,384,256]{2,1,0:T(8,128)(2,1)S(1)}, f16[4,384,256]{2,1,0:T(8,128)(2,1)S(1)}, u32[]{:S(2)}, u32[]{:S(2)}) collective-permute-start(f16[4,384,256]{2,1,0:T(8,128)(2,1)S(1)} %multiply_convert_fusion.2), channel_id=1, source_target_pairs={{2,4},{3,5},{4,2},{5,3},{10,12},{11,13},{12,10},{13,11},{18,20},{1... | collective-permute-start | bytes 2359304 | tf_op jit(solution)/shard_map/ppermute | solution.py:41
  131.6 1.9 %copy-start.7 = (f32[8,3,128,2,128]{4,3,2,1,0:T(2,128)S(1)}, f32[8,3,128,2,128]{4,3,2,1,0:T(2,128)}, u32[]{:S(2)}) copy-start(f32[8,3,128,2,128]{4,3,2,1,0:T(2,128)} %param.5) | copy-start | bytes 9437188

commit v4 on v3

--- a/solution.py
+++ b/solution.py
@@ -146,22 +146,27 @@
     )
 
 
-def column(place, terms, other, cost, start=None):
-    irreps, rows, kk = terms[0][0].shape
+def column(place, terms, other, start=None):
+    irreps, rows, kk = terms[0][0][0].shape
     wide = terms[0][1][0].shape[-1]
-    lefts = [t[0] for t in terms]
+    lefts = [left for t in terms for left in t[0]]
     flat = [b for t in terms for b in t[1]]
     given = [] if start is None else [start]
 
     def body(place_ref, *refs):
-        a_refs, b_refs, out = refs[: len(terms)], refs[len(terms) : 5 * len(terms)], refs[-1]
+        a_refs, b_refs, out = refs[: len(lefts)], refs[len(lefts) : len(lefts) + len(flat)], refs[-1]
         for m in range(4):
 
             @pl.when(pl.program_id(0) == m)
             def _():
                 total = refs[-2][0] if given else None
-                for s, a in enumerate(a_refs):
-                    term = jnp.dot(a[0], b_refs[4 * s + m][0, 0], preferred_element_type=F32)
+                at = 0
+                for s, t in enumerate(terms):
+                    left = a_refs[at][0]
+                    if len(t[0]) == 2:
+                        left = left + a_refs[at + 1][0]
+                    at += len(t[0])
+                    term = jnp.dot(left, b_refs[4 * s + m][0, 0], preferred_element_type=F32)
                     total = term if total is None else total + term
                 out[0] = total
 
@@ -169,28 +174,13 @@
     sums = pl.BlockSpec((1, rows, wide), irrep_of)
     return call(
         body, place, (irreps,),
-        [pl.BlockSpec((1, rows, kk), irrep_of)] * len(terms)
+        [pl.BlockSpec((1, rows, kk), irrep_of)] * len(lefts)
         + [pl.BlockSpec((1, 1, kk, wide), lambda m, p, n=t[2]: (n, p[2] ^ other, 0, 0)) for t in terms for _ in range(4)]
         + [sums] * len(given),
         sums,
         jax.ShapeDtypeStruct((irreps, rows, wide), F32),
         [*lefts, *flat, *given],
-        cost=cost,
-    )
-
-
-def stretch(place, cost):
-    def body(in_ref, out_ref):
-        for n in range(place.shape[0]):
-            out_ref[n] = in_ref[n]
-
-    return pl.pallas_call(
-        body,
-        in_specs=[pl.BlockSpec(memory_space=pltpu.SMEM)],
-        out_specs=pl.BlockSpec(memory_space=pltpu.SMEM),
-        out_shape=jax.ShapeDtypeStruct(place.shape, place.dtype),
-        cost_estimate=pl.CostEstimate(flops=0, bytes_accessed=cost, transcendentals=0),
-    )(place)
+    )
 
 
 def add_all(place, residual, even, odd):
@@ -235,20 +225,22 @@
 
     x_in = row(b_in, SWAP_X)
     a_in = col(after(a_even, b_in), SWAP_Y)
-    swapped = [row(b, SWAP_CORE) for b in (b_own, x_own, b_in)]
+    swapped = [row(b, SWAP_CORE) for b in (b_own, x_own, b_in, pieces[0])]
     pieces, swapped = hold((pieces, swapped))
     got = [col(pieces[d], XOR_Z[d]) for d in (3, 2, 1)]
-    x_in, got = hold((x_in, got))
-
-    swapped.append(row(x_in, SWAP_CORE))
+    piece_x = row(pieces[0], SWAP_X)
+    x_in, got, a_in, piece_x = hold((x_in, got, a_in, piece_x))
+
+    swapped += [row(x_in, SWAP_CORE), row(piece_x, SWAP_CORE)]
     a_in, got, swapped = hold((a_in, got, swapped))
-    b_rows = [[b_own, x_own, swapped[0], swapped[1]], [b_in, x_in, swapped[2], swapped[3]]]
+    b_rows = [[b_own, x_own, swapped[0], swapped[1]], [b_in, x_in, swapped[2], swapped[4]]]
+    piece_rows = [b[None] for b in (pieces[0], piece_x, swapped[3], swapped[5])]
 
     (p3,) = parts(place, [a_even, a_in], b_rows, [3])
     wire3 = (p3 * WIRE).astype(F16)
 
     wire3, g1, g3_mid, got = hold((wire3, g1, g3_mid, got))
-    got = jnp.stack([pieces[0], got[2], got[1], got[0]])
+    got = jnp.stack([got[2], got[1], got[0]])
     i3 = col(wire3, INWARD)
     g2_end = col(g3_mid, OUTWARD)
     g2_mid = col(g1, MIDDLE)
@@ -264,16 +256,17 @@
     g3_end = col(g2_mid, OUTWARD)
     got_rows = [got, got_x, row(got, SWAP_CORE), row(got_x, SWAP_CORE)]
 
-    lefts = [g, g1, jnp.where(middle, g2_mid, g2_end), jnp.where(middle, g3_mid, g3_end)]
-    terms = [(left, got_rows, n) for n, left in enumerate(lefts)]
-    other = (column(place, terms, 1, 0) * WIRE).astype(F16)
+    terms = [((g,), piece_rows, 0)]
+    terms += [(left, got_rows, n) for n, left in enumerate([(g1,), (g2_mid, g2_end), (g3_mid, g3_end)])]
     turn3 = ((p3 + from_wire(i2)) * WIRE).astype(F16)
-    turn3, m2, other = hold((turn3, m2, other))
-
-    q = col(other, SWAP_Y)
-    s1 = to_wire(p1 + from_wire(m2), XOR_Z[1])
+    turn1 = ((p1 + from_wire(m2)) * WIRE).astype(F16)
+    turn3, turn1, g3_end = hold((turn3, turn1, g3_end))
+
+    s1 = col(turn1, XOR_Z[1])
     m3 = col(turn3, MIDDLE)
-    odd = column(place, terms, 0, 0) + from_wire(q)
+    terms[3] = ((g3_mid, g3_end), got_rows, 2)
+    q = to_wire(column(place, terms, 1), SWAP_Y)
+    odd = column(place, terms, 0) + from_wire(q)
     even, m3, odd = hold((p0 + from_wire(s1), m3, odd))
     even = even + from_wire(m3)
 

time: 137 us -> 131 us (0.956)
  other arithmetic: 6.96 us -> 2.24 us
  waiting for transfers between devices: 68.3 us -> 70.9 us
  Pallas kernels: 18.1 us -> 15.9 us
    ppermute x16, waiting for transfers between devices: 61.8 us -> 65.1 us  [col(): return lax.ppermute(x, 'col', pairs)]
    ppermute x16, starting transfers between devices: 30.8 us -> 27.7 us  [col(): return lax.ppermute(x, 'col', pairs)]
    select_n x2 -> x0, other arithmetic: 2.45 us -> none  [the longest x1 1.23 us: mixed(): jnp.where(middle, g2_mid, g2_end)]
    ppermute x9 -> x12, starting transfers between devices: 5.78 us -> 8.19 us  [row(): return lax.ppermute(x, 'row', pairs)]
    pallas_call x8, Pallas kernels: 18.1 us -> 15.9 us  [call(): pl.pallas_call(body, grid_spec=pltpu.PrefetchScalarGridSpec(num_scalar_pr...]
    unnamed x32 -> x6, local copies, waits for them, and re-layouts: 5.94 us -> 4.64 us
    ppermute x9 -> x12, waiting for transfers between devices: 6.48 us -> 5.78 us  [row(): return lax.ppermute(x, 'row', pairs)]
  transfers between devices with their start and end apart: 25 -> 28, of which waited for: 14 -> 12; matrix products, arithmetic and copies ran while one was open for 5% -> 1% of each run, Pallas kernels for 9% -> 8%
where the time goes in v4:
time: 131 us; the launch traced here: 130 us
  waiting for transfers between devices  70.9 us (54%)
  starting transfers between devices  35.9 us (27%)
  Pallas kernels  15.9 us (12%)
  local copies, waits for them, and re-layouts  4.64 us (4%)
  other arithmetic  2.24 us (2%)
    ppermute x16, waiting for transfers between devices, col(): return lax.ppermute(x, 'col', pairs)  65.1 us
    ppermute x16, starting transfers between devices, col(): return lax.ppermute(x, 'col', pairs)  27.7 us
    pallas_call x8, Pallas kernels, call(): pl.pallas_call(body, grid_spec=pltpu.PrefetchScalarGridSpec(num_scalar_pr...  15.9 us
    ppermute x12, starting transfers between devices, row(): return lax.ppermute(x, 'row', pairs)  8.19 us
    ppermute x12, waiting for transfers between devices, row(): return lax.ppermute(x, 'row', pairs)  5.78 us
    unnamed x6, local copies, waits for them, and re-layouts  4.64 us
  transfers between devices with their start and end apart: 28, of which 12 were waited for; matrix products, arithmetic and copies ran while one was open for 1% of the time, Pallas kernels for 8%

profile of v4, /device:TPU:0, one launch (start us, length us, event | category | flops | bytes accessed | tf_op | source)
XLA Modules:
  0.0 129.8 jit_solution(5168208840356939498)
XLA Ops:
  0.1 1.4 %copy-done.2 = bf16[8,3,128,2,128]{4,3,2,1,0:T(2,128)(2,1)S(1)} copy-done((bf16[8,3,128,2,128]{4,3,2,1,0:T(2,128)(2,1)S(1)}, bf16[8,3,128,2,128]{4,3,2,1,0:T(2,128)(2,1)}, u32[]{:S(2)}) %copy-start.2) | copy-done | bytes 1572888
  1.5 1.1 shard_map.37
  2.6 3.1 %collective-permute-start = (bf16[4,384,256]{2,1,0:T(8,128)(2,1)S(1)}, bf16[4,384,256]{2,1,0:T(8,128)(2,1)S(1)}, u32[]{:S(2)}, u32[]{:S(2)}) collective-permute-start(bf16[4,384,256]{2,1,0:T(8,128)(2,1)S(1)} %get-tuple-element.78.refs_0_), channel_id=1, source_target_pairs={{0,2},{1,3},{2,0},{3,1},{4,6},{5,7},{6,4},{7,5},{8,10},{9,11},{10,... | collective-permute-start | bytes 2359304 | tf_op jit(solution)/shard_map/ppermute | solution.py:41
  5.7 1.6 %copy-done = bf16[2,2,128,16,128]{4,3,2,1,0:T(8,128)(2,1)S(1)} copy-done((bf16[2,2,128,16,128]{4,3,2,1,0:T(8,128)(2,1)S(1)}, bf16[2,2,128,16,128]{4,3,2,1,0:T(8,128)(2,1)}, u32[]{:S(2)}) %copy-start) | copy-done | bytes 2097176
  7.2 1.5 %shard_map.39 = (bf16[4,256,256]{2,1,0:T(8,128)(2,1)S(1)}, bf16[4,256,256]{2,1,0:T(8,128)(2,1)S(1)}) custom-call(s32[3]{0:T(128)S(1)} %pad_add_fusion._.place_ref, bf16[2,2,128,16,128]{4,3,2,1,0:T(8,128)(2,1)S(1)} %copy-done), custom_call_target="tpu_custom_call" | custom-call | tf_op jit(solution)/shard_map/pallas_call | solution.py:61
  8.8 0.7 collective-permute-start.1
  9.5 1.6 %collective-permute-start.3 = (bf16[4,256,256]{2,1,0:T(8,128)(2,1)S(1)}, bf16[4,256,256]{2,1,0:T(8,128)(2,1)S(1)}, u32[]{:S(2)}, u32[]{:S(2)}) collective-permute-start(bf16[4,256,256]{2,1,0:T(8,128)(2,1)S(1)} %get-tuple-element.77), channel_id=1, source_target_pairs={{0,1},{1,0},{2,3},{3,2},{4,5},{5,4},{6,7},{7,6},{8,9},{9,8},{10,11... | collective-permute-start | bytes 1572872 | tf_op jit(solution)/shard_map/ppermute | solution.py:41
  11.1 1.5 %collective-permute-start.2 = (bf16[4,256,256]{2,1,0:T(8,128)(2,1)S(1)}, bf16[4,256,256]{2,1,0:T(8,128)(2,1)S(1)}, u32[]{:S(2)}, u32[]{:S(2)}) collective-permute-start(bf16[4,256,256]{2,1,0:T(8,128)(2,1)S(1)} %get-tuple-element.85.refs_2_.refs_10_.refs_18_), channel_id=1, source_target_pairs={{0,16},{8,24},{16,0},{24,8},{1,17},{9,25},{17,1},{25,9},{2,18},{10... | collective-permute-start | bytes 1572872 | tf_op jit(solution)/shard_map/ppermute | solution.py:45
  12.6 1.5 %shard_map.38 = (bf16[2,256,256]{2,1,0:T(8,128)(2,1)S(1)}, bf16[2,256,256]{2,1,0:T(8,128)(2,1)S(1)}, bf16[2,256,256]{2,1,0:T(8,128)(2,1)S(1)}, bf16[2,256,256]{2,1,0:T(8,128)(2,1)S(1)}) custom-call(s32[3]{0:T(128)S(1)} %pad_add_fusion._.place_ref, bf16[2,2,128,16,128]{4,3,2,1,0:T(8,128)(2,1)S(1)} %copy-done), custom_call_target="tpu_custom_call" | custom-call | tf_op jit(solution)/shard_map/pallas_call | solution.py:61
  14.1 8.8 %collective-permute-done.3.refs_6_.refs_14_.refs_22_ = bf16[4,256,256]{2,1,0:T(8,128)(2,1)S(1)} collective-permute-done((bf16[4,256,256]{2,1,0:T(8,128)(2,1)S(1)}, bf16[4,256,256]{2,1,0:T(8,128)(2,1)S(1)}, u32[]{:S(2)}, u32[]{:S(2)}) %collective-permute-start.3) | collective-permute-done | bytes 524320 | tf_op jit(solution)/shard_map/ppermute | solution.py:41
  22.9 1.2 collective-permute-done.2.refs_3_.refs_11_.refs_19_
  24.2 0.5 collective-permute-start.5
  24.8 0.4 collective-permute-start.7
  25.2 1.5 %collective-permute-start.4 = (bf16[4,256,256]{2,1,0:T(8,128)(2,1)S(1)}, bf16[4,256,256]{2,1,0:T(8,128)(2,1)S(1)}, u32[]{:S(2)}, u32[]{:S(2)}) collective-permute-start(bf16[4,256,256]{2,1,0:T(8,128)(2,1)S(1)} %collective-permute-done.3.refs_6_.refs_14_.refs_22_), channel_id=1, source_target_pairs={{0,16},{8,24},{16,0},{24,8},{1,17},{9,25},{17,1},{25,9},{2,18},{10... | collective-permute-start | bytes 1572872 | tf_op jit(solution)/shard_map/ppermute | solution.py:45
  26.7 0.7 collective-permute-start.12
  27.4 0.6 collective-permute-done.7.refs_8_.refs_16_.refs_24_
  28.0 3.1 %collective-permute-start.9 = (bf16[2,256,256]{2,1,0:T(8,128)(2,1)S(1)}, bf16[2,256,256]{2,1,0:T(8,128)(2,1)S(1)}, u32[]{:S(2)}, u32[]{:S(2)}) collective-permute-start(bf16[2,256,256]{2,1,0:T(8,128)(2,1)S(1)} %get-tuple-element.87), channel_id=1, source_target_pairs={{0,6},{1,7},{2,4},{3,5},{4,2},{5,3},{6,0},{7,1},{8,14},{9,15},{10,... | collective-permute-start | bytes 786440 | tf_op jit(solution)/shard_map/ppermute | solution.py:41
  31.1 5.6 %collective-permute-start.10 = (bf16[2,256,256]{2,1,0:T(8,128)(2,1)S(1)}, bf16[2,256,256]{2,1,0:T(8,128)(2,1)S(1)}, u32[]{:S(2)}, u32[]{:S(2)}) collective-permute-start(bf16[2,256,256]{2,1,0:T(8,128)(2,1)S(1)} %get-tuple-element.88), channel_id=1, source_target_pairs={{0,4},{1,5},{2,6},{3,7},{4,0},{5,1},{6,2},{7,3},{8,12},{9,13},{10,... | collective-permute-start | bytes 786440 | tf_op jit(solution)/shard_map/ppermute | solution.py:41
  36.9 2.2 %collective-permute-done.4.refs_7_.refs_15_.refs_23_ = bf16[4,256,256]{2,1,0:T(8,128)(2,1)S(1)} collective-permute-done((bf16[4,256,256]{2,1,0:T(8,128)(2,1)S(1)}, bf16[4,256,256]{2,1,0:T(8,128)(2,1)S(1)}, u32[]{:S(2)}, u32[]{:S(2)}) %collective-permute-start.4) | collective-permute-done | bytes 524320 | tf_op jit(solution)/shard_map/ppermute | solution.py:45
  39.1 1.5 %collective-permute-start.13 = (bf16[2,256,256]{2,1,0:T(8,128)(2,1)S(1)}, bf16[2,256,256]{2,1,0:T(8,128)(2,1)S(1)}, u32[]{:S(2)}, u32[]{:S(2)}) collective-permute-start(bf16[2,256,256]{2,1,0:T(8,128)(2,1)S(1)} %get-tuple-element.91), channel_id=1, source_target_pairs={{0,16},{8,24},{16,0},{24,8},{1,17},{9,25},{17,1},{25,9},{2,18},{10... | collective-permute-start | bytes 786440 | tf_op jit(solution)/shard_map/ppermute | solution.py:45
  40.6 14.4 %collective-permute-done.10 = bf16[2,256,256]{2,1,0:T(8,128)(2,1)S(1)} collective-permute-done((bf16[2,256,256]{2,1,0:T(8,128)(2,1)S(1)}, bf16[2,256,256]{2,1,0:T(8,128)(2,1)S(1)}, u32[]{:S(2)}, u32[]{:S(2)}) %collective-permute-start.10) | collective-permute-done | bytes 262176 | tf_op jit(solution)/shard_map/ppermute | solution.py:41
  55.1 0.5 collective-permute-start.15
  55.6 1.8 %collective-permute-done.15 = bf16[2,256,256]{2,1,0:T(8,128)(2,1)S(1)} collective-permute-done((bf16[2,256,256]{2,1,0:T(8,128)(2,1)S(1)}, bf16[2,256,256]{2,1,0:T(8,128)(2,1)S(1)}, u32[]{:S(2)}, u32[]{:S(2)}) %collective-permute-start.15) | collective-permute-done | bytes 262176 | tf_op jit(solution)/shard_map/ppermute | solution.py:45
  57.3 1.7 %shard_map.40 = f32[4,384,256]{2,1,0:T(8,128)S(1)} custom-call(s32[3]{0:T(128)S(1)} %pad_add_fusion._.place_ref, bf16[4,384,256]{2,1,0:T(8,128)(2,1)S(1)} %get-tuple-element.113.refs_0_, bf16[4,384,256]{2,1,0:T(8,128)(2,1)S(1)} %collective-permute-done.12.refs_1_, bf16[4,256,256]{2,1,0:T(8,128)(2,1)S(1)} %get-tuple-element.85.refs_2_.refs_10_.refs_18_, ...), custom_call_target="tpu_custom_call" | custom-call | tf_op jit(solution)/shard_map/pallas_call | solution.py:61
  59.3 1.9 %collective-permute-start.17 = (f16[4,384,256]{2,1,0:T(8,128)(2,1)S(1)}, f16[4,384,256]{2,1,0:T(8,128)(2,1)S(1)}, u32[]{:S(2)}, u32[]{:S(2)}) collective-permute-start(f16[4,384,256]{2,1,0:T(8,128)(2,1)S(1)} %multiply_convert_fusion.5), channel_id=1, source_target_pairs={{0,2},{1,3},{6,4},{7,5},{8,10},{9,11},{14,12},{15,13},{16,18},{17,... | collective-permute-start | bytes 2359304 | tf_op jit(solution)/shard_map/ppermute | solution.py:41
  61.3 1.6 %collective-permute-start.19 = (bf16[3,2,256,256]{3,2,1,0:T(8,128)(2,1)S(1)}, bf16[3,2,256,256]{3,2,1,0:T(8,128)(2,1)S(1)}, u32[]{:S(2)}, u32[]{:S(2)}) collective-permute-start(bf16[3,2,256,256]{3,2,1,0:T(8,128)(2,1)S(1)} %pad_maximum_fusion.refs_10_.refs_14_.refs_18_), channel_id=1, source_target_pairs={{0,16},{8,24},{16,0},{24,8},{1,17},{9,25},{17,1},{25,9},{2,18},{10... | collective-permute-start | bytes 2359304 | tf_op jit(solution)/shard_map/ppermute | solution.py:45
  62.8 0.7 collective-permute-start.18
  63.5 1.3 collective-permute-start.20
  64.8 2.7 %shard_map.41 = (f32[4,384,256]{2,1,0:T(8,128)S(1)}, f32[4,384,256]{2,1,0:T(8,128)S(1)}, f32[4,384,256]{2,1,0:T(8,128)S(1)}) custom-call(s32[3]{0:T(128)S(1)} %pad_add_fusion._.place_ref, bf16[4,384,256]{2,1,0:T(8,128)(2,1)S(1)} %get-tuple-element.113.refs_0_, bf16[4,384,256]{2,1,0:T(8,128)(2,1)S(1)} %collective-permute-done.12.refs_1_, ...), custom_call_target="tpu_custom_call" | custom-call | tf_op jit(solution)/shard_map/pallas_call | solution.py:61
  67.6 10.6 %collective-permute-done.17 = f16[4,384,256]{2,1,0:T(8,128)(2,1)S(1)} collective-permute-done((f16[4,384,256]{2,1,0:T(8,128)(2,1)S(1)}, f16[4,384,256]{2,1,0:T(8,128)(2,1)S(1)}, u32[]{:S(2)}, u32[]{:S(2)}) %collective-permute-start.17) | collective-permute-done | bytes 786464 | tf_op jit(solution)/shard_map/ppermute | solution.py:41
  78.2 0.5 multiply_convert_fusion.2
  78.7 4.4 %collective-permute-start.16 = (f16[4,384,256]{2,1,0:T(8,128)(2,1)S(1)}, f16[4,384,256]{2,1,0:T(8,128)(2,1)S(1)}, u32[]{:S(2)}, u32[]{:S(2)}) collective-permute-start(f16[4,384,256]{2,1,0:T(8,128)(2,1)S(1)} %get-tuple-element.136), channel_id=1, source_target_pairs={{0,2},{1,3},{6,4},{7,5},{8,10},{9,11},{14,12},{15,13},{16,18},{17,... | collective-permute-start | bytes 2359304 | tf_op jit(solution)/shard_map/ppermute | solution.py:41
  83.2 1.3 %collective-permute-done.20.refs_3_ = bf16[4,384,256]{2,1,0:T(8,128)(2,1)S(1)} collective-permute-done((bf16[4,384,256]{2,1,0:T(8,128)(2,1)S(1)}, bf16[4,384,256]{2,1,0:T(8,128)(2,1)S(1)}, u32[]{:S(2)}, u32[]{:S(2)}) %collective-permute-start.20) | collective-permute-done | bytes 786464 | tf_op jit(solution)/shard_map/ppermute | solution.py:41
  84.5 0.7 collective-permute-start.21
  85.2 1.3 collective-permute-start.22
  86.5 0.5 collective-permute-start.26
  87.0 12.3 %collective-permute-done.16 = f16[4,384,256]{2,1,0:T(8,128)(2,1)S(1)} collective-permute-done((f16[4,384,256]{2,1,0:T(8,128)(2,1)S(1)}, f16[4,384,256]{2,1,0:T(8,128)(2,1)S(1)}, u32[]{:S(2)}, u32[]{:S(2)}) %collective-permute-start.16) | collective-permute-done | bytes 786464 | tf_op jit(solution)/shard_map/ppermute | solution.py:41
  99.3 0.3 multiply_convert_fusion.3
  99.7 0.3 multiply_convert_fusion.1
  100.0 5.2 %collective-permute-done.22.refs_5_ = bf16[4,384,256]{2,1,0:T(8,128)(2,1)S(1)} collective-permute-done((bf16[4,384,256]{2,1,0:T(8,128)(2,1)S(1)}, bf16[4,384,256]{2,1,0:T(8,128)(2,1)S(1)}, u32[]{:S(2)}, u32[]{:S(2)}) %collective-permute-start.22) | collective-permute-done | bytes 786464 | tf_op jit(solution)/shard_map/ppermute | solution.py:41
  105.2 2.3 %shard_map.43 = f32[4,384,256]{2,1,0:T(8,128)S(1)} custom-call(s32[3]{0:T(128)S(1)} %pad_add_fusion._.place_ref, bf16[4,384,256]{2,1,0:T(8,128)(2,1)S(1)} %get-tuple-element.78.refs_0_, bf16[4,384,256]{2,1,0:T(8,128)(2,1)S(1)} %collective-permute-done.refs_1_, bf16[4,384,256]{2,1,0:T(8,128)(2,1)S(1)} %collective-permute-done.18.refs_2_, ...), custom_call_target="tpu_custom_call" | custom-call | tf_op jit(solution)/shard_map/pallas_call | solution.py:61
  107.7 1.6 %collective-permute-start.27 = (f16[4,384,256]{2,1,0:T(8,128)(2,1)S(1)}, f16[4,384,256]{2,1,0:T(8,128)(2,1)S(1)}, u32[]{:S(2)}, u32[]{:S(2)}) collective-permute-start(f16[4,384,256]{2,1,0:T(8,128)(2,1)S(1)} %multiply_convert_fusion), channel_id=1, source_target_pairs={{0,1},{1,0},{2,3},{3,2},{4,5},{5,4},{6,7},{7,6},{8,9},{9,8},{10,11... | collective-permute-start | bytes 2359304 | tf_op jit(solution)/shard_map/ppermute | solution.py:41
  109.3 0.7 collective-permute-start.24
  110.0 2.3 %shard_map.42 = f32[4,384,256]{2,1,0:T(8,128)S(1)} custom-call(s32[3]{0:T(128)S(1)} %pad_add_fusion._.place_ref, bf16[4,384,256]{2,1,0:T(8,128)(2,1)S(1)} %get-tuple-element.78.refs_0_, bf16[4,384,256]{2,1,0:T(8,128)(2,1)S(1)} %collective-permute-done.refs_1_, bf16[4,384,256]{2,1,0:T(8,128)(2,1)S(1)} %collective-permute-done.18.refs_2_, ...), custom_call_target="tpu_custom_call" | custom-call | tf_op jit(solution)/shard_map/pallas_call | solution.py:61
  112.3 10.1 %collective-permute-done.23 = f16[4,384,256]{2,1,0:T(8,128)(2,1)S(1)} collective-permute-done((f16[4,384,256]{2,1,0:T(8,128)(2,1)S(1)}, f16[4,384,256]{2,1,0:T(8,128)(2,1)S(1)}, u32[]{:S(2)}, u32[]{:S(2)}) %collective-permute-start.23) | collective-permute-done | bytes 786464 | tf_op jit(solution)/shard_map/ppermute | solution.py:41
  122.6 2.4 %collective-permute-done.27 = f16[4,384,256]{2,1,0:T(8,128)(2,1)S(1)} collective-permute-done((f16[4,384,256]{2,1,0:T(8,128)(2,1)S(1)}, f16[4,384,256]{2,1,0:T(8,128)(2,1)S(1)}, u32[]{:S(2)}, u32[]{:S(2)}) %collective-permute-start.27) | collective-permute-done | bytes 786464 | tf_op jit(solution)/shard_map/ppermute | solution.py:41
  125.4 1.6 %copy-done.1 = f32[8,3,128,2,128]{4,3,2,1,0:T(2,128)S(1)} copy-done((f32[8,3,128,2,128]{4,3,2,1,0:T(2,128)S(1)}, f32[8,3,128,2,128]{4,3,2,1,0:T(2,128)}, u32[]{:S(2)}) %copy-start.1) | copy-done | bytes 3145752
  127.0 2.8 %shard_map.44 = f32[8,768,128]{2,1,0:T(8,128)} custom-call(s32[3]{0:T(128)S(1)} %pad_add_fusion._.place_ref, f32[8,768,128]{2,1,0:T(8,128)S(1)} %bitcast.13, f32[4,384,256]{2,1,0:T(8,128)S(1)} %multiply_add_fusion.even_ref, f32[4,384,256]{2,1,0:T(8,128)S(1)} %multiply_add_fusion.1.odd_ref), custom_call_target="tpu_custom_call" | custom-call | tf_op jit(solution)/shard_map/pallas_call | solution.py:61
  (32 shorter events, 1.7 us)
Async XLA Ops:
  0.1 1.4 %copy-start.2 = (bf16[8,3,128,2,128]{4,3,2,1,0:T(2,128)(2,1)S(1)}, bf16[8,3,128,2,128]{4,3,2,1,0:T(2,128)(2,1)}, u32[]{:S(2)}) copy-start(bf16[8,3,128,2,128]{4,3,2,1,0:T(2,128)(2,1)} %param.4) | copy-start | bytes 4718596
  2.6 21.6 %collective-permute-start = (bf16[4,384,256]{2,1,0:T(8,128)(2,1)S(1)}, bf16[4,384,256]{2,1,0:T(8,128)(2,1)S(1)}, u32[]{:S(2)}, u32[]{:S(2)}) collective-permute-start(bf16[4,384,256]{2,1,0:T(8,128)(2,1)S(1)} %get-tuple-element.78.refs_0_), channel_id=1, source_target_pairs={{0,2},{1,3},{2,0},{3,1},{4,6},{5,7},{6,4},{7,5},{8,10},{9,11},{10,... | collective-permute-start | bytes 2359304 | tf_op jit(solution)/shard_map/ppermute | solution.py:41
  5.7 1.6 %copy-start = (bf16[2,2,128,16,128]{4,3,2,1,0:T(8,128)(2,1)S(1)}, bf16[2,2,128,16,128]{4,3,2,1,0:T(8,128)(2,1)}, u32[]{:S(2)}) copy-start(bf16[2,2,128,16,128]{4,3,2,1,0:T(8,128)(2,1)} %in_ref.1) | copy-start | bytes 6291460
  8.8 15.4 %collective-permute-start.1 = (bf16[4,384,256]{2,1,0:T(8,128)(2,1)S(1)}, bf16[4,384,256]{2,1,0:T(8,128)(2,1)S(1)}, u32[]{:S(2)}, u32[]{:S(2)}) collective-permute-start(bf16[4,384,256]{2,1,0:T(8,128)(2,1)S(1)} %get-tuple-element.78.refs_0_), channel_id=1, source_target_pairs={{2,4},{3,5},{4,2},{5,3},{10,12},{11,13},{12,10},{13,11},{18,20},{1... | collective-permute-start | bytes 2359304 | tf_op jit(solution)/shard_map/ppermute | solution.py:41
  9.5 13.4 %collective-permute-start.3 = (bf16[4,256,256]{2,1,0:T(8,128)(2,1)S(1)}, bf16[4,256,256]{2,1,0:T(8,128)(2,1)S(1)}, u32[]{:S(2)}, u32[]{:S(2)}) collective-permute-start(bf16[4,256,256]{2,1,0:T(8,128)(2,1)S(1)} %get-tuple-element.77), channel_id=1, source_target_pairs={{0,1},{1,0},{2,3},{3,2},{4,5},{5,4},{6,7},{7,6},{8,9},{9,8},{10,11... | collective-permute-start | bytes 1572872 | tf_op jit(solution)/shard_map/ppermute | solution.py:41
  11.1 13.1 %collective-permute-start.2 = (bf16[4,256,256]{2,1,0:T(8,128)(2,1)S(1)}, bf16[4,256,256]{2,1,0:T(8,128)(2,1)S(1)}, u32[]{:S(2)}, u32[]{:S(2)}) collective-permute-start(bf16[4,256,256]{2,1,0:T(8,128)(2,1)S(1)} %get-tuple-element.85.refs_2_.refs_10_.refs_18_), channel_id=1, source_target_pairs={{0,16},{8,24},{16,0},{24,8},{1,17},{9,25},{17,1},{25,9},{2,18},{10... | collective-permute-start | bytes 1572872 | tf_op jit(solution)/shard_map/ppermute | solution.py:45
  24.2 2.5 %collective-permute-start.8 = (bf16[2,256,256]{2,1,0:T(8,128)(2,1)S(1)}, bf16[2,256,256]{2,1,0:T(8,128)(2,1)S(1)}, u32[]{:S(2)}, u32[]{:S(2)}) collective-permute-start(bf16[2,256,256]{2,1,0:T(8,128)(2,1)S(1)} %get-tuple-element.91), channel_id=1, source_target_pairs={{0,8},{8,0},{16,24},{24,16},{1,9},{9,1},{17,25},{25,17},{2,10},{10... | collective-permute-start | bytes 786440 | tf_op jit(solution)/shard_map/ppermute | solution.py:45
  24.2 3.2 %collective-permute-start.5 = (bf16[4,256,256]{2,1,0:T(8,128)(2,1)S(1)}, bf16[4,256,256]{2,1,0:T(8,128)(2,1)S(1)}, u32[]{:S(2)}, u32[]{:S(2)}) collective-permute-start(bf16[4,256,256]{2,1,0:T(8,128)(2,1)S(1)} %get-tuple-element.85.refs_2_.refs_10_.refs_18_), channel_id=1, source_target_pairs={{0,8},{8,0},{16,24},{24,16},{1,9},{9,1},{17,25},{25,17},{2,10},{10... | collective-permute-start | bytes 1572872 | tf_op jit(solution)/shard_map/ppermute | solution.py:45
  24.7 2.7 %collective-permute-start.6 = (bf16[4,256,256]{2,1,0:T(8,128)(2,1)S(1)}, bf16[4,256,256]{2,1,0:T(8,128)(2,1)S(1)}, u32[]{:S(2)}, u32[]{:S(2)}) collective-permute-start(bf16[4,256,256]{2,1,0:T(8,128)(2,1)S(1)} %collective-permute-done.2.refs_3_.refs_11_.refs_19_), channel_id=1, source_target_pairs={{0,8},{8,0},{16,24},{24,16},{1,9},{9,1},{17,25},{25,17},{2,10},{10... | collective-permute-start | bytes 1572872 | tf_op jit(solution)/shard_map/ppermute | solution.py:45
  24.8 3.2 %collective-permute-start.7 = (bf16[4,256,256]{2,1,0:T(8,128)(2,1)S(1)}, bf16[4,256,256]{2,1,0:T(8,128)(2,1)S(1)}, u32[]{:S(2)}, u32[]{:S(2)}) collective-permute-start(bf16[4,256,256]{2,1,0:T(8,128)(2,1)S(1)} %collective-permute-done.3.refs_6_.refs_14_.refs_22_), channel_id=1, source_target_pairs={{0,8},{8,0},{16,24},{24,16},{1,9},{9,1},{17,25},{25,17},{2,10},{10... | collective-permute-start | bytes 1572872 | tf_op jit(solution)/shard_map/ppermute | solution.py:45
  25.2 13.9 %collective-permute-start.4 = (bf16[4,256,256]{2,1,0:T(8,128)(2,1)S(1)}, bf16[4,256,256]{2,1,0:T(8,128)(2,1)S(1)}, u32[]{:S(2)}, u32[]{:S(2)}) collective-permute-start(bf16[4,256,256]{2,1,0:T(8,128)(2,1)S(1)} %collective-permute-done.3.refs_6_.refs_14_.refs_22_), channel_id=1, source_target_pairs={{0,16},{8,24},{16,0},{24,8},{1,17},{9,25},{17,1},{25,9},{2,18},{10... | collective-permute-start | bytes 1572872 | tf_op jit(solution)/shard_map/ppermute | solution.py:45
  26.7 28.3 %collective-permute-start.12 = (bf16[4,384,256]{2,1,0:T(8,128)(2,1)S(1)}, bf16[4,384,256]{2,1,0:T(8,128)(2,1)S(1)}, u32[]{:S(2)}, u32[]{:S(2)}) collective-permute-start(bf16[4,384,256]{2,1,0:T(8,128)(2,1)S(1)} %get-tuple-element.113.refs_0_), channel_id=1, source_target_pairs={{0,1},{1,0},{2,3},{3,2},{4,5},{5,4},{6,7},{7,6},{8,9},{9,8},{10,11... | collective-permute-start | bytes 2359304 | tf_op jit(solution)/shard_map/ppermute | solution.py:41
  28.0 12.6 %collective-permute-start.9 = (bf16[2,256,256]{2,1,0:T(8,128)(2,1)S(1)}, bf16[2,256,256]{2,1,0:T(8,128)(2,1)S(1)}, u32[]{:S(2)}, u32[]{:S(2)}) collective-permute-start(bf16[2,256,256]{2,1,0:T(8,128)(2,1)S(1)} %get-tuple-element.87), channel_id=1, source_target_pairs={{0,6},{1,7},{2,4},{3,5},{4,2},{5,3},{6,0},{7,1},{8,14},{9,15},{10,... | collective-permute-start | bytes 786440 | tf_op jit(solution)/shard_map/ppermute | solution.py:41
  31.1 23.9 %collective-permute-start.10 = (bf16[2,256,256]{2,1,0:T(8,128)(2,1)S(1)}, bf16[2,256,256]{2,1,0:T(8,128)(2,1)S(1)}, u32[]{:S(2)}, u32[]{:S(2)}) collective-permute-start(bf16[2,256,256]{2,1,0:T(8,128)(2,1)S(1)} %get-tuple-element.88), channel_id=1, source_target_pairs={{0,4},{1,5},{2,6},{3,7},{4,0},{5,1},{6,2},{7,3},{8,12},{9,13},{10,... | collective-permute-start | bytes 786440 | tf_op jit(solution)/shard_map/ppermute | solution.py:41
  36.7 18.3 %collective-permute-start.11 = (bf16[2,256,256]{2,1,0:T(8,128)(2,1)S(1)}, bf16[2,256,256]{2,1,0:T(8,128)(2,1)S(1)}, u32[]{:S(2)}, u32[]{:S(2)}) collective-permute-start(bf16[2,256,256]{2,1,0:T(8,128)(2,1)S(1)} %get-tuple-element.89), channel_id=1, source_target_pairs={{0,2},{1,3},{2,0},{3,1},{4,6},{5,7},{6,4},{7,5},{8,10},{9,11},{10,... | collective-permute-start | bytes 786440 | tf_op jit(solution)/shard_map/ppermute | solution.py:41
  39.1 15.9 %collective-permute-start.13 = (bf16[2,256,256]{2,1,0:T(8,128)(2,1)S(1)}, bf16[2,256,256]{2,1,0:T(8,128)(2,1)S(1)}, u32[]{:S(2)}, u32[]{:S(2)}) collective-permute-start(bf16[2,256,256]{2,1,0:T(8,128)(2,1)S(1)} %get-tuple-element.91), channel_id=1, source_target_pairs={{0,16},{8,24},{16,0},{24,8},{1,17},{9,25},{17,1},{25,9},{2,18},{10... | collective-permute-start | bytes 786440 | tf_op jit(solution)/shard_map/ppermute | solution.py:45
  55.0 2.4 %collective-permute-start.14 = (bf16[4,256,256]{2,1,0:T(8,128)(2,1)S(1)}, bf16[4,256,256]{2,1,0:T(8,128)(2,1)S(1)}, u32[]{:S(2)}, u32[]{:S(2)}) collective-permute-start(bf16[4,256,256]{2,1,0:T(8,128)(2,1)S(1)} %collective-permute-done.4.refs_7_.refs_15_.refs_23_), channel_id=1, source_target_pairs={{0,8},{8,0},{16,24},{24,16},{1,9},{9,1},{17,25},{25,17},{2,10},{10... | collective-permute-start | bytes 1572872 | tf_op jit(solution)/shard_map/ppermute | solution.py:45
  55.1 2.3 %collective-permute-start.15 = (bf16[2,256,256]{2,1,0:T(8,128)(2,1)S(1)}, bf16[2,256,256]{2,1,0:T(8,128)(2,1)S(1)}, u32[]{:S(2)}, u32[]{:S(2)}) collective-permute-start(bf16[2,256,256]{2,1,0:T(8,128)(2,1)S(1)} %collective-permute-done.13), channel_id=1, source_target_pairs={{0,8},{8,0},{16,24},{24,16},{1,9},{9,1},{17,25},{25,17},{2,10},{10... | collective-permute-start | bytes 786440 | tf_op jit(solution)/shard_map/ppermute | solution.py:45
  59.3 19.0 %collective-permute-start.17 = (f16[4,384,256]{2,1,0:T(8,128)(2,1)S(1)}, f16[4,384,256]{2,1,0:T(8,128)(2,1)S(1)}, u32[]{:S(2)}, u32[]{:S(2)}) collective-permute-start(f16[4,384,256]{2,1,0:T(8,128)(2,1)S(1)} %multiply_convert_fusion.5), channel_id=1, source_target_pairs={{0,2},{1,3},{6,4},{7,5},{8,10},{9,11},{14,12},{15,13},{16,18},{17,... | collective-permute-start | bytes 2359304 | tf_op jit(solution)/shard_map/ppermute | solution.py:41
  61.3 21.9 %collective-permute-start.19 = (bf16[3,2,256,256]{3,2,1,0:T(8,128)(2,1)S(1)}, bf16[3,2,256,256]{3,2,1,0:T(8,128)(2,1)S(1)}, u32[]{:S(2)}, u32[]{:S(2)}) collective-permute-start(bf16[3,2,256,256]{3,2,1,0:T(8,128)(2,1)S(1)} %pad_maximum_fusion.refs_10_.refs_14_.refs_18_), channel_id=1, source_target_pairs={{0,16},{8,24},{16,0},{24,8},{1,17},{9,25},{17,1},{25,9},{2,18},{10... | collective-permute-start | bytes 2359304 | tf_op jit(solution)/shard_map/ppermute | solution.py:45
  62.8 20.3 %collective-permute-start.18 = (bf16[4,384,256]{2,1,0:T(8,128)(2,1)S(1)}, bf16[4,384,256]{2,1,0:T(8,128)(2,1)S(1)}, u32[]{:S(2)}, u32[]{:S(2)}) collective-permute-start(bf16[4,384,256]{2,1,0:T(8,128)(2,1)S(1)} %collective-permute-done.refs_1_), channel_id=1, source_target_pairs={{2,4},{3,5},{4,2},{5,3},{10,12},{11,13},{12,10},{13,11},{18,20},{1... | collective-permute-start | bytes 2359304 | tf_op jit(solution)/shard_map/ppermute | solution.py:41
  63.5 20.9 %collective-permute-start.20 = (bf16[4,384,256]{2,1,0:T(8,128)(2,1)S(1)}, bf16[4,384,256]{2,1,0:T(8,128)(2,1)S(1)}, u32[]{:S(2)}, u32[]{:S(2)}) collective-permute-start(bf16[4,384,256]{2,1,0:T(8,128)(2,1)S(1)} %collective-permute-done.1.refs_4_), channel_id=1, source_target_pairs={{2,0},{3,1},{4,6},{5,7},{10,8},{11,9},{12,14},{13,15},{18,16},{19,... | collective-permute-start | bytes 2359304 | tf_op jit(solution)/shard_map/ppermute | solution.py:41
  78.7 20.6 %collective-permute-start.16 = (f16[4,384,256]{2,1,0:T(8,128)(2,1)S(1)}, f16[4,384,256]{2,1,0:T(8,128)(2,1)S(1)}, u32[]{:S(2)}, u32[]{:S(2)}) collective-permute-start(f16[4,384,256]{2,1,0:T(8,128)(2,1)S(1)} %get-tuple-element.136), channel_id=1, source_target_pairs={{0,2},{1,3},{6,4},{7,5},{8,10},{9,11},{14,12},{15,13},{16,18},{17,... | collective-permute-start | bytes 2359304 | tf_op jit(solution)/shard_map/ppermute | solution.py:41
  84.5 15.2 %collective-permute-start.21 = (f16[4,384,256]{2,1,0:T(8,128)(2,1)S(1)}, f16[4,384,256]{2,1,0:T(8,128)(2,1)S(1)}, u32[]{:S(2)}, u32[]{:S(2)}) collective-permute-start(f16[4,384,256]{2,1,0:T(8,128)(2,1)S(1)} %get-tuple-element.123), channel_id=1, source_target_pairs={{2,4},{3,5},{4,2},{5,3},{10,12},{11,13},{12,10},{13,11},{18,20},{1... | collective-permute-start | bytes 2359304 | tf_op jit(solution)/shard_map/ppermute | solution.py:41
  85.2 20.0 %collective-permute-start.22 = (bf16[4,384,256]{2,1,0:T(8,128)(2,1)S(1)}, bf16[4,384,256]{2,1,0:T(8,128)(2,1)S(1)}, u32[]{:S(2)}, u32[]{:S(2)}) collective-permute-start(bf16[4,384,256]{2,1,0:T(8,128)(2,1)S(1)} %collective-permute-done.18.refs_2_), channel_id=1, source_target_pairs={{2,0},{3,1},{4,6},{5,7},{10,8},{11,9},{12,14},{13,15},{18,16},{19,... | collective-permute-start | bytes 2359304 | tf_op jit(solution)/shard_map/ppermute | solution.py:41
  86.5 18.7 %collective-permute-start.25 = (bf16[3,2,256,256]{3,2,1,0:T(8,128)(2,1)S(1)}, bf16[3,2,256,256]{3,2,1,0:T(8,128)(2,1)S(1)}, u32[]{:S(2)}, u32[]{:S(2)}) collective-permute-start(bf16[3,2,256,256]{3,2,1,0:T(8,128)(2,1)S(1)} %pad_maximum_fusion.refs_10_.refs_14_.refs_18_), channel_id=1, source_target_pairs={{0,8},{8,0},{16,24},{24,16},{1,9},{9,1},{17,25},{25,17},{2,10},{10... | collective-permute-start | bytes 2359304 | tf_op jit(solution)/shard_map/ppermute | solution.py:45
  86.5 18.6 %collective-permute-start.26 = (bf16[3,2,256,256]{3,2,1,0:T(8,128)(2,1)S(1)}, bf16[3,2,256,256]{3,2,1,0:T(8,128)(2,1)S(1)}, u32[]{:S(2)}, u32[]{:S(2)}) collective-permute-start(bf16[3,2,256,256]{3,2,1,0:T(8,128)(2,1)S(1)} %collective-permute-done.19.refs_11_.refs_15_.refs_19_), channel_id=1, source_target_pairs={{0,8},{8,0},{16,24},{24,16},{1,9},{9,1},{17,25},{25,17},{2,10},{10... | collective-permute-start | bytes 2359304 | tf_op jit(solution)/shard_map/ppermute | solution.py:45
  105.2 17.2 %collective-permute-start.23 = (f16[4,384,256]{2,1,0:T(8,128)(2,1)S(1)}, f16[4,384,256]{2,1,0:T(8,128)(2,1)S(1)}, u32[]{:S(2)}, u32[]{:S(2)}) collective-permute-start(f16[4,384,256]{2,1,0:T(8,128)(2,1)S(1)} %multiply_convert_fusion.1), channel_id=1, source_target_pairs={{0,2},{1,3},{2,0},{3,1},{4,6},{5,7},{6,4},{7,5},{8,10},{9,11},{10,... | collective-permute-start | bytes 2359304 | tf_op jit(solution)/shard_map/ppermute | solution.py:41
  107.7 17.3 %collective-permute-start.27 = (f16[4,384,256]{2,1,0:T(8,128)(2,1)S(1)}, f16[4,384,256]{2,1,0:T(8,128)(2,1)S(1)}, u32[]{:S(2)}, u32[]{:S(2)}) collective-permute-start(f16[4,384,256]{2,1,0:T(8,128)(2,1)S(1)} %multiply_convert_fusion), channel_id=1, source_target_pairs={{0,1},{1,0},{2,3},{3,2},{4,5},{5,4},{6,7},{7,6},{8,9},{9,8},{10,11... | collective-permute-start | bytes 2359304 | tf_op jit(solution)/shard_map/ppermute | solution.py:41
  109.3 15.9 %collective-permute-start.24 = (f16[4,384,256]{2,1,0:T(8,128)(2,1)S(1)}, f16[4,384,256]{2,1,0:T(8,128)(2,1)S(1)}, u32[]{:S(2)}, u32[]{:S(2)}) collective-permute-start(f16[4,384,256]{2,1,0:T(8,128)(2,1)S(1)} %multiply_convert_fusion.3), channel_id=1, source_target_pairs={{2,4},{3,5},{4,2},{5,3},{10,12},{11,13},{12,10},{13,11},{18,20},{1... | collective-permute-start | bytes 2359304 | tf_op jit(solution)/shard_map/ppermute | solution.py:41
  125.1 1.9 %copy-start.1 = (f32[8,3,128,2,128]{4,3,2,1,0:T(2,128)S(1)}, f32[8,3,128,2,128]{4,3,2,1,0:T(2,128)}, u32[]{:S(2)}) copy-start(f32[8,3,128,2,128]{4,3,2,1,0:T(2,128)} %param.5) | copy-start | bytes 9437188

commit v5 on v4

--- a/solution.py
+++ b/solution.py
@@ -7,7 +7,6 @@
 
 BF16, F16, F32 = jnp.bfloat16, jnp.float16, jnp.float32
 WIRE = 32.0
-LONG = 48 * 2**20
 PARAMS = pltpu.CompilerParams(vmem_limit_bytes=32 * 2**20)
 
 
@@ -57,7 +56,7 @@
     return lax.optimization_barrier((x, *others))[0]
 
 
-def call(body, place, grid, ins, outs, shapes, operands, scratch=(), cost=0, **more):
+def call(body, place, grid, ins, outs, shapes, operands, scratch=(), **more):
     return pl.pallas_call(
         body,
         grid_spec=pltpu.PrefetchScalarGridSpec(
@@ -65,7 +64,7 @@
         ),
         out_shape=shapes,
         compiler_params=PARAMS,
-        cost_estimate=pl.CostEstimate(flops=0, bytes_accessed=cost, transcendentals=0),
+        cost_estimate=pl.CostEstimate(flops=0, bytes_accessed=0, transcendentals=0),
         **more,
     )(place, *operands)
 
@@ -110,11 +109,7 @@
     )
 
 
-def across(m):
-    return (0, 2, 1, 3)[m]
-
-
-def parts(place, lefts, rights, steps, cost=0):
+def parts(place, lefts, rights, steps):
     irreps, rows, kk = lefts[0].shape
     wide = rights[0][0].shape[-1]
     flat = [b for source in rights for b in source]
@@ -142,7 +137,6 @@
         [pl.BlockSpec((1, rows, wide), irrep_of)] * len(steps),
         [jax.ShapeDtypeStruct((irreps, rows, wide), F32)] * len(steps),
         [*lefts, *(flat * len(steps))],
-        cost=cost,
     )
 
 
@@ -183,21 +177,25 @@
     )
 
 
-def add_all(place, residual, even, odd):
+def add_half(place, residual, cycle, parity, result=None):
     irreps, double, lanes = residual.shape
     rows = double // 2
 
-    def body(_, res_ref, even_ref, odd_ref, out):
-        for n, add_ref in enumerate((even_ref, odd_ref)):
-            for b in range(2):
-                spot = pl.ds(b, rows, stride=2)
-                out[n, spot, :] = res_ref[n, spot, :] + add_ref[0, :, b * lanes : (b + 1) * lanes]
-
-    pair = pl.BlockSpec((2, double, lanes), lambda i, _: (i, 0, 0))
-    half = pl.BlockSpec((1, rows, 2 * lanes), lambda i, _: (i, 0, 0))
-    return call(
-        body, place, (irreps // 2,), [pair, half, half], pair,
-        jax.ShapeDtypeStruct(residual.shape, F32), [residual, even, odd],
+    def body(_, res_ref, add_ref, *refs):
+        out = refs[-1]
+        for b in range(2):
+            place = pl.ds(b, rows, stride=2)
+            out[0, place, :] = res_ref[0, place, :] + add_ref[0, :, b * lanes : (b + 1) * lanes]
+
+    mine = pl.BlockSpec((1, double, lanes), lambda i, _: (2 * i + parity, 0, 0))
+    given = [] if result is None else [result]
+    return call(
+        body, place, (irreps // 2,),
+        [mine, pl.BlockSpec((1, rows, 2 * lanes), lambda i, _: (i, 0, 0))] + [pl.BlockSpec(memory_space=pl.ANY)] * len(given),
+        mine,
+        jax.ShapeDtypeStruct(residual.shape, F32),
+        [residual, cycle, *given],
+        input_output_aliases={3: 0} if given else {},
     )
 
 
@@ -224,21 +222,19 @@
     pieces, g1, g3_mid, x_own, b_in, b_own = hold((pieces, g1, g3_mid, x_own, b_in, b_own))
 
     x_in = row(b_in, SWAP_X)
-    a_in = col(after(a_even, b_in), SWAP_Y)
-    swapped = [row(b, SWAP_CORE) for b in (b_own, x_own, b_in, pieces[0])]
+    a_in = col(a_even, SWAP_Y)
+    swapped = [row(b, SWAP_CORE) for b in (b_own, x_own)]
     pieces, swapped = hold((pieces, swapped))
     got = [col(pieces[d], XOR_Z[d]) for d in (3, 2, 1)]
     piece_x = row(pieces[0], SWAP_X)
     x_in, got, a_in, piece_x = hold((x_in, got, a_in, piece_x))
-
-    swapped += [row(x_in, SWAP_CORE), row(piece_x, SWAP_CORE)]
+    swapped += [row(b, SWAP_CORE) for b in (b_in, pieces[0], x_in, piece_x)]
     a_in, got, swapped = hold((a_in, got, swapped))
     b_rows = [[b_own, x_own, swapped[0], swapped[1]], [b_in, x_in, swapped[2], swapped[4]]]
     piece_rows = [b[None] for b in (pieces[0], piece_x, swapped[3], swapped[5])]
 
     (p3,) = parts(place, [a_even, a_in], b_rows, [3])
     wire3 = (p3 * WIRE).astype(F16)
-
     wire3, g1, g3_mid, got = hold((wire3, g1, g3_mid, got))
     got = jnp.stack([got[2], got[1], got[0]])
     i3 = col(wire3, INWARD)
@@ -251,27 +247,25 @@
     turn2 = ((p2 + from_wire(i3)) * WIRE).astype(F16)
     turn2, p1, g2_mid, got_x, g2_end = hold((turn2, p1, g2_mid, got_x, g2_end))
 
-
     m2 = col(turn2, MIDDLE)
     g3_end = col(g2_mid, OUTWARD)
     got_rows = [got, got_x, row(got, SWAP_CORE), row(got_x, SWAP_CORE)]
-
     terms = [((g,), piece_rows, 0)]
     terms += [(left, got_rows, n) for n, left in enumerate([(g1,), (g2_mid, g2_end), (g3_mid, g3_end)])]
     turn3 = ((p3 + from_wire(i2)) * WIRE).astype(F16)
     turn1 = ((p1 + from_wire(m2)) * WIRE).astype(F16)
-    turn3, turn1, g3_end = hold((turn3, turn1, g3_end))
+    turn3, turn1 = hold((turn3, turn1))
+    g3_end = after(g3_end, turn1, turn3)
 
     s1 = col(turn1, XOR_Z[1])
     m3 = col(turn3, MIDDLE)
     terms[3] = ((g3_mid, g3_end), got_rows, 2)
     q = to_wire(column(place, terms, 1), SWAP_Y)
-    odd = column(place, terms, 0) + from_wire(q)
-    even, m3, odd = hold((p0 + from_wire(s1), m3, odd))
-    even = even + from_wire(m3)
-
+    own = column(place, terms, 0)
+    even = (p0 + from_wire(s1)) + from_wire(m3)
     result = residual_in.reshape(irreps, row_blocks * block * 2, block)
-    done = add_all(place, result, even, odd)
+    done = add_half(place, result, even, 0)
+    done = add_half(place, result, own + from_wire(q), 1, done)
     return done.reshape(residual_in.shape)
 
 

time: 131 us -> 128 us (0.977)
  waiting for transfers between devices: 70.9 us -> 64.4 us
  starting transfers between devices: 35.9 us -> 38.8 us
  Pallas kernels: 15.9 us -> 17.7 us
    ppermute x16, waiting for transfers between devices: 65.1 us -> 61.6 us  [col(): return lax.ppermute(x, 'col', pairs)]
    ppermute x16, starting transfers between devices: 27.7 us -> 31.1 us  [col(): return lax.ppermute(x, 'col', pairs)]
    ppermute x12, waiting for transfers between devices: 5.78 us -> 2.75 us  [row(): return lax.ppermute(x, 'row', pairs)]
    pallas_call x8 -> x9, Pallas kernels: 15.9 us -> 17.7 us  [call(): pl.pallas_call(body, grid_spec=pltpu.PrefetchScalarGridSpec(num_scalar_pr...]
  transfers between devices with their start and end apart: 28 -> 28, of which waited for: 12 -> 11; matrix products, arithmetic and copies ran while one was open for 1% -> 1% of each run, Pallas kernels for 8% -> 10%
where the time goes in v5:
time: 128 us
  waiting for transfers between devices  64.4 us (50%)
  starting transfers between devices  38.8 us (30%)
  Pallas kernels  17.7 us (14%)
  local copies, waits for them, and re-layouts  4.58 us (4%)
  other arithmetic  2.13 us (2%)
    ppermute x16, waiting for transfers between devices, col(): return lax.ppermute(x, 'col', pairs)  61.6 us
    ppermute x16, starting transfers between devices, col(): return lax.ppermute(x, 'col', pairs)  31.1 us
    pallas_call x9, Pallas kernels, call(): pl.pallas_call(body, grid_spec=pltpu.PrefetchScalarGridSpec(num_scalar_pr...  17.7 us
    ppermute x12, starting transfers between devices, row(): return lax.ppermute(x, 'row', pairs)  7.75 us
    unnamed x6, local copies, waits for them, and re-layouts  4.58 us
    ppermute x12, waiting for transfers between devices, row(): return lax.ppermute(x, 'row', pairs)  2.75 us
  transfers between devices with their start and end apart: 28, of which 11 were waited for; matrix products, arithmetic and copies ran while one was open for 1% of the time, Pallas kernels for 10%

profile of v5, /device:TPU:0, one launch (start us, length us, event | category | flops | bytes accessed | tf_op | source)
XLA Modules:
  0.0 127.9 jit_solution(18001068085680681426)
XLA Ops:
  0.1 1.4 %copy-done.2 = bf16[8,3,128,2,128]{4,3,2,1,0:T(2,128)(2,1)S(1)} copy-done((bf16[8,3,128,2,128]{4,3,2,1,0:T(2,128)(2,1)S(1)}, bf16[8,3,128,2,128]{4,3,2,1,0:T(2,128)(2,1)}, u32[]{:S(2)}) %copy-start.2) | copy-done | bytes 1572888
  1.5 1.1 shard_map.37
  2.6 3.1 %collective-permute-start = (bf16[4,384,256]{2,1,0:T(8,128)(2,1)S(1)}, bf16[4,384,256]{2,1,0:T(8,128)(2,1)S(1)}, u32[]{:S(2)}, u32[]{:S(2)}) collective-permute-start(bf16[4,384,256]{2,1,0:T(8,128)(2,1)S(1)} %get-tuple-element.72.refs_0_), channel_id=1, source_target_pairs={{0,2},{1,3},{2,0},{3,1},{4,6},{5,7},{6,4},{7,5},{8,10},{9,11},{10,... | collective-permute-start | bytes 2359304 | tf_op jit(solution)/shard_map/ppermute | solution.py:40
  5.7 1.6 %copy-done.1 = bf16[2,2,128,16,128]{4,3,2,1,0:T(8,128)(2,1)S(1)} copy-done((bf16[2,2,128,16,128]{4,3,2,1,0:T(8,128)(2,1)S(1)}, bf16[2,2,128,16,128]{4,3,2,1,0:T(8,128)(2,1)}, u32[]{:S(2)}) %copy-start.1) | copy-done | bytes 2097176
  7.2 1.5 %shard_map.39 = (bf16[4,256,256]{2,1,0:T(8,128)(2,1)S(1)}, bf16[4,256,256]{2,1,0:T(8,128)(2,1)S(1)}) custom-call(s32[3]{0:T(128)S(1)} %pad_add_fusion._.place_ref, bf16[2,2,128,16,128]{4,3,2,1,0:T(8,128)(2,1)S(1)} %copy-done.1), custom_call_target="tpu_custom_call" | custom-call | tf_op jit(solution)/shard_map/pallas_call | solution.py:60
  8.8 0.7 collective-permute-start.1
  9.5 1.6 %collective-permute-start.3 = (bf16[4,256,256]{2,1,0:T(8,128)(2,1)S(1)}, bf16[4,256,256]{2,1,0:T(8,128)(2,1)S(1)}, u32[]{:S(2)}, u32[]{:S(2)}) collective-permute-start(bf16[4,256,256]{2,1,0:T(8,128)(2,1)S(1)} %get-tuple-element.71), channel_id=1, source_target_pairs={{0,1},{1,0},{2,3},{3,2},{4,5},{5,4},{6,7},{7,6},{8,9},{9,8},{10,11... | collective-permute-start | bytes 1572872 | tf_op jit(solution)/shard_map/ppermute | solution.py:40
  11.1 1.5 %collective-permute-start.2 = (bf16[4,256,256]{2,1,0:T(8,128)(2,1)S(1)}, bf16[4,256,256]{2,1,0:T(8,128)(2,1)S(1)}, u32[]{:S(2)}, u32[]{:S(2)}) collective-permute-start(bf16[4,256,256]{2,1,0:T(8,128)(2,1)S(1)} %get-tuple-element.79.refs_2_.refs_10_.refs_18_), channel_id=1, source_target_pairs={{0,16},{8,24},{16,0},{24,8},{1,17},{9,25},{17,1},{25,9},{2,18},{10... | collective-permute-start | bytes 1572872 | tf_op jit(solution)/shard_map/ppermute | solution.py:44
  12.6 0.5 collective-permute-start.10
  13.1 1.5 %shard_map.38 = (bf16[2,256,256]{2,1,0:T(8,128)(2,1)S(1)}, bf16[2,256,256]{2,1,0:T(8,128)(2,1)S(1)}, bf16[2,256,256]{2,1,0:T(8,128)(2,1)S(1)}, bf16[2,256,256]{2,1,0:T(8,128)(2,1)S(1)}) custom-call(s32[3]{0:T(128)S(1)} %pad_add_fusion._.place_ref, bf16[2,2,128,16,128]{4,3,2,1,0:T(8,128)(2,1)S(1)} %copy-done.1), custom_call_target="tpu_custom_call" | custom-call | tf_op jit(solution)/shard_map/pallas_call | solution.py:60
  14.6 9.8 %collective-permute-done.3.refs_6_.refs_14_.refs_22_ = bf16[4,256,256]{2,1,0:T(8,128)(2,1)S(1)} collective-permute-done((bf16[4,256,256]{2,1,0:T(8,128)(2,1)S(1)}, bf16[4,256,256]{2,1,0:T(8,128)(2,1)S(1)}, u32[]{:S(2)}, u32[]{:S(2)}) %collective-permute-start.3) | collective-permute-done | bytes 524320 | tf_op jit(solution)/shard_map/ppermute | solution.py:40
  24.5 0.5 collective-permute-start.6
  25.0 1.5 %collective-permute-start.4 = (bf16[4,256,256]{2,1,0:T(8,128)(2,1)S(1)}, bf16[4,256,256]{2,1,0:T(8,128)(2,1)S(1)}, u32[]{:S(2)}, u32[]{:S(2)}) collective-permute-start(bf16[4,256,256]{2,1,0:T(8,128)(2,1)S(1)} %collective-permute-done.3.refs_6_.refs_14_.refs_22_), channel_id=1, source_target_pairs={{0,16},{8,24},{16,0},{24,8},{1,17},{9,25},{17,1},{25,9},{2,18},{10... | collective-permute-start | bytes 1572872 | tf_op jit(solution)/shard_map/ppermute | solution.py:44
  26.5 0.7 collective-permute-done.6.refs_5_.refs_13_.refs_21_
  27.1 2.5 %collective-permute-start.7 = (bf16[2,256,256]{2,1,0:T(8,128)(2,1)S(1)}, bf16[2,256,256]{2,1,0:T(8,128)(2,1)S(1)}, u32[]{:S(2)}, u32[]{:S(2)}) collective-permute-start(bf16[2,256,256]{2,1,0:T(8,128)(2,1)S(1)} %get-tuple-element.81), channel_id=1, source_target_pairs={{0,6},{1,7},{2,4},{3,5},{4,2},{5,3},{6,0},{7,1},{8,14},{9,15},{10,... | collective-permute-start | bytes 786440 | tf_op jit(solution)/shard_map/ppermute | solution.py:40
  29.6 5.6 %collective-permute-start.8 = (bf16[2,256,256]{2,1,0:T(8,128)(2,1)S(1)}, bf16[2,256,256]{2,1,0:T(8,128)(2,1)S(1)}, u32[]{:S(2)}, u32[]{:S(2)}) collective-permute-start(bf16[2,256,256]{2,1,0:T(8,128)(2,1)S(1)} %get-tuple-element.82), channel_id=1, source_target_pairs={{0,4},{1,5},{2,6},{3,7},{4,0},{5,1},{6,2},{7,3},{8,12},{9,13},{10,... | collective-permute-start | bytes 786440 | tf_op jit(solution)/shard_map/ppermute | solution.py:40
  35.5 4.3 %collective-permute-done.10.refs_1_ = bf16[4,384,256]{2,1,0:T(8,128)(2,1)S(1)} collective-permute-done((bf16[4,384,256]{2,1,0:T(8,128)(2,1)S(1)}, bf16[4,384,256]{2,1,0:T(8,128)(2,1)S(1)}, u32[]{:S(2)}, u32[]{:S(2)}) %collective-permute-start.10) | collective-permute-done | bytes 786464 | tf_op jit(solution)/shard_map/ppermute | solution.py:40
  39.8 1.5 %collective-permute-start.11 = (bf16[2,256,256]{2,1,0:T(8,128)(2,1)S(1)}, bf16[2,256,256]{2,1,0:T(8,128)(2,1)S(1)}, u32[]{:S(2)}, u32[]{:S(2)}) collective-permute-start(bf16[2,256,256]{2,1,0:T(8,128)(2,1)S(1)} %get-tuple-element.84), channel_id=1, source_target_pairs={{0,16},{8,24},{16,0},{24,8},{1,17},{9,25},{17,1},{25,9},{2,18},{10... | collective-permute-start | bytes 786440 | tf_op jit(solution)/shard_map/ppermute | solution.py:44
  41.3 12.8 %collective-permute-done.8 = bf16[2,256,256]{2,1,0:T(8,128)(2,1)S(1)} collective-permute-done((bf16[2,256,256]{2,1,0:T(8,128)(2,1)S(1)}, bf16[2,256,256]{2,1,0:T(8,128)(2,1)S(1)}, u32[]{:S(2)}, u32[]{:S(2)}) %collective-permute-start.8) | collective-permute-done | bytes 262176 | tf_op jit(solution)/shard_map/ppermute | solution.py:40
  54.2 0.5 collective-permute-start.13
  54.7 1.7 %collective-permute-done.13 = bf16[2,256,256]{2,1,0:T(8,128)(2,1)S(1)} collective-permute-done((bf16[2,256,256]{2,1,0:T(8,128)(2,1)S(1)}, bf16[2,256,256]{2,1,0:T(8,128)(2,1)S(1)}, u32[]{:S(2)}, u32[]{:S(2)}) %collective-permute-start.13) | collective-permute-done | bytes 262176 | tf_op jit(solution)/shard_map/ppermute | solution.py:44
  56.4 0.4 collective-permute-done.15
  56.8 1.7 %shard_map.40 = f32[4,384,256]{2,1,0:T(8,128)S(1)} custom-call(s32[3]{0:T(128)S(1)} %pad_add_fusion._.place_ref, bf16[4,384,256]{2,1,0:T(8,128)(2,1)S(1)} %get-tuple-element.105.refs_0_, bf16[4,384,256]{2,1,0:T(8,128)(2,1)S(1)} %collective-permute-done.10.refs_1_, bf16[4,256,256]{2,1,0:T(8,128)(2,1)S(1)} %get-tuple-element.79.refs_2_.refs_10_.refs_18_, ...), custom_call_target="tpu_custom_call" | custom-call | tf_op jit(solution)/shard_map/pallas_call | solution.py:60
  58.7 1.6 %collective-permute-start.16 = (f16[4,384,256]{2,1,0:T(8,128)(2,1)S(1)}, f16[4,384,256]{2,1,0:T(8,128)(2,1)S(1)}, u32[]{:S(2)}, u32[]{:S(2)}) collective-permute-start(f16[4,384,256]{2,1,0:T(8,128)(2,1)S(1)} %multiply_convert_fusion.5), channel_id=1, source_target_pairs={{0,2},{1,3},{6,4},{7,5},{8,10},{9,11},{14,12},{15,13},{16,18},{17,... | collective-permute-start | bytes 2359304 | tf_op jit(solution)/shard_map/ppermute | solution.py:40
  60.5 1.6 %collective-permute-start.18 = (bf16[3,2,256,256]{3,2,1,0:T(8,128)(2,1)S(1)}, bf16[3,2,256,256]{3,2,1,0:T(8,128)(2,1)S(1)}, u32[]{:S(2)}, u32[]{:S(2)}) collective-permute-start(bf16[3,2,256,256]{3,2,1,0:T(8,128)(2,1)S(1)} %pad_maximum_fusion.refs_10_.refs_14_.refs_18_), channel_id=1, source_target_pairs={{0,16},{8,24},{16,0},{24,8},{1,17},{9,25},{17,1},{25,9},{2,18},{10... | collective-permute-start | bytes 2359304 | tf_op jit(solution)/shard_map/ppermute | solution.py:44
  62.0 0.7 collective-permute-start.17
  62.7 1.3 %collective-permute-start.19 = (bf16[4,384,256]{2,1,0:T(8,128)(2,1)S(1)}, bf16[4,384,256]{2,1,0:T(8,128)(2,1)S(1)}, u32[]{:S(2)}, u32[]{:S(2)}) collective-permute-start(bf16[4,384,256]{2,1,0:T(8,128)(2,1)S(1)} %collective-permute-done.1.refs_4_), channel_id=1, source_target_pairs={{2,0},{3,1},{4,6},{5,7},{10,8},{11,9},{12,14},{13,15},{18,16},{19,... | collective-permute-start | bytes 2359304 | tf_op jit(solution)/shard_map/ppermute | solution.py:40
  64.0 2.7 %shard_map.41 = (f32[4,384,256]{2,1,0:T(8,128)S(1)}, f32[4,384,256]{2,1,0:T(8,128)S(1)}, f32[4,384,256]{2,1,0:T(8,128)S(1)}) custom-call(s32[3]{0:T(128)S(1)} %pad_add_fusion._.place_ref, bf16[4,384,256]{2,1,0:T(8,128)(2,1)S(1)} %get-tuple-element.105.refs_0_, bf16[4,384,256]{2,1,0:T(8,128)(2,1)S(1)} %collective-permute-done.10.refs_1_, ...), custom_call_target="tpu_custom_call" | custom-call | tf_op jit(solution)/shard_map/pallas_call | solution.py:60
  66.8 10.6 %collective-permute-done.16 = f16[4,384,256]{2,1,0:T(8,128)(2,1)S(1)} collective-permute-done((f16[4,384,256]{2,1,0:T(8,128)(2,1)S(1)}, f16[4,384,256]{2,1,0:T(8,128)(2,1)S(1)}, u32[]{:S(2)}, u32[]{:S(2)}) %collective-permute-start.16) | collective-permute-done | bytes 786464 | tf_op jit(solution)/shard_map/ppermute | solution.py:40
  77.4 0.5 multiply_convert_fusion.3
  77.9 4.4 %collective-permute-start.21 = (f16[4,384,256]{2,1,0:T(8,128)(2,1)S(1)}, f16[4,384,256]{2,1,0:T(8,128)(2,1)S(1)}, u32[]{:S(2)}, u32[]{:S(2)}) collective-permute-start(f16[4,384,256]{2,1,0:T(8,128)(2,1)S(1)} %get-tuple-element.123), channel_id=1, source_target_pairs={{0,2},{1,3},{6,4},{7,5},{8,10},{9,11},{14,12},{15,13},{16,18},{17,... | collective-permute-start | bytes 2359304 | tf_op jit(solution)/shard_map/ppermute | solution.py:40
  82.3 1.3 %collective-permute-done.19.refs_3_ = bf16[4,384,256]{2,1,0:T(8,128)(2,1)S(1)} collective-permute-done((bf16[4,384,256]{2,1,0:T(8,128)(2,1)S(1)}, bf16[4,384,256]{2,1,0:T(8,128)(2,1)S(1)}, u32[]{:S(2)}, u32[]{:S(2)}) %collective-permute-start.19) | collective-permute-done | bytes 786464 | tf_op jit(solution)/shard_map/ppermute | solution.py:40
  83.6 0.7 collective-permute-start.22
  84.4 1.3 %collective-permute-start.20 = (bf16[4,384,256]{2,1,0:T(8,128)(2,1)S(1)}, bf16[4,384,256]{2,1,0:T(8,128)(2,1)S(1)}, u32[]{:S(2)}, u32[]{:S(2)}) collective-permute-start(bf16[4,384,256]{2,1,0:T(8,128)(2,1)S(1)} %collective-permute-done.17.refs_2_), channel_id=1, source_target_pairs={{2,0},{3,1},{4,6},{5,7},{10,8},{11,9},{12,14},{13,15},{18,16},{19,... | collective-permute-start | bytes 2359304 | tf_op jit(solution)/shard_map/ppermute | solution.py:40
  85.7 0.5 collective-permute-start.24
  86.2 12.3 %collective-permute-done.21 = f16[4,384,256]{2,1,0:T(8,128)(2,1)S(1)} collective-permute-done((f16[4,384,256]{2,1,0:T(8,128)(2,1)S(1)}, f16[4,384,256]{2,1,0:T(8,128)(2,1)S(1)}, u32[]{:S(2)}, u32[]{:S(2)}) %collective-permute-start.21) | collective-permute-done | bytes 786464 | tf_op jit(solution)/shard_map/ppermute | solution.py:40
  98.5 0.3 multiply_convert_fusion.2
  98.9 0.3 multiply_convert_fusion.1
  99.2 4.5 %collective-permute-start.26 = (f16[4,384,256]{2,1,0:T(8,128)(2,1)S(1)}, f16[4,384,256]{2,1,0:T(8,128)(2,1)S(1)}, u32[]{:S(2)}, u32[]{:S(2)}) collective-permute-start(f16[4,384,256]{2,1,0:T(8,128)(2,1)S(1)} %multiply_convert_fusion.1), channel_id=1, source_target_pairs={{0,2},{1,3},{2,0},{3,1},{4,6},{5,7},{6,4},{7,5},{8,10},{9,11},{10,... | collective-permute-start | bytes 2359304 | tf_op jit(solution)/shard_map/ppermute | solution.py:40
  103.7 0.7 collective-permute-start.27
  104.4 1.7 %collective-permute-done.20.refs_5_ = bf16[4,384,256]{2,1,0:T(8,128)(2,1)S(1)} collective-permute-done((bf16[4,384,256]{2,1,0:T(8,128)(2,1)S(1)}, bf16[4,384,256]{2,1,0:T(8,128)(2,1)S(1)}, u32[]{:S(2)}, u32[]{:S(2)}) %collective-permute-start.20) | collective-permute-done | bytes 786464 | tf_op jit(solution)/shard_map/ppermute | solution.py:40
  106.2 2.3 %shard_map.43 = f32[4,384,256]{2,1,0:T(8,128)S(1)} custom-call(s32[3]{0:T(128)S(1)} %pad_add_fusion._.place_ref, bf16[4,384,256]{2,1,0:T(8,128)(2,1)S(1)} %get-tuple-element.72.refs_0_, bf16[4,384,256]{2,1,0:T(8,128)(2,1)S(1)} %collective-permute-done.refs_1_, bf16[4,384,256]{2,1,0:T(8,128)(2,1)S(1)} %collective-permute-done.17.refs_2_, ...), custom_call_target="tpu_custom_call" | custom-call | tf_op jit(solution)/shard_map/pallas_call | solution.py:60
  108.6 1.6 %collective-permute-start.25 = (f16[4,384,256]{2,1,0:T(8,128)(2,1)S(1)}, f16[4,384,256]{2,1,0:T(8,128)(2,1)S(1)}, u32[]{:S(2)}, u32[]{:S(2)}) collective-permute-start(f16[4,384,256]{2,1,0:T(8,128)(2,1)S(1)} %multiply_convert_fusion), channel_id=1, source_target_pairs={{0,1},{1,0},{2,3},{3,2},{4,5},{5,4},{6,7},{7,6},{8,9},{9,8},{10,11... | collective-permute-start | bytes 2359304 | tf_op jit(solution)/shard_map/ppermute | solution.py:40
  110.2 2.3 %shard_map.42 = f32[4,384,256]{2,1,0:T(8,128)S(1)} custom-call(s32[3]{0:T(128)S(1)} %pad_add_fusion._.place_ref, bf16[4,384,256]{2,1,0:T(8,128)(2,1)S(1)} %get-tuple-element.72.refs_0_, bf16[4,384,256]{2,1,0:T(8,128)(2,1)S(1)} %collective-permute-done.refs_1_, bf16[4,384,256]{2,1,0:T(8,128)(2,1)S(1)} %collective-permute-done.17.refs_2_, ...), custom_call_target="tpu_custom_call" | custom-call | tf_op jit(solution)/shard_map/pallas_call | solution.py:60
  112.5 8.7 %collective-permute-done.26 = f16[4,384,256]{2,1,0:T(8,128)(2,1)S(1)} collective-permute-done((f16[4,384,256]{2,1,0:T(8,128)(2,1)S(1)}, f16[4,384,256]{2,1,0:T(8,128)(2,1)S(1)}, u32[]{:S(2)}, u32[]{:S(2)}) %collective-permute-start.26) | collective-permute-done | bytes 786464 | tf_op jit(solution)/shard_map/ppermute | solution.py:40
  121.5 1.6 %copy-done = f32[8,3,128,2,128]{4,3,2,1,0:T(2,128)S(1)} copy-done((f32[8,3,128,2,128]{4,3,2,1,0:T(2,128)S(1)}, f32[8,3,128,2,128]{4,3,2,1,0:T(2,128)}, u32[]{:S(2)}) %copy-start) | copy-done | bytes 3145752
  123.1 2.3 %shard_map.44.refs_0_ = f32[8,768,128]{2,1,0:T(8,128)} custom-call(s32[3]{0:T(128)S(1)} %pad_add_fusion._.place_ref, f32[8,768,128]{2,1,0:T(8,128)S(1)} %bitcast.13, f32[4,384,256]{2,1,0:T(8,128)S(1)} %multiply_add_fusion.add_ref), custom_call_target="tpu_custom_call" | custom-call | tf_op jit(solution)/shard_map/pallas_call | solution.py:60
  125.6 2.3 %shard_map.45 = f32[8,768,128]{2,1,0:T(8,128)} custom-call(s32[3]{0:T(128)S(1)} %pad_add_fusion._.place_ref, f32[8,768,128]{2,1,0:T(8,128)S(1)} %bitcast.14, f32[4,384,256]{2,1,0:T(8,128)S(1)} %multiply_add_fusion.1.add_ref, f32[8,768,128]{2,1,0:T(8,128)} %shard_map.44.refs_0_), custom_call_target="tpu_custom_call", output_to_operand_aliasing={{}: (3, {})} | custom-call | tf_op jit(solution)/shard_map/pallas_call | solution.py:60
  (32 shorter events, 1.6 us)
Async XLA Ops:
  0.1 1.4 %copy-start.2 = (bf16[8,3,128,2,128]{4,3,2,1,0:T(2,128)(2,1)S(1)}, bf16[8,3,128,2,128]{4,3,2,1,0:T(2,128)(2,1)}, u32[]{:S(2)}) copy-start(bf16[8,3,128,2,128]{4,3,2,1,0:T(2,128)(2,1)} %param.4) | copy-start | bytes 4718596
  2.6 21.9 %collective-permute-start = (bf16[4,384,256]{2,1,0:T(8,128)(2,1)S(1)}, bf16[4,384,256]{2,1,0:T(8,128)(2,1)S(1)}, u32[]{:S(2)}, u32[]{:S(2)}) collective-permute-start(bf16[4,384,256]{2,1,0:T(8,128)(2,1)S(1)} %get-tuple-element.72.refs_0_), channel_id=1, source_target_pairs={{0,2},{1,3},{2,0},{3,1},{4,6},{5,7},{6,4},{7,5},{8,10},{9,11},{10,... | collective-permute-start | bytes 2359304 | tf_op jit(solution)/shard_map/ppermute | solution.py:40
  5.7 1.6 %copy-start.1 = (bf16[2,2,128,16,128]{4,3,2,1,0:T(8,128)(2,1)S(1)}, bf16[2,2,128,16,128]{4,3,2,1,0:T(8,128)(2,1)}, u32[]{:S(2)}) copy-start(bf16[2,2,128,16,128]{4,3,2,1,0:T(8,128)(2,1)} %in_ref.1) | copy-start | bytes 6291460
  8.8 15.6 %collective-permute-start.1 = (bf16[4,384,256]{2,1,0:T(8,128)(2,1)S(1)}, bf16[4,384,256]{2,1,0:T(8,128)(2,1)S(1)}, u32[]{:S(2)}, u32[]{:S(2)}) collective-permute-start(bf16[4,384,256]{2,1,0:T(8,128)(2,1)S(1)} %get-tuple-element.72.refs_0_), channel_id=1, source_target_pairs={{2,4},{3,5},{4,2},{5,3},{10,12},{11,13},{12,10},{13,11},{18,20},{1... | collective-permute-start | bytes 2359304 | tf_op jit(solution)/shard_map/ppermute | solution.py:40
  9.5 14.9 %collective-permute-start.3 = (bf16[4,256,256]{2,1,0:T(8,128)(2,1)S(1)}, bf16[4,256,256]{2,1,0:T(8,128)(2,1)S(1)}, u32[]{:S(2)}, u32[]{:S(2)}) collective-permute-start(bf16[4,256,256]{2,1,0:T(8,128)(2,1)S(1)} %get-tuple-element.71), channel_id=1, source_target_pairs={{0,1},{1,0},{2,3},{3,2},{4,5},{5,4},{6,7},{7,6},{8,9},{9,8},{10,11... | collective-permute-start | bytes 1572872 | tf_op jit(solution)/shard_map/ppermute | solution.py:40
  11.1 13.3 %collective-permute-start.2 = (bf16[4,256,256]{2,1,0:T(8,128)(2,1)S(1)}, bf16[4,256,256]{2,1,0:T(8,128)(2,1)S(1)}, u32[]{:S(2)}, u32[]{:S(2)}) collective-permute-start(bf16[4,256,256]{2,1,0:T(8,128)(2,1)S(1)} %get-tuple-element.79.refs_2_.refs_10_.refs_18_), channel_id=1, source_target_pairs={{0,16},{8,24},{16,0},{24,8},{1,17},{9,25},{17,1},{25,9},{2,18},{10... | collective-permute-start | bytes 1572872 | tf_op jit(solution)/shard_map/ppermute | solution.py:44
  12.6 27.2 %collective-permute-start.10 = (bf16[4,384,256]{2,1,0:T(8,128)(2,1)S(1)}, bf16[4,384,256]{2,1,0:T(8,128)(2,1)S(1)}, u32[]{:S(2)}, u32[]{:S(2)}) collective-permute-start(bf16[4,384,256]{2,1,0:T(8,128)(2,1)S(1)} %get-tuple-element.105.refs_0_), channel_id=1, source_target_pairs={{0,1},{1,0},{2,3},{3,2},{4,5},{5,4},{6,7},{7,6},{8,9},{9,8},{10,11... | collective-permute-start | bytes 2359304 | tf_op jit(solution)/shard_map/ppermute | solution.py:40
  24.4 2.1 %collective-permute-start.5 = (bf16[4,256,256]{2,1,0:T(8,128)(2,1)S(1)}, bf16[4,256,256]{2,1,0:T(8,128)(2,1)S(1)}, u32[]{:S(2)}, u32[]{:S(2)}) collective-permute-start(bf16[4,256,256]{2,1,0:T(8,128)(2,1)S(1)} %get-tuple-element.79.refs_2_.refs_10_.refs_18_), channel_id=1, source_target_pairs={{0,8},{8,0},{16,24},{24,16},{1,9},{9,1},{17,25},{25,17},{2,10},{10... | collective-permute-start | bytes 1572872 | tf_op jit(solution)/shard_map/ppermute | solution.py:44
  24.5 2.6 %collective-permute-start.6 = (bf16[4,256,256]{2,1,0:T(8,128)(2,1)S(1)}, bf16[4,256,256]{2,1,0:T(8,128)(2,1)S(1)}, u32[]{:S(2)}, u32[]{:S(2)}) collective-permute-start(bf16[4,256,256]{2,1,0:T(8,128)(2,1)S(1)} %collective-permute-done.2.refs_3_.refs_11_.refs_19_), channel_id=1, source_target_pairs={{0,8},{8,0},{16,24},{24,16},{1,9},{9,1},{17,25},{25,17},{2,10},{10... | collective-permute-start | bytes 1572872 | tf_op jit(solution)/shard_map/ppermute | solution.py:44
  25.0 16.3 %collective-permute-start.4 = (bf16[4,256,256]{2,1,0:T(8,128)(2,1)S(1)}, bf16[4,256,256]{2,1,0:T(8,128)(2,1)S(1)}, u32[]{:S(2)}, u32[]{:S(2)}) collective-permute-start(bf16[4,256,256]{2,1,0:T(8,128)(2,1)S(1)} %collective-permute-done.3.refs_6_.refs_14_.refs_22_), channel_id=1, source_target_pairs={{0,16},{8,24},{16,0},{24,8},{1,17},{9,25},{17,1},{25,9},{2,18},{10... | collective-permute-start | bytes 1572872 | tf_op jit(solution)/shard_map/ppermute | solution.py:44
  27.1 14.2 %collective-permute-start.7 = (bf16[2,256,256]{2,1,0:T(8,128)(2,1)S(1)}, bf16[2,256,256]{2,1,0:T(8,128)(2,1)S(1)}, u32[]{:S(2)}, u32[]{:S(2)}) collective-permute-start(bf16[2,256,256]{2,1,0:T(8,128)(2,1)S(1)} %get-tuple-element.81), channel_id=1, source_target_pairs={{0,6},{1,7},{2,4},{3,5},{4,2},{5,3},{6,0},{7,1},{8,14},{9,15},{10,... | collective-permute-start | bytes 786440 | tf_op jit(solution)/shard_map/ppermute | solution.py:40
  29.6 24.5 %collective-permute-start.8 = (bf16[2,256,256]{2,1,0:T(8,128)(2,1)S(1)}, bf16[2,256,256]{2,1,0:T(8,128)(2,1)S(1)}, u32[]{:S(2)}, u32[]{:S(2)}) collective-permute-start(bf16[2,256,256]{2,1,0:T(8,128)(2,1)S(1)} %get-tuple-element.82), channel_id=1, source_target_pairs={{0,4},{1,5},{2,6},{3,7},{4,0},{5,1},{6,2},{7,3},{8,12},{9,13},{10,... | collective-permute-start | bytes 786440 | tf_op jit(solution)/shard_map/ppermute | solution.py:40
  35.2 18.9 %collective-permute-start.9 = (bf16[2,256,256]{2,1,0:T(8,128)(2,1)S(1)}, bf16[2,256,256]{2,1,0:T(8,128)(2,1)S(1)}, u32[]{:S(2)}, u32[]{:S(2)}) collective-permute-start(bf16[2,256,256]{2,1,0:T(8,128)(2,1)S(1)} %get-tuple-element.83), channel_id=1, source_target_pairs={{0,2},{1,3},{2,0},{3,1},{4,6},{5,7},{6,4},{7,5},{8,10},{9,11},{10,... | collective-permute-start | bytes 786440 | tf_op jit(solution)/shard_map/ppermute | solution.py:40
  39.8 14.4 %collective-permute-start.11 = (bf16[2,256,256]{2,1,0:T(8,128)(2,1)S(1)}, bf16[2,256,256]{2,1,0:T(8,128)(2,1)S(1)}, u32[]{:S(2)}, u32[]{:S(2)}) collective-permute-start(bf16[2,256,256]{2,1,0:T(8,128)(2,1)S(1)} %get-tuple-element.84), channel_id=1, source_target_pairs={{0,16},{8,24},{16,0},{24,8},{1,17},{9,25},{17,1},{25,9},{2,18},{10... | collective-permute-start | bytes 786440 | tf_op jit(solution)/shard_map/ppermute | solution.py:44
  41.3 13.4 %collective-permute-start.12 = (bf16[4,256,256]{2,1,0:T(8,128)(2,1)S(1)}, bf16[4,256,256]{2,1,0:T(8,128)(2,1)S(1)}, u32[]{:S(2)}, u32[]{:S(2)}) collective-permute-start(bf16[4,256,256]{2,1,0:T(8,128)(2,1)S(1)} %collective-permute-done.3.refs_6_.refs_14_.refs_22_), channel_id=1, source_target_pairs={{0,8},{8,0},{16,24},{24,16},{1,9},{9,1},{17,25},{25,17},{2,10},{10... | collective-permute-start | bytes 1572872 | tf_op jit(solution)/shard_map/ppermute | solution.py:44
  54.2 2.7 %collective-permute-start.14 = (bf16[4,256,256]{2,1,0:T(8,128)(2,1)S(1)}, bf16[4,256,256]{2,1,0:T(8,128)(2,1)S(1)}, u32[]{:S(2)}, u32[]{:S(2)}) collective-permute-start(bf16[4,256,256]{2,1,0:T(8,128)(2,1)S(1)} %collective-permute-done.4.refs_7_.refs_15_.refs_23_), channel_id=1, source_target_pairs={{0,8},{8,0},{16,24},{24,16},{1,9},{9,1},{17,25},{25,17},{2,10},{10... | collective-permute-start | bytes 1572872 | tf_op jit(solution)/shard_map/ppermute | solution.py:44
  54.2 2.3 %collective-permute-start.13 = (bf16[2,256,256]{2,1,0:T(8,128)(2,1)S(1)}, bf16[2,256,256]{2,1,0:T(8,128)(2,1)S(1)}, u32[]{:S(2)}, u32[]{:S(2)}) collective-permute-start(bf16[2,256,256]{2,1,0:T(8,128)(2,1)S(1)} %get-tuple-element.84), channel_id=1, source_target_pairs={{0,8},{8,0},{16,24},{24,16},{1,9},{9,1},{17,25},{25,17},{2,10},{10... | collective-permute-start | bytes 786440 | tf_op jit(solution)/shard_map/ppermute | solution.py:44
  54.7 2.1 %collective-permute-start.15 = (bf16[2,256,256]{2,1,0:T(8,128)(2,1)S(1)}, bf16[2,256,256]{2,1,0:T(8,128)(2,1)S(1)}, u32[]{:S(2)}, u32[]{:S(2)}) collective-permute-start(bf16[2,256,256]{2,1,0:T(8,128)(2,1)S(1)} %collective-permute-done.11), channel_id=1, source_target_pairs={{0,8},{8,0},{16,24},{24,16},{1,9},{9,1},{17,25},{25,17},{2,10},{10... | collective-permute-start | bytes 786440 | tf_op jit(solution)/shard_map/ppermute | solution.py:44
  58.7 18.7 %collective-permute-start.16 = (f16[4,384,256]{2,1,0:T(8,128)(2,1)S(1)}, f16[4,384,256]{2,1,0:T(8,128)(2,1)S(1)}, u32[]{:S(2)}, u32[]{:S(2)}) collective-permute-start(f16[4,384,256]{2,1,0:T(8,128)(2,1)S(1)} %multiply_convert_fusion.5), channel_id=1, source_target_pairs={{0,2},{1,3},{6,4},{7,5},{8,10},{9,11},{14,12},{15,13},{16,18},{17,... | collective-permute-start | bytes 2359304 | tf_op jit(solution)/shard_map/ppermute | solution.py:40
  60.5 21.9 %collective-permute-start.18 = (bf16[3,2,256,256]{3,2,1,0:T(8,128)(2,1)S(1)}, bf16[3,2,256,256]{3,2,1,0:T(8,128)(2,1)S(1)}, u32[]{:S(2)}, u32[]{:S(2)}) collective-permute-start(bf16[3,2,256,256]{3,2,1,0:T(8,128)(2,1)S(1)} %pad_maximum_fusion.refs_10_.refs_14_.refs_18_), channel_id=1, source_target_pairs={{0,16},{8,24},{16,0},{24,8},{1,17},{9,25},{17,1},{25,9},{2,18},{10... | collective-permute-start | bytes 2359304 | tf_op jit(solution)/shard_map/ppermute | solution.py:44
  62.0 20.3 %collective-permute-start.17 = (bf16[4,384,256]{2,1,0:T(8,128)(2,1)S(1)}, bf16[4,384,256]{2,1,0:T(8,128)(2,1)S(1)}, u32[]{:S(2)}, u32[]{:S(2)}) collective-permute-start(bf16[4,384,256]{2,1,0:T(8,128)(2,1)S(1)} %collective-permute-done.refs_1_), channel_id=1, source_target_pairs={{2,4},{3,5},{4,2},{5,3},{10,12},{11,13},{12,10},{13,11},{18,20},{1... | collective-permute-start | bytes 2359304 | tf_op jit(solution)/shard_map/ppermute | solution.py:40
  62.7 20.9 %collective-permute-start.19 = (bf16[4,384,256]{2,1,0:T(8,128)(2,1)S(1)}, bf16[4,384,256]{2,1,0:T(8,128)(2,1)S(1)}, u32[]{:S(2)}, u32[]{:S(2)}) collective-permute-start(bf16[4,384,256]{2,1,0:T(8,128)(2,1)S(1)} %collective-permute-done.1.refs_4_), channel_id=1, source_target_pairs={{2,0},{3,1},{4,6},{5,7},{10,8},{11,9},{12,14},{13,15},{18,16},{19,... | collective-permute-start | bytes 2359304 | tf_op jit(solution)/shard_map/ppermute | solution.py:40
  77.9 20.6 %collective-permute-start.21 = (f16[4,384,256]{2,1,0:T(8,128)(2,1)S(1)}, f16[4,384,256]{2,1,0:T(8,128)(2,1)S(1)}, u32[]{:S(2)}, u32[]{:S(2)}) collective-permute-start(f16[4,384,256]{2,1,0:T(8,128)(2,1)S(1)} %get-tuple-element.123), channel_id=1, source_target_pairs={{0,2},{1,3},{6,4},{7,5},{8,10},{9,11},{14,12},{15,13},{16,18},{17,... | collective-permute-start | bytes 2359304 | tf_op jit(solution)/shard_map/ppermute | solution.py:40
  83.6 15.2 %collective-permute-start.22 = (f16[4,384,256]{2,1,0:T(8,128)(2,1)S(1)}, f16[4,384,256]{2,1,0:T(8,128)(2,1)S(1)}, u32[]{:S(2)}, u32[]{:S(2)}) collective-permute-start(f16[4,384,256]{2,1,0:T(8,128)(2,1)S(1)} %get-tuple-element.115), channel_id=1, source_target_pairs={{2,4},{3,5},{4,2},{5,3},{10,12},{11,13},{12,10},{13,11},{18,20},{1... | collective-permute-start | bytes 2359304 | tf_op jit(solution)/shard_map/ppermute | solution.py:40
  84.4 21.8 %collective-permute-start.20 = (bf16[4,384,256]{2,1,0:T(8,128)(2,1)S(1)}, bf16[4,384,256]{2,1,0:T(8,128)(2,1)S(1)}, u32[]{:S(2)}, u32[]{:S(2)}) collective-permute-start(bf16[4,384,256]{2,1,0:T(8,128)(2,1)S(1)} %collective-permute-done.17.refs_2_), channel_id=1, source_target_pairs={{2,0},{3,1},{4,6},{5,7},{10,8},{11,9},{12,14},{13,15},{18,16},{19,... | collective-permute-start | bytes 2359304 | tf_op jit(solution)/shard_map/ppermute | solution.py:40
  85.7 20.5 %collective-permute-start.23 = (bf16[3,2,256,256]{3,2,1,0:T(8,128)(2,1)S(1)}, bf16[3,2,256,256]{3,2,1,0:T(8,128)(2,1)S(1)}, u32[]{:S(2)}, u32[]{:S(2)}) collective-permute-start(bf16[3,2,256,256]{3,2,1,0:T(8,128)(2,1)S(1)} %pad_maximum_fusion.refs_10_.refs_14_.refs_18_), channel_id=1, source_target_pairs={{0,8},{8,0},{16,24},{24,16},{1,9},{9,1},{17,25},{25,17},{2,10},{10... | collective-permute-start | bytes 2359304 | tf_op jit(solution)/shard_map/ppermute | solution.py:44
  85.7 20.4 %collective-permute-start.24 = (bf16[3,2,256,256]{3,2,1,0:T(8,128)(2,1)S(1)}, bf16[3,2,256,256]{3,2,1,0:T(8,128)(2,1)S(1)}, u32[]{:S(2)}, u32[]{:S(2)}) collective-permute-start(bf16[3,2,256,256]{3,2,1,0:T(8,128)(2,1)S(1)} %collective-permute-done.18.refs_11_.refs_15_.refs_19_), channel_id=1, source_target_pairs={{0,8},{8,0},{16,24},{24,16},{1,9},{9,1},{17,25},{25,17},{2,10},{10... | collective-permute-start | bytes 2359304 | tf_op jit(solution)/shard_map/ppermute | solution.py:44
  99.2 22.0 %collective-permute-start.26 = (f16[4,384,256]{2,1,0:T(8,128)(2,1)S(1)}, f16[4,384,256]{2,1,0:T(8,128)(2,1)S(1)}, u32[]{:S(2)}, u32[]{:S(2)}) collective-permute-start(f16[4,384,256]{2,1,0:T(8,128)(2,1)S(1)} %multiply_convert_fusion.1), channel_id=1, source_target_pairs={{0,2},{1,3},{2,0},{3,1},{4,6},{5,7},{6,4},{7,5},{8,10},{9,11},{10,... | collective-permute-start | bytes 2359304 | tf_op jit(solution)/shard_map/ppermute | solution.py:40
  103.7 17.5 %collective-permute-start.27 = (f16[4,384,256]{2,1,0:T(8,128)(2,1)S(1)}, f16[4,384,256]{2,1,0:T(8,128)(2,1)S(1)}, u32[]{:S(2)}, u32[]{:S(2)}) collective-permute-start(f16[4,384,256]{2,1,0:T(8,128)(2,1)S(1)} %multiply_convert_fusion.2), channel_id=1, source_target_pairs={{2,4},{3,5},{4,2},{5,3},{10,12},{11,13},{12,10},{13,11},{18,20},{1... | collective-permute-start | bytes 2359304 | tf_op jit(solution)/shard_map/ppermute | solution.py:40
  108.6 16.8 %collective-permute-start.25 = (f16[4,384,256]{2,1,0:T(8,128)(2,1)S(1)}, f16[4,384,256]{2,1,0:T(8,128)(2,1)S(1)}, u32[]{:S(2)}, u32[]{:S(2)}) collective-permute-start(f16[4,384,256]{2,1,0:T(8,128)(2,1)S(1)} %multiply_convert_fusion), channel_id=1, source_target_pairs={{0,1},{1,0},{2,3},{3,2},{4,5},{5,4},{6,7},{7,6},{8,9},{9,8},{10,11... | collective-permute-start | bytes 2359304 | tf_op jit(solution)/shard_map/ppermute | solution.py:40
  121.2 1.9 %copy-start = (f32[8,3,128,2,128]{4,3,2,1,0:T(2,128)S(1)}, f32[8,3,128,2,128]{4,3,2,1,0:T(2,128)}, u32[]{:S(2)}) copy-start(f32[8,3,128,2,128]{4,3,2,1,0:T(2,128)} %param.5) | copy-start | bytes 9437188

commit v6 on v5

--- a/solution.py
+++ b/solution.py
@@ -225,7 +225,7 @@
     a_in = col(a_even, SWAP_Y)
     swapped = [row(b, SWAP_CORE) for b in (b_own, x_own)]
     pieces, swapped = hold((pieces, swapped))
-    got = [col(pieces[d], XOR_Z[d]) for d in (3, 2, 1)]
+    got = [col(pieces[d], XOR_Z[d]) for d in (3, 1, 2)]
     piece_x = row(pieces[0], SWAP_X)
     x_in, got, a_in, piece_x = hold((x_in, got, a_in, piece_x))
     swapped += [row(b, SWAP_CORE) for b in (b_in, pieces[0], x_in, piece_x)]
@@ -236,7 +236,7 @@
     (p3,) = parts(place, [a_even, a_in], b_rows, [3])
     wire3 = (p3 * WIRE).astype(F16)
     wire3, g1, g3_mid, got = hold((wire3, g1, g3_mid, got))
-    got = jnp.stack([got[2], got[1], got[0]])
+    got = jnp.stack([got[1], got[2], got[0]])
     i3 = col(wire3, INWARD)
     g2_end = col(g3_mid, OUTWARD)
     g2_mid = col(g1, MIDDLE)

time: 128 us -> 128 us (level)
  transfers between devices with their start and end apart: 28 -> 28, of which waited for: 11 -> 12; matrix products, arithmetic and copies ran while one was open for 1% -> 1% of each run, Pallas kernels for 10% -> 10%
where the time goes in v6:
time: 128 us
  waiting for transfers between devices  64.4 us (50%)
  starting transfers between devices  38.8 us (30%)
  Pallas kernels  17.7 us (14%)
  local copies, waits for them, and re-layouts  4.58 us (4%)
  other arithmetic  2.13 us (2%)
    ppermute x16, waiting for transfers between devices, col(): return lax.ppermute(x, 'col', pairs)  61.6 us
    ppermute x16, starting transfers between devices, col(): return lax.ppermute(x, 'col', pairs)  31.1 us
    pallas_call x9, Pallas kernels, call(): pl.pallas_call(body, grid_spec=pltpu.PrefetchScalarGridSpec(num_scalar_pr...  17.7 us
    ppermute x12, starting transfers between devices, row(): return lax.ppermute(x, 'row', pairs)  7.71 us
    unnamed x6, local copies, waits for them, and re-layouts  4.58 us
    ppermute x12, waiting for transfers between devices, row(): return lax.ppermute(x, 'row', pairs)  2.79 us
  transfers between devices with their start and end apart: 28, of which 12 were waited for; matrix products, arithmetic and copies ran while one was open for 1% of the time, Pallas kernels for 10%

profile of v6, /device:TPU:0, one launch (start us, length us, event | category | flops | bytes accessed | tf_op | source)
XLA Modules:
  0.0 127.9 jit_solution(4205969088958952048)
XLA Ops:
  0.1 1.4 %copy-done.2 = bf16[8,3,128,2,128]{4,3,2,1,0:T(2,128)(2,1)S(1)} copy-done((bf16[8,3,128,2,128]{4,3,2,1,0:T(2,128)(2,1)S(1)}, bf16[8,3,128,2,128]{4,3,2,1,0:T(2,128)(2,1)}, u32[]{:S(2)}) %copy-start.2) | copy-done | bytes 1572888
  1.5 1.1 shard_map.37
  2.6 3.1 %collective-permute-start = (bf16[4,384,256]{2,1,0:T(8,128)(2,1)S(1)}, bf16[4,384,256]{2,1,0:T(8,128)(2,1)S(1)}, u32[]{:S(2)}, u32[]{:S(2)}) collective-permute-start(bf16[4,384,256]{2,1,0:T(8,128)(2,1)S(1)} %get-tuple-element.72.refs_0_), channel_id=1, source_target_pairs={{0,2},{1,3},{2,0},{3,1},{4,6},{5,7},{6,4},{7,5},{8,10},{9,11},{10,... | collective-permute-start | bytes 2359304 | tf_op jit(solution)/shard_map/ppermute | solution.py:40
  5.7 1.6 %copy-done.1 = bf16[2,2,128,16,128]{4,3,2,1,0:T(8,128)(2,1)S(1)} copy-done((bf16[2,2,128,16,128]{4,3,2,1,0:T(8,128)(2,1)S(1)}, bf16[2,2,128,16,128]{4,3,2,1,0:T(8,128)(2,1)}, u32[]{:S(2)}) %copy-start.1) | copy-done | bytes 2097176
  7.2 1.5 %shard_map.39 = (bf16[4,256,256]{2,1,0:T(8,128)(2,1)S(1)}, bf16[4,256,256]{2,1,0:T(8,128)(2,1)S(1)}) custom-call(s32[3]{0:T(128)S(1)} %pad_add_fusion._.place_ref, bf16[2,2,128,16,128]{4,3,2,1,0:T(8,128)(2,1)S(1)} %copy-done.1), custom_call_target="tpu_custom_call" | custom-call | tf_op jit(solution)/shard_map/pallas_call | solution.py:60
  8.8 0.7 collective-permute-start.1
  9.5 1.6 %collective-permute-start.3 = (bf16[4,256,256]{2,1,0:T(8,128)(2,1)S(1)}, bf16[4,256,256]{2,1,0:T(8,128)(2,1)S(1)}, u32[]{:S(2)}, u32[]{:S(2)}) collective-permute-start(bf16[4,256,256]{2,1,0:T(8,128)(2,1)S(1)} %get-tuple-element.71), channel_id=1, source_target_pairs={{0,1},{1,0},{2,3},{3,2},{4,5},{5,4},{6,7},{7,6},{8,9},{9,8},{10,11... | collective-permute-start | bytes 1572872 | tf_op jit(solution)/shard_map/ppermute | solution.py:40
  11.1 1.5 %collective-permute-start.2 = (bf16[4,256,256]{2,1,0:T(8,128)(2,1)S(1)}, bf16[4,256,256]{2,1,0:T(8,128)(2,1)S(1)}, u32[]{:S(2)}, u32[]{:S(2)}) collective-permute-start(bf16[4,256,256]{2,1,0:T(8,128)(2,1)S(1)} %get-tuple-element.79.refs_2_.refs_10_.refs_18_), channel_id=1, source_target_pairs={{0,16},{8,24},{16,0},{24,8},{1,17},{9,25},{17,1},{25,9},{2,18},{10... | collective-permute-start | bytes 1572872 | tf_op jit(solution)/shard_map/ppermute | solution.py:44
  12.6 0.5 collective-permute-start.10
  13.1 1.5 %shard_map.38 = (bf16[2,256,256]{2,1,0:T(8,128)(2,1)S(1)}, bf16[2,256,256]{2,1,0:T(8,128)(2,1)S(1)}, bf16[2,256,256]{2,1,0:T(8,128)(2,1)S(1)}, bf16[2,256,256]{2,1,0:T(8,128)(2,1)S(1)}) custom-call(s32[3]{0:T(128)S(1)} %pad_add_fusion._.place_ref, bf16[2,2,128,16,128]{4,3,2,1,0:T(8,128)(2,1)S(1)} %copy-done.1), custom_call_target="tpu_custom_call" | custom-call | tf_op jit(solution)/shard_map/pallas_call | solution.py:60
  14.6 9.8 %collective-permute-done.3.refs_6_.refs_14_.refs_22_ = bf16[4,256,256]{2,1,0:T(8,128)(2,1)S(1)} collective-permute-done((bf16[4,256,256]{2,1,0:T(8,128)(2,1)S(1)}, bf16[4,256,256]{2,1,0:T(8,128)(2,1)S(1)}, u32[]{:S(2)}, u32[]{:S(2)}) %collective-permute-start.3) | collective-permute-done | bytes 524320 | tf_op jit(solution)/shard_map/ppermute | solution.py:40
  24.5 0.5 collective-permute-start.6
  25.0 1.5 %collective-permute-start.4 = (bf16[4,256,256]{2,1,0:T(8,128)(2,1)S(1)}, bf16[4,256,256]{2,1,0:T(8,128)(2,1)S(1)}, u32[]{:S(2)}, u32[]{:S(2)}) collective-permute-start(bf16[4,256,256]{2,1,0:T(8,128)(2,1)S(1)} %collective-permute-done.3.refs_6_.refs_14_.refs_22_), channel_id=1, source_target_pairs={{0,16},{8,24},{16,0},{24,8},{1,17},{9,25},{17,1},{25,9},{2,18},{10... | collective-permute-start | bytes 1572872 | tf_op jit(solution)/shard_map/ppermute | solution.py:44
  26.5 0.7 collective-permute-done.6.refs_5_.refs_13_.refs_21_
  27.1 2.5 %collective-permute-start.7 = (bf16[2,256,256]{2,1,0:T(8,128)(2,1)S(1)}, bf16[2,256,256]{2,1,0:T(8,128)(2,1)S(1)}, u32[]{:S(2)}, u32[]{:S(2)}) collective-permute-start(bf16[2,256,256]{2,1,0:T(8,128)(2,1)S(1)} %get-tuple-element.81), channel_id=1, source_target_pairs={{0,6},{1,7},{2,4},{3,5},{4,2},{5,3},{6,0},{7,1},{8,14},{9,15},{10,... | collective-permute-start | bytes 786440 | tf_op jit(solution)/shard_map/ppermute | solution.py:40
  29.6 5.9 %collective-permute-start.8 = (bf16[2,256,256]{2,1,0:T(8,128)(2,1)S(1)}, bf16[2,256,256]{2,1,0:T(8,128)(2,1)S(1)}, u32[]{:S(2)}, u32[]{:S(2)}) collective-permute-start(bf16[2,256,256]{2,1,0:T(8,128)(2,1)S(1)} %get-tuple-element.82), channel_id=1, source_target_pairs={{0,2},{1,3},{2,0},{3,1},{4,6},{5,7},{6,4},{7,5},{8,10},{9,11},{10,... | collective-permute-start | bytes 786440 | tf_op jit(solution)/shard_map/ppermute | solution.py:40
  35.5 4.3 %collective-permute-done.10.refs_1_ = bf16[4,384,256]{2,1,0:T(8,128)(2,1)S(1)} collective-permute-done((bf16[4,384,256]{2,1,0:T(8,128)(2,1)S(1)}, bf16[4,384,256]{2,1,0:T(8,128)(2,1)S(1)}, u32[]{:S(2)}, u32[]{:S(2)}) %collective-permute-start.10) | collective-permute-done | bytes 786464 | tf_op jit(solution)/shard_map/ppermute | solution.py:40
  39.8 1.5 %collective-permute-start.11 = (bf16[2,256,256]{2,1,0:T(8,128)(2,1)S(1)}, bf16[2,256,256]{2,1,0:T(8,128)(2,1)S(1)}, u32[]{:S(2)}, u32[]{:S(2)}) collective-permute-start(bf16[2,256,256]{2,1,0:T(8,128)(2,1)S(1)} %get-tuple-element.84), channel_id=1, source_target_pairs={{0,16},{8,24},{16,0},{24,8},{1,17},{9,25},{17,1},{25,9},{2,18},{10... | collective-permute-start | bytes 786440 | tf_op jit(solution)/shard_map/ppermute | solution.py:44
  41.3 1.6 %collective-permute-done.8 = bf16[2,256,256]{2,1,0:T(8,128)(2,1)S(1)} collective-permute-done((bf16[2,256,256]{2,1,0:T(8,128)(2,1)S(1)}, bf16[2,256,256]{2,1,0:T(8,128)(2,1)S(1)}, u32[]{:S(2)}, u32[]{:S(2)}) %collective-permute-start.8) | collective-permute-done | bytes 262176 | tf_op jit(solution)/shard_map/ppermute | solution.py:40
  42.9 11.2 %collective-permute-done.9 = bf16[2,256,256]{2,1,0:T(8,128)(2,1)S(1)} collective-permute-done((bf16[2,256,256]{2,1,0:T(8,128)(2,1)S(1)}, bf16[2,256,256]{2,1,0:T(8,128)(2,1)S(1)}, u32[]{:S(2)}, u32[]{:S(2)}) %collective-permute-start.9) | collective-permute-done | bytes 262176 | tf_op jit(solution)/shard_map/ppermute | solution.py:40
  54.2 0.5 collective-permute-start.13
  54.7 1.7 %collective-permute-done.13 = bf16[2,256,256]{2,1,0:T(8,128)(2,1)S(1)} collective-permute-done((bf16[2,256,256]{2,1,0:T(8,128)(2,1)S(1)}, bf16[2,256,256]{2,1,0:T(8,128)(2,1)S(1)}, u32[]{:S(2)}, u32[]{:S(2)}) %collective-permute-start.13) | collective-permute-done | bytes 262176 | tf_op jit(solution)/shard_map/ppermute | solution.py:44
  56.4 0.4 collective-permute-done.15
  56.8 1.7 %shard_map.40 = f32[4,384,256]{2,1,0:T(8,128)S(1)} custom-call(s32[3]{0:T(128)S(1)} %pad_add_fusion._.place_ref, bf16[4,384,256]{2,1,0:T(8,128)(2,1)S(1)} %get-tuple-element.105.refs_0_, bf16[4,384,256]{2,1,0:T(8,128)(2,1)S(1)} %collective-permute-done.10.refs_1_, bf16[4,256,256]{2,1,0:T(8,128)(2,1)S(1)} %get-tuple-element.79.refs_2_.refs_10_.refs_18_, ...), custom_call_target="tpu_custom_call" | custom-call | tf_op jit(solution)/shard_map/pallas_call | solution.py:60
  58.7 1.6 %collective-permute-start.16 = (f16[4,384,256]{2,1,0:T(8,128)(2,1)S(1)}, f16[4,384,256]{2,1,0:T(8,128)(2,1)S(1)}, u32[]{:S(2)}, u32[]{:S(2)}) collective-permute-start(f16[4,384,256]{2,1,0:T(8,128)(2,1)S(1)} %multiply_convert_fusion.5), channel_id=1, source_target_pairs={{0,2},{1,3},{6,4},{7,5},{8,10},{9,11},{14,12},{15,13},{16,18},{17,... | collective-permute-start | bytes 2359304 | tf_op jit(solution)/shard_map/ppermute | solution.py:40
  60.5 1.6 %collective-permute-start.18 = (bf16[3,2,256,256]{3,2,1,0:T(8,128)(2,1)S(1)}, bf16[3,2,256,256]{3,2,1,0:T(8,128)(2,1)S(1)}, u32[]{:S(2)}, u32[]{:S(2)}) collective-permute-start(bf16[3,2,256,256]{3,2,1,0:T(8,128)(2,1)S(1)} %pad_maximum_fusion.refs_10_.refs_14_.refs_18_), channel_id=1, source_target_pairs={{0,16},{8,24},{16,0},{24,8},{1,17},{9,25},{17,1},{25,9},{2,18},{10... | collective-permute-start | bytes 2359304 | tf_op jit(solution)/shard_map/ppermute | solution.py:44
  62.0 0.7 collective-permute-start.17
  62.7 1.3 %collective-permute-start.19 = (bf16[4,384,256]{2,1,0:T(8,128)(2,1)S(1)}, bf16[4,384,256]{2,1,0:T(8,128)(2,1)S(1)}, u32[]{:S(2)}, u32[]{:S(2)}) collective-permute-start(bf16[4,384,256]{2,1,0:T(8,128)(2,1)S(1)} %collective-permute-done.1.refs_4_), channel_id=1, source_target_pairs={{2,0},{3,1},{4,6},{5,7},{10,8},{11,9},{12,14},{13,15},{18,16},{19,... | collective-permute-start | bytes 2359304 | tf_op jit(solution)/shard_map/ppermute | solution.py:40
  64.0 2.7 %shard_map.41 = (f32[4,384,256]{2,1,0:T(8,128)S(1)}, f32[4,384,256]{2,1,0:T(8,128)S(1)}, f32[4,384,256]{2,1,0:T(8,128)S(1)}) custom-call(s32[3]{0:T(128)S(1)} %pad_add_fusion._.place_ref, bf16[4,384,256]{2,1,0:T(8,128)(2,1)S(1)} %get-tuple-element.105.refs_0_, bf16[4,384,256]{2,1,0:T(8,128)(2,1)S(1)} %collective-permute-done.10.refs_1_, ...), custom_call_target="tpu_custom_call" | custom-call | tf_op jit(solution)/shard_map/pallas_call | solution.py:60
  66.8 10.6 %collective-permute-done.16 = f16[4,384,256]{2,1,0:T(8,128)(2,1)S(1)} collective-permute-done((f16[4,384,256]{2,1,0:T(8,128)(2,1)S(1)}, f16[4,384,256]{2,1,0:T(8,128)(2,1)S(1)}, u32[]{:S(2)}, u32[]{:S(2)}) %collective-permute-start.16) | collective-permute-done | bytes 786464 | tf_op jit(solution)/shard_map/ppermute | solution.py:40
  77.4 0.5 multiply_convert_fusion.3
  77.9 4.4 %collective-permute-start.21 = (f16[4,384,256]{2,1,0:T(8,128)(2,1)S(1)}, f16[4,384,256]{2,1,0:T(8,128)(2,1)S(1)}, u32[]{:S(2)}, u32[]{:S(2)}) collective-permute-start(f16[4,384,256]{2,1,0:T(8,128)(2,1)S(1)} %get-tuple-element.123), channel_id=1, source_target_pairs={{0,2},{1,3},{6,4},{7,5},{8,10},{9,11},{14,12},{15,13},{16,18},{17,... | collective-permute-start | bytes 2359304 | tf_op jit(solution)/shard_map/ppermute | solution.py:40
  82.3 1.3 %collective-permute-done.19.refs_3_ = bf16[4,384,256]{2,1,0:T(8,128)(2,1)S(1)} collective-permute-done((bf16[4,384,256]{2,1,0:T(8,128)(2,1)S(1)}, bf16[4,384,256]{2,1,0:T(8,128)(2,1)S(1)}, u32[]{:S(2)}, u32[]{:S(2)}) %collective-permute-start.19) | collective-permute-done | bytes 786464 | tf_op jit(solution)/shard_map/ppermute | solution.py:40
  83.6 0.7 collective-permute-start.22
  84.3 1.3 %collective-permute-start.20 = (bf16[4,384,256]{2,1,0:T(8,128)(2,1)S(1)}, bf16[4,384,256]{2,1,0:T(8,128)(2,1)S(1)}, u32[]{:S(2)}, u32[]{:S(2)}) collective-permute-start(bf16[4,384,256]{2,1,0:T(8,128)(2,1)S(1)} %collective-permute-done.17.refs_2_), channel_id=1, source_target_pairs={{2,0},{3,1},{4,6},{5,7},{10,8},{11,9},{12,14},{13,15},{18,16},{19,... | collective-permute-start | bytes 2359304 | tf_op jit(solution)/shard_map/ppermute | solution.py:40
  85.7 0.5 collective-permute-start.24
  86.2 12.3 %collective-permute-done.21 = f16[4,384,256]{2,1,0:T(8,128)(2,1)S(1)} collective-permute-done((f16[4,384,256]{2,1,0:T(8,128)(2,1)S(1)}, f16[4,384,256]{2,1,0:T(8,128)(2,1)S(1)}, u32[]{:S(2)}, u32[]{:S(2)}) %collective-permute-start.21) | collective-permute-done | bytes 786464 | tf_op jit(solution)/shard_map/ppermute | solution.py:40
  98.9 0.3 multiply_convert_fusion.1
  99.2 4.6 %collective-permute-start.26 = (f16[4,384,256]{2,1,0:T(8,128)(2,1)S(1)}, f16[4,384,256]{2,1,0:T(8,128)(2,1)S(1)}, u32[]{:S(2)}, u32[]{:S(2)}) collective-permute-start(f16[4,384,256]{2,1,0:T(8,128)(2,1)S(1)} %multiply_convert_fusion.1), channel_id=1, source_target_pairs={{0,2},{1,3},{2,0},{3,1},{4,6},{5,7},{6,4},{7,5},{8,10},{9,11},{10,... | collective-permute-start | bytes 2359304 | tf_op jit(solution)/shard_map/ppermute | solution.py:40
  103.7 0.7 collective-permute-start.27
  104.4 1.7 %collective-permute-done.20.refs_5_ = bf16[4,384,256]{2,1,0:T(8,128)(2,1)S(1)} collective-permute-done((bf16[4,384,256]{2,1,0:T(8,128)(2,1)S(1)}, bf16[4,384,256]{2,1,0:T(8,128)(2,1)S(1)}, u32[]{:S(2)}, u32[]{:S(2)}) %collective-permute-start.20) | collective-permute-done | bytes 786464 | tf_op jit(solution)/shard_map/ppermute | solution.py:40
  106.2 2.3 %shard_map.43 = f32[4,384,256]{2,1,0:T(8,128)S(1)} custom-call(s32[3]{0:T(128)S(1)} %pad_add_fusion._.place_ref, bf16[4,384,256]{2,1,0:T(8,128)(2,1)S(1)} %get-tuple-element.72.refs_0_, bf16[4,384,256]{2,1,0:T(8,128)(2,1)S(1)} %collective-permute-done.refs_1_, bf16[4,384,256]{2,1,0:T(8,128)(2,1)S(1)} %collective-permute-done.17.refs_2_, ...), custom_call_target="tpu_custom_call" | custom-call | tf_op jit(solution)/shard_map/pallas_call | solution.py:60
  108.6 1.6 %collective-permute-start.25 = (f16[4,384,256]{2,1,0:T(8,128)(2,1)S(1)}, f16[4,384,256]{2,1,0:T(8,128)(2,1)S(1)}, u32[]{:S(2)}, u32[]{:S(2)}) collective-permute-start(f16[4,384,256]{2,1,0:T(8,128)(2,1)S(1)} %multiply_convert_fusion), channel_id=1, source_target_pairs={{0,1},{1,0},{2,3},{3,2},{4,5},{5,4},{6,7},{7,6},{8,9},{9,8},{10,11... | collective-permute-start | bytes 2359304 | tf_op jit(solution)/shard_map/ppermute | solution.py:40
  110.2 2.3 %shard_map.42 = f32[4,384,256]{2,1,0:T(8,128)S(1)} custom-call(s32[3]{0:T(128)S(1)} %pad_add_fusion._.place_ref, bf16[4,384,256]{2,1,0:T(8,128)(2,1)S(1)} %get-tuple-element.72.refs_0_, bf16[4,384,256]{2,1,0:T(8,128)(2,1)S(1)} %collective-permute-done.refs_1_, bf16[4,384,256]{2,1,0:T(8,128)(2,1)S(1)} %collective-permute-done.17.refs_2_, ...), custom_call_target="tpu_custom_call" | custom-call | tf_op jit(solution)/shard_map/pallas_call | solution.py:60
  112.5 8.7 %collective-permute-done.26 = f16[4,384,256]{2,1,0:T(8,128)(2,1)S(1)} collective-permute-done((f16[4,384,256]{2,1,0:T(8,128)(2,1)S(1)}, f16[4,384,256]{2,1,0:T(8,128)(2,1)S(1)}, u32[]{:S(2)}, u32[]{:S(2)}) %collective-permute-start.26) | collective-permute-done | bytes 786464 | tf_op jit(solution)/shard_map/ppermute | solution.py:40
  121.5 1.6 %copy-done = f32[8,3,128,2,128]{4,3,2,1,0:T(2,128)S(1)} copy-done((f32[8,3,128,2,128]{4,3,2,1,0:T(2,128)S(1)}, f32[8,3,128,2,128]{4,3,2,1,0:T(2,128)}, u32[]{:S(2)}) %copy-start) | copy-done | bytes 3145752
  123.1 2.3 %shard_map.44.refs_0_ = f32[8,768,128]{2,1,0:T(8,128)} custom-call(s32[3]{0:T(128)S(1)} %pad_add_fusion._.place_ref, f32[8,768,128]{2,1,0:T(8,128)S(1)} %bitcast.13, f32[4,384,256]{2,1,0:T(8,128)S(1)} %multiply_add_fusion.add_ref), custom_call_target="tpu_custom_call" | custom-call | tf_op jit(solution)/shard_map/pallas_call | solution.py:60
  125.6 2.3 %shard_map.45 = f32[8,768,128]{2,1,0:T(8,128)} custom-call(s32[3]{0:T(128)S(1)} %pad_add_fusion._.place_ref, f32[8,768,128]{2,1,0:T(8,128)S(1)} %bitcast.14, f32[4,384,256]{2,1,0:T(8,128)S(1)} %multiply_add_fusion.1.add_ref, f32[8,768,128]{2,1,0:T(8,128)} %shard_map.44.refs_0_), custom_call_target="tpu_custom_call", output_to_operand_aliasing={{}: (3, {})} | custom-call | tf_op jit(solution)/shard_map/pallas_call | solution.py:60
  (32 shorter events, 1.6 us)
Async XLA Ops:
  0.1 1.4 %copy-start.2 = (bf16[8,3,128,2,128]{4,3,2,1,0:T(2,128)(2,1)S(1)}, bf16[8,3,128,2,128]{4,3,2,1,0:T(2,128)(2,1)}, u32[]{:S(2)}) copy-start(bf16[8,3,128,2,128]{4,3,2,1,0:T(2,128)(2,1)} %param.4) | copy-start | bytes 4718596
  2.6 21.9 %collective-permute-start = (bf16[4,384,256]{2,1,0:T(8,128)(2,1)S(1)}, bf16[4,384,256]{2,1,0:T(8,128)(2,1)S(1)}, u32[]{:S(2)}, u32[]{:S(2)}) collective-permute-start(bf16[4,384,256]{2,1,0:T(8,128)(2,1)S(1)} %get-tuple-element.72.refs_0_), channel_id=1, source_target_pairs={{0,2},{1,3},{2,0},{3,1},{4,6},{5,7},{6,4},{7,5},{8,10},{9,11},{10,... | collective-permute-start | bytes 2359304 | tf_op jit(solution)/shard_map/ppermute | solution.py:40
  5.7 1.6 %copy-start.1 = (bf16[2,2,128,16,128]{4,3,2,1,0:T(8,128)(2,1)S(1)}, bf16[2,2,128,16,128]{4,3,2,1,0:T(8,128)(2,1)}, u32[]{:S(2)}) copy-start(bf16[2,2,128,16,128]{4,3,2,1,0:T(8,128)(2,1)} %in_ref.1) | copy-start | bytes 6291460
  8.8 15.6 %collective-permute-start.1 = (bf16[4,384,256]{2,1,0:T(8,128)(2,1)S(1)}, bf16[4,384,256]{2,1,0:T(8,128)(2,1)S(1)}, u32[]{:S(2)}, u32[]{:S(2)}) collective-permute-start(bf16[4,384,256]{2,1,0:T(8,128)(2,1)S(1)} %get-tuple-element.72.refs_0_), channel_id=1, source_target_pairs={{2,4},{3,5},{4,2},{5,3},{10,12},{11,13},{12,10},{13,11},{18,20},{1... | collective-permute-start | bytes 2359304 | tf_op jit(solution)/shard_map/ppermute | solution.py:40
  9.5 14.9 %collective-permute-start.3 = (bf16[4,256,256]{2,1,0:T(8,128)(2,1)S(1)}, bf16[4,256,256]{2,1,0:T(8,128)(2,1)S(1)}, u32[]{:S(2)}, u32[]{:S(2)}) collective-permute-start(bf16[4,256,256]{2,1,0:T(8,128)(2,1)S(1)} %get-tuple-element.71), channel_id=1, source_target_pairs={{0,1},{1,0},{2,3},{3,2},{4,5},{5,4},{6,7},{7,6},{8,9},{9,8},{10,11... | collective-permute-start | bytes 1572872 | tf_op jit(solution)/shard_map/ppermute | solution.py:40
  11.1 13.3 %collective-permute-start.2 = (bf16[4,256,256]{2,1,0:T(8,128)(2,1)S(1)}, bf16[4,256,256]{2,1,0:T(8,128)(2,1)S(1)}, u32[]{:S(2)}, u32[]{:S(2)}) collective-permute-start(bf16[4,256,256]{2,1,0:T(8,128)(2,1)S(1)} %get-tuple-element.79.refs_2_.refs_10_.refs_18_), channel_id=1, source_target_pairs={{0,16},{8,24},{16,0},{24,8},{1,17},{9,25},{17,1},{25,9},{2,18},{10... | collective-permute-start | bytes 1572872 | tf_op jit(solution)/shard_map/ppermute | solution.py:44
  12.6 27.2 %collective-permute-start.10 = (bf16[4,384,256]{2,1,0:T(8,128)(2,1)S(1)}, bf16[4,384,256]{2,1,0:T(8,128)(2,1)S(1)}, u32[]{:S(2)}, u32[]{:S(2)}) collective-permute-start(bf16[4,384,256]{2,1,0:T(8,128)(2,1)S(1)} %get-tuple-element.105.refs_0_), channel_id=1, source_target_pairs={{0,1},{1,0},{2,3},{3,2},{4,5},{5,4},{6,7},{7,6},{8,9},{9,8},{10,11... | collective-permute-start | bytes 2359304 | tf_op jit(solution)/shard_map/ppermute | solution.py:40
  24.4 2.1 %collective-permute-start.5 = (bf16[4,256,256]{2,1,0:T(8,128)(2,1)S(1)}, bf16[4,256,256]{2,1,0:T(8,128)(2,1)S(1)}, u32[]{:S(2)}, u32[]{:S(2)}) collective-permute-start(bf16[4,256,256]{2,1,0:T(8,128)(2,1)S(1)} %get-tuple-element.79.refs_2_.refs_10_.refs_18_), channel_id=1, source_target_pairs={{0,8},{8,0},{16,24},{24,16},{1,9},{9,1},{17,25},{25,17},{2,10},{10... | collective-permute-start | bytes 1572872 | tf_op jit(solution)/shard_map/ppermute | solution.py:44
  24.5 2.6 %collective-permute-start.6 = (bf16[4,256,256]{2,1,0:T(8,128)(2,1)S(1)}, bf16[4,256,256]{2,1,0:T(8,128)(2,1)S(1)}, u32[]{:S(2)}, u32[]{:S(2)}) collective-permute-start(bf16[4,256,256]{2,1,0:T(8,128)(2,1)S(1)} %collective-permute-done.2.refs_3_.refs_11_.refs_19_), channel_id=1, source_target_pairs={{0,8},{8,0},{16,24},{24,16},{1,9},{9,1},{17,25},{25,17},{2,10},{10... | collective-permute-start | bytes 1572872 | tf_op jit(solution)/shard_map/ppermute | solution.py:44
  25.0 16.3 %collective-permute-start.4 = (bf16[4,256,256]{2,1,0:T(8,128)(2,1)S(1)}, bf16[4,256,256]{2,1,0:T(8,128)(2,1)S(1)}, u32[]{:S(2)}, u32[]{:S(2)}) collective-permute-start(bf16[4,256,256]{2,1,0:T(8,128)(2,1)S(1)} %collective-permute-done.3.refs_6_.refs_14_.refs_22_), channel_id=1, source_target_pairs={{0,16},{8,24},{16,0},{24,8},{1,17},{9,25},{17,1},{25,9},{2,18},{10... | collective-permute-start | bytes 1572872 | tf_op jit(solution)/shard_map/ppermute | solution.py:44
  27.1 14.2 %collective-permute-start.7 = (bf16[2,256,256]{2,1,0:T(8,128)(2,1)S(1)}, bf16[2,256,256]{2,1,0:T(8,128)(2,1)S(1)}, u32[]{:S(2)}, u32[]{:S(2)}) collective-permute-start(bf16[2,256,256]{2,1,0:T(8,128)(2,1)S(1)} %get-tuple-element.81), channel_id=1, source_target_pairs={{0,6},{1,7},{2,4},{3,5},{4,2},{5,3},{6,0},{7,1},{8,14},{9,15},{10,... | collective-permute-start | bytes 786440 | tf_op jit(solution)/shard_map/ppermute | solution.py:40
  29.6 13.3 %collective-permute-start.8 = (bf16[2,256,256]{2,1,0:T(8,128)(2,1)S(1)}, bf16[2,256,256]{2,1,0:T(8,128)(2,1)S(1)}, u32[]{:S(2)}, u32[]{:S(2)}) collective-permute-start(bf16[2,256,256]{2,1,0:T(8,128)(2,1)S(1)} %get-tuple-element.82), channel_id=1, source_target_pairs={{0,2},{1,3},{2,0},{3,1},{4,6},{5,7},{6,4},{7,5},{8,10},{9,11},{10,... | collective-permute-start | bytes 786440 | tf_op jit(solution)/shard_map/ppermute | solution.py:40
  35.5 18.7 %collective-permute-start.9 = (bf16[2,256,256]{2,1,0:T(8,128)(2,1)S(1)}, bf16[2,256,256]{2,1,0:T(8,128)(2,1)S(1)}, u32[]{:S(2)}, u32[]{:S(2)}) collective-permute-start(bf16[2,256,256]{2,1,0:T(8,128)(2,1)S(1)} %get-tuple-element.83), channel_id=1, source_target_pairs={{0,4},{1,5},{2,6},{3,7},{4,0},{5,1},{6,2},{7,3},{8,12},{9,13},{10,... | collective-permute-start | bytes 786440 | tf_op jit(solution)/shard_map/ppermute | solution.py:40
  39.8 14.4 %collective-permute-start.11 = (bf16[2,256,256]{2,1,0:T(8,128)(2,1)S(1)}, bf16[2,256,256]{2,1,0:T(8,128)(2,1)S(1)}, u32[]{:S(2)}, u32[]{:S(2)}) collective-permute-start(bf16[2,256,256]{2,1,0:T(8,128)(2,1)S(1)} %get-tuple-element.84), channel_id=1, source_target_pairs={{0,16},{8,24},{16,0},{24,8},{1,17},{9,25},{17,1},{25,9},{2,18},{10... | collective-permute-start | bytes 786440 | tf_op jit(solution)/shard_map/ppermute | solution.py:44
  41.3 13.4 %collective-permute-start.12 = (bf16[4,256,256]{2,1,0:T(8,128)(2,1)S(1)}, bf16[4,256,256]{2,1,0:T(8,128)(2,1)S(1)}, u32[]{:S(2)}, u32[]{:S(2)}) collective-permute-start(bf16[4,256,256]{2,1,0:T(8,128)(2,1)S(1)} %collective-permute-done.3.refs_6_.refs_14_.refs_22_), channel_id=1, source_target_pairs={{0,8},{8,0},{16,24},{24,16},{1,9},{9,1},{17,25},{25,17},{2,10},{10... | collective-permute-start | bytes 1572872 | tf_op jit(solution)/shard_map/ppermute | solution.py:44
  54.2 2.7 %collective-permute-start.14 = (bf16[4,256,256]{2,1,0:T(8,128)(2,1)S(1)}, bf16[4,256,256]{2,1,0:T(8,128)(2,1)S(1)}, u32[]{:S(2)}, u32[]{:S(2)}) collective-permute-start(bf16[4,256,256]{2,1,0:T(8,128)(2,1)S(1)} %collective-permute-done.4.refs_7_.refs_15_.refs_23_), channel_id=1, source_target_pairs={{0,8},{8,0},{16,24},{24,16},{1,9},{9,1},{17,25},{25,17},{2,10},{10... | collective-permute-start | bytes 1572872 | tf_op jit(solution)/shard_map/ppermute | solution.py:44
  54.2 2.3 %collective-permute-start.13 = (bf16[2,256,256]{2,1,0:T(8,128)(2,1)S(1)}, bf16[2,256,256]{2,1,0:T(8,128)(2,1)S(1)}, u32[]{:S(2)}, u32[]{:S(2)}) collective-permute-start(bf16[2,256,256]{2,1,0:T(8,128)(2,1)S(1)} %get-tuple-element.84), channel_id=1, source_target_pairs={{0,8},{8,0},{16,24},{24,16},{1,9},{9,1},{17,25},{25,17},{2,10},{10... | collective-permute-start | bytes 786440 | tf_op jit(solution)/shard_map/ppermute | solution.py:44
  54.7 2.1 %collective-permute-start.15 = (bf16[2,256,256]{2,1,0:T(8,128)(2,1)S(1)}, bf16[2,256,256]{2,1,0:T(8,128)(2,1)S(1)}, u32[]{:S(2)}, u32[]{:S(2)}) collective-permute-start(bf16[2,256,256]{2,1,0:T(8,128)(2,1)S(1)} %collective-permute-done.11), channel_id=1, source_target_pairs={{0,8},{8,0},{16,24},{24,16},{1,9},{9,1},{17,25},{25,17},{2,10},{10... | collective-permute-start | bytes 786440 | tf_op jit(solution)/shard_map/ppermute | solution.py:44
  58.7 18.7 %collective-permute-start.16 = (f16[4,384,256]{2,1,0:T(8,128)(2,1)S(1)}, f16[4,384,256]{2,1,0:T(8,128)(2,1)S(1)}, u32[]{:S(2)}, u32[]{:S(2)}) collective-permute-start(f16[4,384,256]{2,1,0:T(8,128)(2,1)S(1)} %multiply_convert_fusion.5), channel_id=1, source_target_pairs={{0,2},{1,3},{6,4},{7,5},{8,10},{9,11},{14,12},{15,13},{16,18},{17,... | collective-permute-start | bytes 2359304 | tf_op jit(solution)/shard_map/ppermute | solution.py:40
  60.5 21.9 %collective-permute-start.18 = (bf16[3,2,256,256]{3,2,1,0:T(8,128)(2,1)S(1)}, bf16[3,2,256,256]{3,2,1,0:T(8,128)(2,1)S(1)}, u32[]{:S(2)}, u32[]{:S(2)}) collective-permute-start(bf16[3,2,256,256]{3,2,1,0:T(8,128)(2,1)S(1)} %pad_maximum_fusion.refs_10_.refs_14_.refs_18_), channel_id=1, source_target_pairs={{0,16},{8,24},{16,0},{24,8},{1,17},{9,25},{17,1},{25,9},{2,18},{10... | collective-permute-start | bytes 2359304 | tf_op jit(solution)/shard_map/ppermute | solution.py:44
  62.0 20.3 %collective-permute-start.17 = (bf16[4,384,256]{2,1,0:T(8,128)(2,1)S(1)}, bf16[4,384,256]{2,1,0:T(8,128)(2,1)S(1)}, u32[]{:S(2)}, u32[]{:S(2)}) collective-permute-start(bf16[4,384,256]{2,1,0:T(8,128)(2,1)S(1)} %collective-permute-done.refs_1_), channel_id=1, source_target_pairs={{2,4},{3,5},{4,2},{5,3},{10,12},{11,13},{12,10},{13,11},{18,20},{1... | collective-permute-start | bytes 2359304 | tf_op jit(solution)/shard_map/ppermute | solution.py:40
  62.7 20.9 %collective-permute-start.19 = (bf16[4,384,256]{2,1,0:T(8,128)(2,1)S(1)}, bf16[4,384,256]{2,1,0:T(8,128)(2,1)S(1)}, u32[]{:S(2)}, u32[]{:S(2)}) collective-permute-start(bf16[4,384,256]{2,1,0:T(8,128)(2,1)S(1)} %collective-permute-done.1.refs_4_), channel_id=1, source_target_pairs={{2,0},{3,1},{4,6},{5,7},{10,8},{11,9},{12,14},{13,15},{18,16},{19,... | collective-permute-start | bytes 2359304 | tf_op jit(solution)/shard_map/ppermute | solution.py:40
  77.9 20.6 %collective-permute-start.21 = (f16[4,384,256]{2,1,0:T(8,128)(2,1)S(1)}, f16[4,384,256]{2,1,0:T(8,128)(2,1)S(1)}, u32[]{:S(2)}, u32[]{:S(2)}) collective-permute-start(f16[4,384,256]{2,1,0:T(8,128)(2,1)S(1)} %get-tuple-element.123), channel_id=1, source_target_pairs={{0,2},{1,3},{6,4},{7,5},{8,10},{9,11},{14,12},{15,13},{16,18},{17,... | collective-permute-start | bytes 2359304 | tf_op jit(solution)/shard_map/ppermute | solution.py:40
  83.6 15.2 %collective-permute-start.22 = (f16[4,384,256]{2,1,0:T(8,128)(2,1)S(1)}, f16[4,384,256]{2,1,0:T(8,128)(2,1)S(1)}, u32[]{:S(2)}, u32[]{:S(2)}) collective-permute-start(f16[4,384,256]{2,1,0:T(8,128)(2,1)S(1)} %get-tuple-element.115), channel_id=1, source_target_pairs={{2,4},{3,5},{4,2},{5,3},{10,12},{11,13},{12,10},{13,11},{18,20},{1... | collective-permute-start | bytes 2359304 | tf_op jit(solution)/shard_map/ppermute | solution.py:40
  84.3 21.8 %collective-permute-start.20 = (bf16[4,384,256]{2,1,0:T(8,128)(2,1)S(1)}, bf16[4,384,256]{2,1,0:T(8,128)(2,1)S(1)}, u32[]{:S(2)}, u32[]{:S(2)}) collective-permute-start(bf16[4,384,256]{2,1,0:T(8,128)(2,1)S(1)} %collective-permute-done.17.refs_2_), channel_id=1, source_target_pairs={{2,0},{3,1},{4,6},{5,7},{10,8},{11,9},{12,14},{13,15},{18,16},{19,... | collective-permute-start | bytes 2359304 | tf_op jit(solution)/shard_map/ppermute | solution.py:40
  85.6 20.5 %collective-permute-start.23 = (bf16[3,2,256,256]{3,2,1,0:T(8,128)(2,1)S(1)}, bf16[3,2,256,256]{3,2,1,0:T(8,128)(2,1)S(1)}, u32[]{:S(2)}, u32[]{:S(2)}) collective-permute-start(bf16[3,2,256,256]{3,2,1,0:T(8,128)(2,1)S(1)} %pad_maximum_fusion.refs_10_.refs_14_.refs_18_), channel_id=1, source_target_pairs={{0,8},{8,0},{16,24},{24,16},{1,9},{9,1},{17,25},{25,17},{2,10},{10... | collective-permute-start | bytes 2359304 | tf_op jit(solution)/shard_map/ppermute | solution.py:44
  85.7 20.4 %collective-permute-start.24 = (bf16[3,2,256,256]{3,2,1,0:T(8,128)(2,1)S(1)}, bf16[3,2,256,256]{3,2,1,0:T(8,128)(2,1)S(1)}, u32[]{:S(2)}, u32[]{:S(2)}) collective-permute-start(bf16[3,2,256,256]{3,2,1,0:T(8,128)(2,1)S(1)} %collective-permute-done.18.refs_11_.refs_15_.refs_19_), channel_id=1, source_target_pairs={{0,8},{8,0},{16,24},{24,16},{1,9},{9,1},{17,25},{25,17},{2,10},{10... | collective-permute-start | bytes 2359304 | tf_op jit(solution)/shard_map/ppermute | solution.py:44
  99.2 22.0 %collective-permute-start.26 = (f16[4,384,256]{2,1,0:T(8,128)(2,1)S(1)}, f16[4,384,256]{2,1,0:T(8,128)(2,1)S(1)}, u32[]{:S(2)}, u32[]{:S(2)}) collective-permute-start(f16[4,384,256]{2,1,0:T(8,128)(2,1)S(1)} %multiply_convert_fusion.1), channel_id=1, source_target_pairs={{0,2},{1,3},{2,0},{3,1},{4,6},{5,7},{6,4},{7,5},{8,10},{9,11},{10,... | collective-permute-start | bytes 2359304 | tf_op jit(solution)/shard_map/ppermute | solution.py:40
  103.7 17.5 %collective-permute-start.27 = (f16[4,384,256]{2,1,0:T(8,128)(2,1)S(1)}, f16[4,384,256]{2,1,0:T(8,128)(2,1)S(1)}, u32[]{:S(2)}, u32[]{:S(2)}) collective-permute-start(f16[4,384,256]{2,1,0:T(8,128)(2,1)S(1)} %multiply_convert_fusion.2), channel_id=1, source_target_pairs={{2,4},{3,5},{4,2},{5,3},{10,12},{11,13},{12,10},{13,11},{18,20},{1... | collective-permute-start | bytes 2359304 | tf_op jit(solution)/shard_map/ppermute | solution.py:40
  108.6 16.8 %collective-permute-start.25 = (f16[4,384,256]{2,1,0:T(8,128)(2,1)S(1)}, f16[4,384,256]{2,1,0:T(8,128)(2,1)S(1)}, u32[]{:S(2)}, u32[]{:S(2)}) collective-permute-start(f16[4,384,256]{2,1,0:T(8,128)(2,1)S(1)} %multiply_convert_fusion), channel_id=1, source_target_pairs={{0,1},{1,0},{2,3},{3,2},{4,5},{5,4},{6,7},{7,6},{8,9},{9,8},{10,11... | collective-permute-start | bytes 2359304 | tf_op jit(solution)/shard_map/ppermute | solution.py:40
  121.2 1.9 %copy-start = (f32[8,3,128,2,128]{4,3,2,1,0:T(2,128)S(1)}, f32[8,3,128,2,128]{4,3,2,1,0:T(2,128)}, u32[]{:S(2)}) copy-start(f32[8,3,128,2,128]{4,3,2,1,0:T(2,128)} %param.5) | copy-start | bytes 9437188

commit v7 on v5

--- a/solution.py
+++ b/solution.py
@@ -228,14 +228,15 @@
     got = [col(pieces[d], XOR_Z[d]) for d in (3, 2, 1)]
     piece_x = row(pieces[0], SWAP_X)
     x_in, got, a_in, piece_x = hold((x_in, got, a_in, piece_x))
-    swapped += [row(b, SWAP_CORE) for b in (b_in, pieces[0], x_in, piece_x)]
+    swapped += [row(b, SWAP_CORE) for b in (b_in, x_in)]
     a_in, got, swapped = hold((a_in, got, swapped))
-    b_rows = [[b_own, x_own, swapped[0], swapped[1]], [b_in, x_in, swapped[2], swapped[4]]]
-    piece_rows = [b[None] for b in (pieces[0], piece_x, swapped[3], swapped[5])]
+    b_rows = [[b_own, x_own, swapped[0], swapped[1]], [b_in, x_in, swapped[2], swapped[3]]]
+    piece_core = [row(after(b, swapped[3]), SWAP_CORE) for b in (pieces[0], piece_x)]
 
     (p3,) = parts(place, [a_even, a_in], b_rows, [3])
     wire3 = (p3 * WIRE).astype(F16)
-    wire3, g1, g3_mid, got = hold((wire3, g1, g3_mid, got))
+    wire3, g1, g3_mid, got, piece_core = hold((wire3, g1, g3_mid, got, piece_core))
+    piece_rows = [b[None] for b in (pieces[0], piece_x, *piece_core)]
     got = jnp.stack([got[2], got[1], got[0]])
     i3 = col(wire3, INWARD)
     g2_end = col(g3_mid, OUTWARD)

time: 128 us -> 128 us (level)
  transfers between devices with their start and end apart: 28 -> 28, of which waited for: 11 -> 10; matrix products, arithmetic and copies ran while one was open for 1% -> 1% of each run, Pallas kernels for 10% -> 11%
where the time goes in v7:
time: 128 us
  waiting for transfers between devices  64.2 us (50%)
  starting transfers between devices  38.8 us (30%)
  Pallas kernels  17.7 us (14%)
  local copies, waits for them, and re-layouts  4.58 us (4%)
  other arithmetic  2.13 us (2%)
    ppermute x16, waiting for transfers between devices, col(): return lax.ppermute(x, 'col', pairs)  61.6 us
    ppermute x16, starting transfers between devices, col(): return lax.ppermute(x, 'col', pairs)  31.1 us
    pallas_call x9, Pallas kernels, call(): pl.pallas_call(body, grid_spec=pltpu.PrefetchScalarGridSpec(num_scalar_pr...  17.7 us
    ppermute x12, starting transfers between devices, row(): return lax.ppermute(x, 'row', pairs)  7.71 us
    unnamed x6, local copies, waits for them, and re-layouts  4.58 us
  transfers between devices with their start and end apart: 28, of which 10 were waited for; matrix products, arithmetic and copies ran while one was open for 1% of the time, Pallas kernels for 11%

profile of v7, /device:TPU:0, one launch (start us, length us, event | category | flops | bytes accessed | tf_op | source)
XLA Modules:
  0.0 127.7 jit_solution(6783503867768195627)
XLA Ops:
  0.1 1.4 %copy-done.2 = bf16[8,3,128,2,128]{4,3,2,1,0:T(2,128)(2,1)S(1)} copy-done((bf16[8,3,128,2,128]{4,3,2,1,0:T(2,128)(2,1)S(1)}, bf16[8,3,128,2,128]{4,3,2,1,0:T(2,128)(2,1)}, u32[]{:S(2)}) %copy-start.2) | copy-done | bytes 1572888
  1.5 1.1 shard_map.37
  2.6 3.1 %collective-permute-start = (bf16[4,384,256]{2,1,0:T(8,128)(2,1)S(1)}, bf16[4,384,256]{2,1,0:T(8,128)(2,1)S(1)}, u32[]{:S(2)}, u32[]{:S(2)}) collective-permute-start(bf16[4,384,256]{2,1,0:T(8,128)(2,1)S(1)} %get-tuple-element.74.refs_0_), channel_id=1, source_target_pairs={{0,2},{1,3},{2,0},{3,1},{4,6},{5,7},{6,4},{7,5},{8,10},{9,11},{10,... | collective-permute-start | bytes 2359304 | tf_op jit(solution)/shard_map/ppermute | solution.py:40
  5.7 1.6 %copy-done.1 = bf16[2,2,128,16,128]{4,3,2,1,0:T(8,128)(2,1)S(1)} copy-done((bf16[2,2,128,16,128]{4,3,2,1,0:T(8,128)(2,1)S(1)}, bf16[2,2,128,16,128]{4,3,2,1,0:T(8,128)(2,1)}, u32[]{:S(2)}) %copy-start.1) | copy-done | bytes 2097176
  7.2 1.5 %shard_map.39 = (bf16[4,256,256]{2,1,0:T(8,128)(2,1)S(1)}, bf16[4,256,256]{2,1,0:T(8,128)(2,1)S(1)}) custom-call(s32[3]{0:T(128)S(1)} %pad_add_fusion._.place_ref, bf16[2,2,128,16,128]{4,3,2,1,0:T(8,128)(2,1)S(1)} %copy-done.1), custom_call_target="tpu_custom_call" | custom-call | tf_op jit(solution)/shard_map/pallas_call | solution.py:60
  8.8 0.7 collective-permute-start.1
  9.5 1.6 %collective-permute-start.3 = (bf16[4,256,256]{2,1,0:T(8,128)(2,1)S(1)}, bf16[4,256,256]{2,1,0:T(8,128)(2,1)S(1)}, u32[]{:S(2)}, u32[]{:S(2)}) collective-permute-start(bf16[4,256,256]{2,1,0:T(8,128)(2,1)S(1)} %get-tuple-element.73), channel_id=1, source_target_pairs={{0,1},{1,0},{2,3},{3,2},{4,5},{5,4},{6,7},{7,6},{8,9},{9,8},{10,11... | collective-permute-start | bytes 1572872 | tf_op jit(solution)/shard_map/ppermute | solution.py:40
  11.1 1.5 %collective-permute-start.2 = (bf16[4,256,256]{2,1,0:T(8,128)(2,1)S(1)}, bf16[4,256,256]{2,1,0:T(8,128)(2,1)S(1)}, u32[]{:S(2)}, u32[]{:S(2)}) collective-permute-start(bf16[4,256,256]{2,1,0:T(8,128)(2,1)S(1)} %get-tuple-element.81.refs_2_.refs_10_.refs_18_), channel_id=1, source_target_pairs={{0,16},{8,24},{16,0},{24,8},{1,17},{9,25},{17,1},{25,9},{2,18},{10... | collective-permute-start | bytes 1572872 | tf_op jit(solution)/shard_map/ppermute | solution.py:44
  12.6 0.5 collective-permute-start.10
  13.1 1.5 %shard_map.38 = (bf16[2,256,256]{2,1,0:T(8,128)(2,1)S(1)}, bf16[2,256,256]{2,1,0:T(8,128)(2,1)S(1)}, bf16[2,256,256]{2,1,0:T(8,128)(2,1)S(1)}, bf16[2,256,256]{2,1,0:T(8,128)(2,1)S(1)}) custom-call(s32[3]{0:T(128)S(1)} %pad_add_fusion._.place_ref, bf16[2,2,128,16,128]{4,3,2,1,0:T(8,128)(2,1)S(1)} %copy-done.1), custom_call_target="tpu_custom_call" | custom-call | tf_op jit(solution)/shard_map/pallas_call | solution.py:60
  14.6 9.8 %collective-permute-done.3.refs_6_.refs_14_.refs_22_ = bf16[4,256,256]{2,1,0:T(8,128)(2,1)S(1)} collective-permute-done((bf16[4,256,256]{2,1,0:T(8,128)(2,1)S(1)}, bf16[4,256,256]{2,1,0:T(8,128)(2,1)S(1)}, u32[]{:S(2)}, u32[]{:S(2)}) %collective-permute-start.3) | collective-permute-done | bytes 524320 | tf_op jit(solution)/shard_map/ppermute | solution.py:40
  24.5 0.5 collective-permute-start.6
  25.0 1.5 %collective-permute-start.4 = (bf16[4,256,256]{2,1,0:T(8,128)(2,1)S(1)}, bf16[4,256,256]{2,1,0:T(8,128)(2,1)S(1)}, u32[]{:S(2)}, u32[]{:S(2)}) collective-permute-start(bf16[4,256,256]{2,1,0:T(8,128)(2,1)S(1)} %collective-permute-done.3.refs_6_.refs_14_.refs_22_), channel_id=1, source_target_pairs={{0,16},{8,24},{16,0},{24,8},{1,17},{9,25},{17,1},{25,9},{2,18},{10... | collective-permute-start | bytes 1572872 | tf_op jit(solution)/shard_map/ppermute | solution.py:44
  26.5 0.7 collective-permute-done.6.refs_5_.refs_13_.refs_21_
  27.1 2.5 %collective-permute-start.7 = (bf16[2,256,256]{2,1,0:T(8,128)(2,1)S(1)}, bf16[2,256,256]{2,1,0:T(8,128)(2,1)S(1)}, u32[]{:S(2)}, u32[]{:S(2)}) collective-permute-start(bf16[2,256,256]{2,1,0:T(8,128)(2,1)S(1)} %get-tuple-element.83), channel_id=1, source_target_pairs={{0,6},{1,7},{2,4},{3,5},{4,2},{5,3},{6,0},{7,1},{8,14},{9,15},{10,... | collective-permute-start | bytes 786440 | tf_op jit(solution)/shard_map/ppermute | solution.py:40
  29.6 5.6 %collective-permute-start.8 = (bf16[2,256,256]{2,1,0:T(8,128)(2,1)S(1)}, bf16[2,256,256]{2,1,0:T(8,128)(2,1)S(1)}, u32[]{:S(2)}, u32[]{:S(2)}) collective-permute-start(bf16[2,256,256]{2,1,0:T(8,128)(2,1)S(1)} %get-tuple-element.84), channel_id=1, source_target_pairs={{0,4},{1,5},{2,6},{3,7},{4,0},{5,1},{6,2},{7,3},{8,12},{9,13},{10,... | collective-permute-start | bytes 786440 | tf_op jit(solution)/shard_map/ppermute | solution.py:40
  35.5 4.3 %collective-permute-done.10.refs_1_ = bf16[4,384,256]{2,1,0:T(8,128)(2,1)S(1)} collective-permute-done((bf16[4,384,256]{2,1,0:T(8,128)(2,1)S(1)}, bf16[4,384,256]{2,1,0:T(8,128)(2,1)S(1)}, u32[]{:S(2)}, u32[]{:S(2)}) %collective-permute-start.10) | collective-permute-done | bytes 786464 | tf_op jit(solution)/shard_map/ppermute | solution.py:40
  39.8 1.5 %collective-permute-start.11 = (bf16[2,256,256]{2,1,0:T(8,128)(2,1)S(1)}, bf16[2,256,256]{2,1,0:T(8,128)(2,1)S(1)}, u32[]{:S(2)}, u32[]{:S(2)}) collective-permute-start(bf16[2,256,256]{2,1,0:T(8,128)(2,1)S(1)} %get-tuple-element.104), channel_id=1, source_target_pairs={{0,16},{8,24},{16,0},{24,8},{1,17},{9,25},{17,1},{25,9},{2,18},{10... | collective-permute-start | bytes 786440 | tf_op jit(solution)/shard_map/ppermute | solution.py:44
  41.3 12.8 %collective-permute-done.8 = bf16[2,256,256]{2,1,0:T(8,128)(2,1)S(1)} collective-permute-done((bf16[2,256,256]{2,1,0:T(8,128)(2,1)S(1)}, bf16[2,256,256]{2,1,0:T(8,128)(2,1)S(1)}, u32[]{:S(2)}, u32[]{:S(2)}) %collective-permute-start.8) | collective-permute-done | bytes 262176 | tf_op jit(solution)/shard_map/ppermute | solution.py:40
  54.2 1.9 %collective-permute-done.13.refs_9_.refs_17_.refs_25_ = bf16[4,256,256]{2,1,0:T(8,128)(2,1)S(1)} collective-permute-done((bf16[4,256,256]{2,1,0:T(8,128)(2,1)S(1)}, bf16[4,256,256]{2,1,0:T(8,128)(2,1)S(1)}, u32[]{:S(2)}, u32[]{:S(2)}) %collective-permute-start.13) | collective-permute-done | bytes 524320 | tf_op jit(solution)/shard_map/ppermute | solution.py:44
  56.2 0.4 collective-permute-start.15
  56.6 1.7 %shard_map.40 = f32[4,384,256]{2,1,0:T(8,128)S(1)} custom-call(s32[3]{0:T(128)S(1)} %pad_add_fusion._.place_ref, bf16[4,384,256]{2,1,0:T(8,128)(2,1)S(1)} %get-tuple-element.109.refs_0_, bf16[4,384,256]{2,1,0:T(8,128)(2,1)S(1)} %collective-permute-done.10.refs_1_, bf16[4,256,256]{2,1,0:T(8,128)(2,1)S(1)} %get-tuple-element.81.refs_2_.refs_10_.refs_18_, ...), custom_call_target="tpu_custom_call" | custom-call | tf_op jit(solution)/shard_map/pallas_call | solution.py:60
  58.5 1.6 %collective-permute-start.16 = (f16[4,384,256]{2,1,0:T(8,128)(2,1)S(1)}, f16[4,384,256]{2,1,0:T(8,128)(2,1)S(1)}, u32[]{:S(2)}, u32[]{:S(2)}) collective-permute-start(f16[4,384,256]{2,1,0:T(8,128)(2,1)S(1)} %multiply_convert_fusion.5), channel_id=1, source_target_pairs={{0,2},{1,3},{6,4},{7,5},{8,10},{9,11},{14,12},{15,13},{16,18},{17,... | collective-permute-start | bytes 2359304 | tf_op jit(solution)/shard_map/ppermute | solution.py:40
  60.2 1.6 %collective-permute-start.18 = (bf16[3,2,256,256]{3,2,1,0:T(8,128)(2,1)S(1)}, bf16[3,2,256,256]{3,2,1,0:T(8,128)(2,1)S(1)}, u32[]{:S(2)}, u32[]{:S(2)}) collective-permute-start(bf16[3,2,256,256]{3,2,1,0:T(8,128)(2,1)S(1)} %pad_maximum_fusion.refs_10_.refs_14_.refs_18_), channel_id=1, source_target_pairs={{0,16},{8,24},{16,0},{24,8},{1,17},{9,25},{17,1},{25,9},{2,18},{10... | collective-permute-start | bytes 2359304 | tf_op jit(solution)/shard_map/ppermute | solution.py:44
  61.8 0.7 collective-permute-start.17
  62.5 1.3 %collective-permute-start.19 = (bf16[4,384,256]{2,1,0:T(8,128)(2,1)S(1)}, bf16[4,384,256]{2,1,0:T(8,128)(2,1)S(1)}, u32[]{:S(2)}, u32[]{:S(2)}) collective-permute-start(bf16[4,384,256]{2,1,0:T(8,128)(2,1)S(1)} %collective-permute-done.1.refs_4_), channel_id=1, source_target_pairs={{2,0},{3,1},{4,6},{5,7},{10,8},{11,9},{12,14},{13,15},{18,16},{19,... | collective-permute-start | bytes 2359304 | tf_op jit(solution)/shard_map/ppermute | solution.py:40
  63.8 2.7 %shard_map.41 = (f32[4,384,256]{2,1,0:T(8,128)S(1)}, f32[4,384,256]{2,1,0:T(8,128)S(1)}, f32[4,384,256]{2,1,0:T(8,128)S(1)}) custom-call(s32[3]{0:T(128)S(1)} %pad_add_fusion._.place_ref, bf16[4,384,256]{2,1,0:T(8,128)(2,1)S(1)} %get-tuple-element.109.refs_0_, bf16[4,384,256]{2,1,0:T(8,128)(2,1)S(1)} %collective-permute-done.10.refs_1_, ...), custom_call_target="tpu_custom_call" | custom-call | tf_op jit(solution)/shard_map/pallas_call | solution.py:60
  66.6 10.6 %collective-permute-done.16 = f16[4,384,256]{2,1,0:T(8,128)(2,1)S(1)} collective-permute-done((f16[4,384,256]{2,1,0:T(8,128)(2,1)S(1)}, f16[4,384,256]{2,1,0:T(8,128)(2,1)S(1)}, u32[]{:S(2)}, u32[]{:S(2)}) %collective-permute-start.16) | collective-permute-done | bytes 786464 | tf_op jit(solution)/shard_map/ppermute | solution.py:40
  77.2 0.5 multiply_convert_fusion.3
  77.7 4.4 %collective-permute-start.21 = (f16[4,384,256]{2,1,0:T(8,128)(2,1)S(1)}, f16[4,384,256]{2,1,0:T(8,128)(2,1)S(1)}, u32[]{:S(2)}, u32[]{:S(2)}) collective-permute-start(f16[4,384,256]{2,1,0:T(8,128)(2,1)S(1)} %get-tuple-element.127), channel_id=1, source_target_pairs={{0,2},{1,3},{6,4},{7,5},{8,10},{9,11},{14,12},{15,13},{16,18},{17,... | collective-permute-start | bytes 2359304 | tf_op jit(solution)/shard_map/ppermute | solution.py:40
  82.1 1.3 %collective-permute-done.19.refs_3_ = bf16[4,384,256]{2,1,0:T(8,128)(2,1)S(1)} collective-permute-done((bf16[4,384,256]{2,1,0:T(8,128)(2,1)S(1)}, bf16[4,384,256]{2,1,0:T(8,128)(2,1)S(1)}, u32[]{:S(2)}, u32[]{:S(2)}) %collective-permute-start.19) | collective-permute-done | bytes 786464 | tf_op jit(solution)/shard_map/ppermute | solution.py:40
  83.4 0.7 collective-permute-start.22
  84.1 1.3 %collective-permute-start.20 = (bf16[4,384,256]{2,1,0:T(8,128)(2,1)S(1)}, bf16[4,384,256]{2,1,0:T(8,128)(2,1)S(1)}, u32[]{:S(2)}, u32[]{:S(2)}) collective-permute-start(bf16[4,384,256]{2,1,0:T(8,128)(2,1)S(1)} %collective-permute-done.17.refs_2_), channel_id=1, source_target_pairs={{2,0},{3,1},{4,6},{5,7},{10,8},{11,9},{12,14},{13,15},{18,16},{19,... | collective-permute-start | bytes 2359304 | tf_op jit(solution)/shard_map/ppermute | solution.py:40
  85.5 0.5 collective-permute-start.24
  86.0 12.3 %collective-permute-done.21 = f16[4,384,256]{2,1,0:T(8,128)(2,1)S(1)} collective-permute-done((f16[4,384,256]{2,1,0:T(8,128)(2,1)S(1)}, f16[4,384,256]{2,1,0:T(8,128)(2,1)S(1)}, u32[]{:S(2)}, u32[]{:S(2)}) %collective-permute-start.21) | collective-permute-done | bytes 786464 | tf_op jit(solution)/shard_map/ppermute | solution.py:40
  98.3 0.3 multiply_convert_fusion.2
  98.6 0.3 multiply_convert_fusion.1
  99.0 4.5 %collective-permute-start.26 = (f16[4,384,256]{2,1,0:T(8,128)(2,1)S(1)}, f16[4,384,256]{2,1,0:T(8,128)(2,1)S(1)}, u32[]{:S(2)}, u32[]{:S(2)}) collective-permute-start(f16[4,384,256]{2,1,0:T(8,128)(2,1)S(1)} %multiply_convert_fusion.1), channel_id=1, source_target_pairs={{0,2},{1,3},{2,0},{3,1},{4,6},{5,7},{6,4},{7,5},{8,10},{9,11},{10,... | collective-permute-start | bytes 2359304 | tf_op jit(solution)/shard_map/ppermute | solution.py:40
  103.5 0.7 collective-permute-start.27
  104.2 1.7 %collective-permute-done.20.refs_5_ = bf16[4,384,256]{2,1,0:T(8,128)(2,1)S(1)} collective-permute-done((bf16[4,384,256]{2,1,0:T(8,128)(2,1)S(1)}, bf16[4,384,256]{2,1,0:T(8,128)(2,1)S(1)}, u32[]{:S(2)}, u32[]{:S(2)}) %collective-permute-start.20) | collective-permute-done | bytes 786464 | tf_op jit(solution)/shard_map/ppermute | solution.py:40
  105.9 2.3 %shard_map.43 = f32[4,384,256]{2,1,0:T(8,128)S(1)} custom-call(s32[3]{0:T(128)S(1)} %pad_add_fusion._.place_ref, bf16[4,384,256]{2,1,0:T(8,128)(2,1)S(1)} %get-tuple-element.74.refs_0_, bf16[4,384,256]{2,1,0:T(8,128)(2,1)S(1)} %collective-permute-done.refs_1_, bf16[4,384,256]{2,1,0:T(8,128)(2,1)S(1)} %collective-permute-done.17.refs_2_, ...), custom_call_target="tpu_custom_call" | custom-call | tf_op jit(solution)/shard_map/pallas_call | solution.py:60
  108.4 1.6 %collective-permute-start.25 = (f16[4,384,256]{2,1,0:T(8,128)(2,1)S(1)}, f16[4,384,256]{2,1,0:T(8,128)(2,1)S(1)}, u32[]{:S(2)}, u32[]{:S(2)}) collective-permute-start(f16[4,384,256]{2,1,0:T(8,128)(2,1)S(1)} %multiply_convert_fusion), channel_id=1, source_target_pairs={{0,1},{1,0},{2,3},{3,2},{4,5},{5,4},{6,7},{7,6},{8,9},{9,8},{10,11... | collective-permute-start | bytes 2359304 | tf_op jit(solution)/shard_map/ppermute | solution.py:40
  110.0 2.3 %shard_map.42 = f32[4,384,256]{2,1,0:T(8,128)S(1)} custom-call(s32[3]{0:T(128)S(1)} %pad_add_fusion._.place_ref, bf16[4,384,256]{2,1,0:T(8,128)(2,1)S(1)} %get-tuple-element.74.refs_0_, bf16[4,384,256]{2,1,0:T(8,128)(2,1)S(1)} %collective-permute-done.refs_1_, bf16[4,384,256]{2,1,0:T(8,128)(2,1)S(1)} %collective-permute-done.17.refs_2_, ...), custom_call_target="tpu_custom_call" | custom-call | tf_op jit(solution)/shard_map/pallas_call | solution.py:60
  112.3 8.7 %collective-permute-done.26 = f16[4,384,256]{2,1,0:T(8,128)(2,1)S(1)} collective-permute-done((f16[4,384,256]{2,1,0:T(8,128)(2,1)S(1)}, f16[4,384,256]{2,1,0:T(8,128)(2,1)S(1)}, u32[]{:S(2)}, u32[]{:S(2)}) %collective-permute-start.26) | collective-permute-done | bytes 786464 | tf_op jit(solution)/shard_map/ppermute | solution.py:40
  121.0 0.3 multiply_add_fusion.add_ref
  121.3 1.6 %copy-done = f32[8,3,128,2,128]{4,3,2,1,0:T(2,128)S(1)} copy-done((f32[8,3,128,2,128]{4,3,2,1,0:T(2,128)S(1)}, f32[8,3,128,2,128]{4,3,2,1,0:T(2,128)}, u32[]{:S(2)}) %copy-start) | copy-done | bytes 3145752
  122.9 2.3 %shard_map.44.refs_0_ = f32[8,768,128]{2,1,0:T(8,128)} custom-call(s32[3]{0:T(128)S(1)} %pad_add_fusion._.place_ref, f32[8,768,128]{2,1,0:T(8,128)S(1)} %bitcast.13, f32[4,384,256]{2,1,0:T(8,128)S(1)} %multiply_add_fusion.add_ref), custom_call_target="tpu_custom_call" | custom-call | tf_op jit(solution)/shard_map/pallas_call | solution.py:60
  125.4 2.3 %shard_map.45 = f32[8,768,128]{2,1,0:T(8,128)} custom-call(s32[3]{0:T(128)S(1)} %pad_add_fusion._.place_ref, f32[8,768,128]{2,1,0:T(8,128)S(1)} %bitcast.14, f32[4,384,256]{2,1,0:T(8,128)S(1)} %multiply_add_fusion.1.add_ref, f32[8,768,128]{2,1,0:T(8,128)} %shard_map.44.refs_0_), custom_call_target="tpu_custom_call", output_to_operand_aliasing={{}: (3, {})} | custom-call | tf_op jit(solution)/shard_map/pallas_call | solution.py:60
  (32 shorter events, 1.4 us)
Async XLA Ops:
  0.1 1.4 %copy-start.2 = (bf16[8,3,128,2,128]{4,3,2,1,0:T(2,128)(2,1)S(1)}, bf16[8,3,128,2,128]{4,3,2,1,0:T(2,128)(2,1)}, u32[]{:S(2)}) copy-start(bf16[8,3,128,2,128]{4,3,2,1,0:T(2,128)(2,1)} %param.4) | copy-start | bytes 4718596
  2.6 21.9 %collective-permute-start = (bf16[4,384,256]{2,1,0:T(8,128)(2,1)S(1)}, bf16[4,384,256]{2,1,0:T(8,128)(2,1)S(1)}, u32[]{:S(2)}, u32[]{:S(2)}) collective-permute-start(bf16[4,384,256]{2,1,0:T(8,128)(2,1)S(1)} %get-tuple-element.74.refs_0_), channel_id=1, source_target_pairs={{0,2},{1,3},{2,0},{3,1},{4,6},{5,7},{6,4},{7,5},{8,10},{9,11},{10,... | collective-permute-start | bytes 2359304 | tf_op jit(solution)/shard_map/ppermute | solution.py:40
  5.7 1.6 %copy-start.1 = (bf16[2,2,128,16,128]{4,3,2,1,0:T(8,128)(2,1)S(1)}, bf16[2,2,128,16,128]{4,3,2,1,0:T(8,128)(2,1)}, u32[]{:S(2)}) copy-start(bf16[2,2,128,16,128]{4,3,2,1,0:T(8,128)(2,1)} %in_ref.1) | copy-start | bytes 6291460
  8.8 15.6 %collective-permute-start.1 = (bf16[4,384,256]{2,1,0:T(8,128)(2,1)S(1)}, bf16[4,384,256]{2,1,0:T(8,128)(2,1)S(1)}, u32[]{:S(2)}, u32[]{:S(2)}) collective-permute-start(bf16[4,384,256]{2,1,0:T(8,128)(2,1)S(1)} %get-tuple-element.74.refs_0_), channel_id=1, source_target_pairs={{2,4},{3,5},{4,2},{5,3},{10,12},{11,13},{12,10},{13,11},{18,20},{1... | collective-permute-start | bytes 2359304 | tf_op jit(solution)/shard_map/ppermute | solution.py:40
  9.5 14.9 %collective-permute-start.3 = (bf16[4,256,256]{2,1,0:T(8,128)(2,1)S(1)}, bf16[4,256,256]{2,1,0:T(8,128)(2,1)S(1)}, u32[]{:S(2)}, u32[]{:S(2)}) collective-permute-start(bf16[4,256,256]{2,1,0:T(8,128)(2,1)S(1)} %get-tuple-element.73), channel_id=1, source_target_pairs={{0,1},{1,0},{2,3},{3,2},{4,5},{5,4},{6,7},{7,6},{8,9},{9,8},{10,11... | collective-permute-start | bytes 1572872 | tf_op jit(solution)/shard_map/ppermute | solution.py:40
  11.1 13.3 %collective-permute-start.2 = (bf16[4,256,256]{2,1,0:T(8,128)(2,1)S(1)}, bf16[4,256,256]{2,1,0:T(8,128)(2,1)S(1)}, u32[]{:S(2)}, u32[]{:S(2)}) collective-permute-start(bf16[4,256,256]{2,1,0:T(8,128)(2,1)S(1)} %get-tuple-element.81.refs_2_.refs_10_.refs_18_), channel_id=1, source_target_pairs={{0,16},{8,24},{16,0},{24,8},{1,17},{9,25},{17,1},{25,9},{2,18},{10... | collective-permute-start | bytes 1572872 | tf_op jit(solution)/shard_map/ppermute | solution.py:44
  12.6 27.2 %collective-permute-start.10 = (bf16[4,384,256]{2,1,0:T(8,128)(2,1)S(1)}, bf16[4,384,256]{2,1,0:T(8,128)(2,1)S(1)}, u32[]{:S(2)}, u32[]{:S(2)}) collective-permute-start(bf16[4,384,256]{2,1,0:T(8,128)(2,1)S(1)} %get-tuple-element.109.refs_0_), channel_id=1, source_target_pairs={{0,1},{1,0},{2,3},{3,2},{4,5},{5,4},{6,7},{7,6},{8,9},{9,8},{10,11... | collective-permute-start | bytes 2359304 | tf_op jit(solution)/shard_map/ppermute | solution.py:40
  24.4 2.1 %collective-permute-start.5 = (bf16[4,256,256]{2,1,0:T(8,128)(2,1)S(1)}, bf16[4,256,256]{2,1,0:T(8,128)(2,1)S(1)}, u32[]{:S(2)}, u32[]{:S(2)}) collective-permute-start(bf16[4,256,256]{2,1,0:T(8,128)(2,1)S(1)} %get-tuple-element.81.refs_2_.refs_10_.refs_18_), channel_id=1, source_target_pairs={{0,8},{8,0},{16,24},{24,16},{1,9},{9,1},{17,25},{25,17},{2,10},{10... | collective-permute-start | bytes 1572872 | tf_op jit(solution)/shard_map/ppermute | solution.py:44
  24.5 2.6 %collective-permute-start.6 = (bf16[4,256,256]{2,1,0:T(8,128)(2,1)S(1)}, bf16[4,256,256]{2,1,0:T(8,128)(2,1)S(1)}, u32[]{:S(2)}, u32[]{:S(2)}) collective-permute-start(bf16[4,256,256]{2,1,0:T(8,128)(2,1)S(1)} %collective-permute-done.2.refs_3_.refs_11_.refs_19_), channel_id=1, source_target_pairs={{0,8},{8,0},{16,24},{24,16},{1,9},{9,1},{17,25},{25,17},{2,10},{10... | collective-permute-start | bytes 1572872 | tf_op jit(solution)/shard_map/ppermute | solution.py:44
  25.0 16.3 %collective-permute-start.4 = (bf16[4,256,256]{2,1,0:T(8,128)(2,1)S(1)}, bf16[4,256,256]{2,1,0:T(8,128)(2,1)S(1)}, u32[]{:S(2)}, u32[]{:S(2)}) collective-permute-start(bf16[4,256,256]{2,1,0:T(8,128)(2,1)S(1)} %collective-permute-done.3.refs_6_.refs_14_.refs_22_), channel_id=1, source_target_pairs={{0,16},{8,24},{16,0},{24,8},{1,17},{9,25},{17,1},{25,9},{2,18},{10... | collective-permute-start | bytes 1572872 | tf_op jit(solution)/shard_map/ppermute | solution.py:44
  27.1 14.2 %collective-permute-start.7 = (bf16[2,256,256]{2,1,0:T(8,128)(2,1)S(1)}, bf16[2,256,256]{2,1,0:T(8,128)(2,1)S(1)}, u32[]{:S(2)}, u32[]{:S(2)}) collective-permute-start(bf16[2,256,256]{2,1,0:T(8,128)(2,1)S(1)} %get-tuple-element.83), channel_id=1, source_target_pairs={{0,6},{1,7},{2,4},{3,5},{4,2},{5,3},{6,0},{7,1},{8,14},{9,15},{10,... | collective-permute-start | bytes 786440 | tf_op jit(solution)/shard_map/ppermute | solution.py:40
  29.6 24.5 %collective-permute-start.8 = (bf16[2,256,256]{2,1,0:T(8,128)(2,1)S(1)}, bf16[2,256,256]{2,1,0:T(8,128)(2,1)S(1)}, u32[]{:S(2)}, u32[]{:S(2)}) collective-permute-start(bf16[2,256,256]{2,1,0:T(8,128)(2,1)S(1)} %get-tuple-element.84), channel_id=1, source_target_pairs={{0,4},{1,5},{2,6},{3,7},{4,0},{5,1},{6,2},{7,3},{8,12},{9,13},{10,... | collective-permute-start | bytes 786440 | tf_op jit(solution)/shard_map/ppermute | solution.py:40
  35.2 18.9 %collective-permute-start.9 = (bf16[2,256,256]{2,1,0:T(8,128)(2,1)S(1)}, bf16[2,256,256]{2,1,0:T(8,128)(2,1)S(1)}, u32[]{:S(2)}, u32[]{:S(2)}) collective-permute-start(bf16[2,256,256]{2,1,0:T(8,128)(2,1)S(1)} %get-tuple-element.85), channel_id=1, source_target_pairs={{0,2},{1,3},{2,0},{3,1},{4,6},{5,7},{6,4},{7,5},{8,10},{9,11},{10,... | collective-permute-start | bytes 786440 | tf_op jit(solution)/shard_map/ppermute | solution.py:40
  39.8 14.4 %collective-permute-start.11 = (bf16[2,256,256]{2,1,0:T(8,128)(2,1)S(1)}, bf16[2,256,256]{2,1,0:T(8,128)(2,1)S(1)}, u32[]{:S(2)}, u32[]{:S(2)}) collective-permute-start(bf16[2,256,256]{2,1,0:T(8,128)(2,1)S(1)} %get-tuple-element.104), channel_id=1, source_target_pairs={{0,16},{8,24},{16,0},{24,8},{1,17},{9,25},{17,1},{25,9},{2,18},{10... | collective-permute-start | bytes 786440 | tf_op jit(solution)/shard_map/ppermute | solution.py:44
  41.3 12.9 %collective-permute-start.12 = (bf16[4,256,256]{2,1,0:T(8,128)(2,1)S(1)}, bf16[4,256,256]{2,1,0:T(8,128)(2,1)S(1)}, u32[]{:S(2)}, u32[]{:S(2)}) collective-permute-start(bf16[4,256,256]{2,1,0:T(8,128)(2,1)S(1)} %collective-permute-done.3.refs_6_.refs_14_.refs_22_), channel_id=1, source_target_pairs={{0,8},{8,0},{16,24},{24,16},{1,9},{9,1},{17,25},{25,17},{2,10},{10... | collective-permute-start | bytes 1572872 | tf_op jit(solution)/shard_map/ppermute | solution.py:44
  54.2 1.9 %collective-permute-start.13 = (bf16[4,256,256]{2,1,0:T(8,128)(2,1)S(1)}, bf16[4,256,256]{2,1,0:T(8,128)(2,1)S(1)}, u32[]{:S(2)}, u32[]{:S(2)}) collective-permute-start(bf16[4,256,256]{2,1,0:T(8,128)(2,1)S(1)} %collective-permute-done.4.refs_7_.refs_15_.refs_23_), channel_id=1, source_target_pairs={{0,8},{8,0},{16,24},{24,16},{1,9},{9,1},{17,25},{25,17},{2,10},{10... | collective-permute-start | bytes 1572872 | tf_op jit(solution)/shard_map/ppermute | solution.py:44
  56.1 2.4 %collective-permute-start.14 = (bf16[2,256,256]{2,1,0:T(8,128)(2,1)S(1)}, bf16[2,256,256]{2,1,0:T(8,128)(2,1)S(1)}, u32[]{:S(2)}, u32[]{:S(2)}) collective-permute-start(bf16[2,256,256]{2,1,0:T(8,128)(2,1)S(1)} %get-tuple-element.104), channel_id=1, source_target_pairs={{0,8},{8,0},{16,24},{24,16},{1,9},{9,1},{17,25},{25,17},{2,10},{10... | collective-permute-start | bytes 786440 | tf_op jit(solution)/shard_map/ppermute | solution.py:44
  56.2 2.3 %collective-permute-start.15 = (bf16[2,256,256]{2,1,0:T(8,128)(2,1)S(1)}, bf16[2,256,256]{2,1,0:T(8,128)(2,1)S(1)}, u32[]{:S(2)}, u32[]{:S(2)}) collective-permute-start(bf16[2,256,256]{2,1,0:T(8,128)(2,1)S(1)} %collective-permute-done.11), channel_id=1, source_target_pairs={{0,8},{8,0},{16,24},{24,16},{1,9},{9,1},{17,25},{25,17},{2,10},{10... | collective-permute-start | bytes 786440 | tf_op jit(solution)/shard_map/ppermute | solution.py:44
  58.5 18.7 %collective-permute-start.16 = (f16[4,384,256]{2,1,0:T(8,128)(2,1)S(1)}, f16[4,384,256]{2,1,0:T(8,128)(2,1)S(1)}, u32[]{:S(2)}, u32[]{:S(2)}) collective-permute-start(f16[4,384,256]{2,1,0:T(8,128)(2,1)S(1)} %multiply_convert_fusion.5), channel_id=1, source_target_pairs={{0,2},{1,3},{6,4},{7,5},{8,10},{9,11},{14,12},{15,13},{16,18},{17,... | collective-permute-start | bytes 2359304 | tf_op jit(solution)/shard_map/ppermute | solution.py:40
  60.2 21.9 %collective-permute-start.18 = (bf16[3,2,256,256]{3,2,1,0:T(8,128)(2,1)S(1)}, bf16[3,2,256,256]{3,2,1,0:T(8,128)(2,1)S(1)}, u32[]{:S(2)}, u32[]{:S(2)}) collective-permute-start(bf16[3,2,256,256]{3,2,1,0:T(8,128)(2,1)S(1)} %pad_maximum_fusion.refs_10_.refs_14_.refs_18_), channel_id=1, source_target_pairs={{0,16},{8,24},{16,0},{24,8},{1,17},{9,25},{17,1},{25,9},{2,18},{10... | collective-permute-start | bytes 2359304 | tf_op jit(solution)/shard_map/ppermute | solution.py:44
  61.8 20.3 %collective-permute-start.17 = (bf16[4,384,256]{2,1,0:T(8,128)(2,1)S(1)}, bf16[4,384,256]{2,1,0:T(8,128)(2,1)S(1)}, u32[]{:S(2)}, u32[]{:S(2)}) collective-permute-start(bf16[4,384,256]{2,1,0:T(8,128)(2,1)S(1)} %collective-permute-done.refs_1_), channel_id=1, source_target_pairs={{2,4},{3,5},{4,2},{5,3},{10,12},{11,13},{12,10},{13,11},{18,20},{1... | collective-permute-start | bytes 2359304 | tf_op jit(solution)/shard_map/ppermute | solution.py:40
  62.5 20.9 %collective-permute-start.19 = (bf16[4,384,256]{2,1,0:T(8,128)(2,1)S(1)}, bf16[4,384,256]{2,1,0:T(8,128)(2,1)S(1)}, u32[]{:S(2)}, u32[]{:S(2)}) collective-permute-start(bf16[4,384,256]{2,1,0:T(8,128)(2,1)S(1)} %collective-permute-done.1.refs_4_), channel_id=1, source_target_pairs={{2,0},{3,1},{4,6},{5,7},{10,8},{11,9},{12,14},{13,15},{18,16},{19,... | collective-permute-start | bytes 2359304 | tf_op jit(solution)/shard_map/ppermute | solution.py:40
  77.7 20.6 %collective-permute-start.21 = (f16[4,384,256]{2,1,0:T(8,128)(2,1)S(1)}, f16[4,384,256]{2,1,0:T(8,128)(2,1)S(1)}, u32[]{:S(2)}, u32[]{:S(2)}) collective-permute-start(f16[4,384,256]{2,1,0:T(8,128)(2,1)S(1)} %get-tuple-element.127), channel_id=1, source_target_pairs={{0,2},{1,3},{6,4},{7,5},{8,10},{9,11},{14,12},{15,13},{16,18},{17,... | collective-permute-start | bytes 2359304 | tf_op jit(solution)/shard_map/ppermute | solution.py:40
  83.4 15.2 %collective-permute-start.22 = (f16[4,384,256]{2,1,0:T(8,128)(2,1)S(1)}, f16[4,384,256]{2,1,0:T(8,128)(2,1)S(1)}, u32[]{:S(2)}, u32[]{:S(2)}) collective-permute-start(f16[4,384,256]{2,1,0:T(8,128)(2,1)S(1)} %get-tuple-element.119), channel_id=1, source_target_pairs={{2,4},{3,5},{4,2},{5,3},{10,12},{11,13},{12,10},{13,11},{18,20},{1... | collective-permute-start | bytes 2359304 | tf_op jit(solution)/shard_map/ppermute | solution.py:40
  84.1 21.8 %collective-permute-start.20 = (bf16[4,384,256]{2,1,0:T(8,128)(2,1)S(1)}, bf16[4,384,256]{2,1,0:T(8,128)(2,1)S(1)}, u32[]{:S(2)}, u32[]{:S(2)}) collective-permute-start(bf16[4,384,256]{2,1,0:T(8,128)(2,1)S(1)} %collective-permute-done.17.refs_2_), channel_id=1, source_target_pairs={{2,0},{3,1},{4,6},{5,7},{10,8},{11,9},{12,14},{13,15},{18,16},{19,... | collective-permute-start | bytes 2359304 | tf_op jit(solution)/shard_map/ppermute | solution.py:40
  85.4 20.5 %collective-permute-start.23 = (bf16[3,2,256,256]{3,2,1,0:T(8,128)(2,1)S(1)}, bf16[3,2,256,256]{3,2,1,0:T(8,128)(2,1)S(1)}, u32[]{:S(2)}, u32[]{:S(2)}) collective-permute-start(bf16[3,2,256,256]{3,2,1,0:T(8,128)(2,1)S(1)} %pad_maximum_fusion.refs_10_.refs_14_.refs_18_), channel_id=1, source_target_pairs={{0,8},{8,0},{16,24},{24,16},{1,9},{9,1},{17,25},{25,17},{2,10},{10... | collective-permute-start | bytes 2359304 | tf_op jit(solution)/shard_map/ppermute | solution.py:44
  85.5 20.4 %collective-permute-start.24 = (bf16[3,2,256,256]{3,2,1,0:T(8,128)(2,1)S(1)}, bf16[3,2,256,256]{3,2,1,0:T(8,128)(2,1)S(1)}, u32[]{:S(2)}, u32[]{:S(2)}) collective-permute-start(bf16[3,2,256,256]{3,2,1,0:T(8,128)(2,1)S(1)} %collective-permute-done.18.refs_11_.refs_15_.refs_19_), channel_id=1, source_target_pairs={{0,8},{8,0},{16,24},{24,16},{1,9},{9,1},{17,25},{25,17},{2,10},{10... | collective-permute-start | bytes 2359304 | tf_op jit(solution)/shard_map/ppermute | solution.py:44
  99.0 22.0 %collective-permute-start.26 = (f16[4,384,256]{2,1,0:T(8,128)(2,1)S(1)}, f16[4,384,256]{2,1,0:T(8,128)(2,1)S(1)}, u32[]{:S(2)}, u32[]{:S(2)}) collective-permute-start(f16[4,384,256]{2,1,0:T(8,128)(2,1)S(1)} %multiply_convert_fusion.1), channel_id=1, source_target_pairs={{0,2},{1,3},{2,0},{3,1},{4,6},{5,7},{6,4},{7,5},{8,10},{9,11},{10,... | collective-permute-start | bytes 2359304 | tf_op jit(solution)/shard_map/ppermute | solution.py:40
  103.5 17.5 %collective-permute-start.27 = (f16[4,384,256]{2,1,0:T(8,128)(2,1)S(1)}, f16[4,384,256]{2,1,0:T(8,128)(2,1)S(1)}, u32[]{:S(2)}, u32[]{:S(2)}) collective-permute-start(f16[4,384,256]{2,1,0:T(8,128)(2,1)S(1)} %multiply_convert_fusion.2), channel_id=1, source_target_pairs={{2,4},{3,5},{4,2},{5,3},{10,12},{11,13},{12,10},{13,11},{18,20},{1... | collective-permute-start | bytes 2359304 | tf_op jit(solution)/shard_map/ppermute | solution.py:40
  108.4 16.8 %collective-permute-start.25 = (f16[4,384,256]{2,1,0:T(8,128)(2,1)S(1)}, f16[4,384,256]{2,1,0:T(8,128)(2,1)S(1)}, u32[]{:S(2)}, u32[]{:S(2)}) collective-permute-start(f16[4,384,256]{2,1,0:T(8,128)(2,1)S(1)} %multiply_convert_fusion), channel_id=1, source_target_pairs={{0,1},{1,0},{2,3},{3,2},{4,5},{5,4},{6,7},{7,6},{8,9},{9,8},{10,11... | collective-permute-start | bytes 2359304 | tf_op jit(solution)/shard_map/ppermute | solution.py:40
  121.0 1.9 %copy-start = (f32[8,3,128,2,128]{4,3,2,1,0:T(2,128)S(1)}, f32[8,3,128,2,128]{4,3,2,1,0:T(2,128)}, u32[]{:S(2)}) copy-start(f32[8,3,128,2,128]{4,3,2,1,0:T(2,128)} %param.5) | copy-start | bytes 9437188
